TPU v7x, 32 devices: a whole 2x2x4 slice. The times are simulated.
32 devices in a mesh: section: 2 (over y), ctx: 8 (over z, core), wsh: 2 (over x).
Axes of the slice: x: 2, y: 2, z: 4, core: 2. Of those that a mesh axis runs over, the one named last changes fastest.
Arguments:
- tokens: bfloat16 [2, 2, 1024, 768], P(None, 'wsh', 'ctx'), may hold values from -6 to 6
- out_cotangent: bfloat16 [2, 2, 1024, 768], P(None, 'wsh', 'ctx'), may hold values from -6 to 6
- attn_weights: bfloat16 [2, 4, 768, 768], P('section', None, 'wsh')
- up_weights: bfloat16 [2, 768, 3072], P('section', 'wsh'), may hold values from -0.21875 to 0.21875
- down_weights: bfloat16 [2, 3072, 768], P('section', 'wsh'), may hold values from -0.109375 to 0.109375
- norm_gains: bfloat16 [2, 2, 768], P('section', None, 'wsh'), may hold values from 0.25 to 1.75
- bias_rows: bfloat16 [2, 5, 768], P('section', None, 'wsh'), may hold values from -2 to 2
- up_bias: bfloat16 [2, 3072], P('section', 'wsh'), may hold values from -2 to 2
- seq_lengths: int32 [2, 2], P(None, 'wsh'), may hold values from 128 to 1024, as said below
- rand_owner: int32 [2, 2, 16, 12, 3], P(None, 'wsh'), may hold values from 0 to 7, all different within a row; in each aligned block of 24 rows (0 to 23, 24 to 47, ..., all dimensions but the last counted through in order) at most 18 rows name the same one
- rand_local: int32 [2, 2, 16, 12, 3], P(None, 'wsh'), may hold values from 0 to 1
- global_raw: int32 [2, 2, 2], P(None, 'wsh'), may hold values from 0 to 15
Outputs:
- layer_outputs: bfloat16 [2, 2, 2, 1024, 768], P('section', None, 'wsh', 'ctx')
- input_grads: bfloat16 [2, 2, 2, 1024, 768], P('section', None, 'wsh', 'ctx')
- grad_attn: float32 [2, 4, 768, 768], P('section', None, 'wsh')
- grad_up: float32 [2, 768, 3072], P('section', 'wsh')
- grad_down: float32 [2, 3072, 768], P('section', 'wsh')
- grad_gains: float32 [2, 2, 768], P('section', None, 'wsh')
- grad_biases: float32 [2, 5, 768], P('section', None, 'wsh')
- grad_up_bias: float32 [2, 3072], P('section', 'wsh')
- clipped_qk: bfloat16 [2, 2, 768, 768], P('section', None, 'wsh')
Inputs may be any that keep to these rules, and one draw needn't show every extreme that they name: `seq_lengths`: in every shard the sequence of one micro-batch, drawn from the seed, has 1024 tokens. `rand_owner`: within the 24 rows (a query block and head each) of one device's query blocks (aligned blocks) the 3 owners of a row differ and no owner is named by more than 18 of those rows; some device's rows name one owner exactly 18 times.
All inputs are finite; a program needn't handle non-finite values.
Results may differ from a plain program's by a relative error of at most 0.03.
Values may be sent and summed in bfloat16 or wider, within the bound.
A program may use at most 320 MiB of HBM per device.

v0:
```python
import jax
import jax.numpy as jnp
from jax import lax
from jax.sharding import PartitionSpec as P

D = 768
H = 12
HD = 64
FF = 3072
BLK = 64
RND = 3
TOK_DEV = 128
BLK_DEV = 2


norm_eps = 1e-05
clip_limit = 6.0
masked_score = -1e30
peak_score = lax.Precision.HIGHEST


def swapped(block, axis, bit):
    count = lax.axis_size(axis)
    route = []
    for low in range(count):
        high = low | 1 << bit
        if high != low and high < count:
            route += [(low, high), (high, low)]
    return lax.ppermute(block, axis, route)


def padded(cells, sides, width):
    for axis, dim in sides:
        count = lax.axis_size(axis)
        ends = count - 1
        head = lax.slice_in_dim(cells, 0, width, axis=dim)
        tail = lax.slice_in_dim(cells, cells.shape[dim] - width, cells.shape[dim], axis=dim)
        cells = jnp.concatenate(
            [
                lax.ppermute(tail, axis, [(i, (i + 1) % count) for i in range(ends)]),
                cells,
                lax.ppermute(head, axis, [((i + 1) % count, i) for i in range(ends)]),
            ],
            axis=dim,
        )
    return cells


def merged(value, axis, combine):
    everything = jax.tree.map(lambda part: lax.all_gather(part, axis), value)
    leading = jax.tree.map(lambda part: part[0], everything)

    def hop(k, so_far):
        return combine(so_far, jax.tree.map(lambda part: part[k], everything))

    return lax.fori_loop(1, lax.axis_size(axis), hop, leading)


def layer_norm(inputs, norm_gain, norm_shift):
    center = inputs - jnp.mean(inputs, -1, keepdims=True)
    spread = jnp.mean(center * center, -1, keepdims=True)
    return center * lax.rsqrt(spread + norm_eps) * norm_gain + norm_shift


def gelu_exact(values):
    return jax.nn.gelu(values, approximate=False)


def product(left_side, right_side):
    return jnp.dot(left_side, right_side, preferred_element_type=jnp.float32)


def contract_rows(left_side, right_side):
    return lax.dot_general(
        left_side, right_side, (((0,), (0,)), ((), ())), preferred_element_type=jnp.float32
    )


def column_sums(values):
    return jnp.sum(values.astype(jnp.float32), 0)


def across_sections(values):
    return swapped(values, "section", 0)


def spread_grads(grads):
    return (
        lax.psum_scatter(
            grads[0].astype(jnp.bfloat16), "wsh", scatter_dimension=1, tiled=True
        ).astype(jnp.float32),
        lax.psum_scatter(
            grads[1].astype(jnp.bfloat16), "wsh", scatter_dimension=0, tiled=True
        ).astype(jnp.float32),
        lax.psum_scatter(
            grads[2].astype(jnp.bfloat16), "wsh", scatter_dimension=0, tiled=True
        ).astype(jnp.float32),
        lax.psum_scatter(
            grads[3].astype(jnp.bfloat16), "wsh", scatter_dimension=1, tiled=True
        ).astype(jnp.float32),
        lax.psum_scatter(
            grads[4].astype(jnp.bfloat16), "wsh", scatter_dimension=1, tiled=True
        ).astype(jnp.float32),
        lax.psum_scatter(
            grads[5].astype(jnp.bfloat16), "wsh", scatter_dimension=0, tiled=True
        ).astype(jnp.float32),
    )


def weight_grads(rows):
    (
        layer_in,
        grad_queries,
        grad_keys,
        grad_values,
        attended,
        grad_branch,
        normed_low,
        grad_hidden,
        gated,
        grad_down_in,
    ) = rows
    grad_attn = jnp.stack(
        [
            contract_rows(layer_in, grad_queries),
            contract_rows(layer_in, grad_keys),
            contract_rows(layer_in, grad_values),
            contract_rows(attended, grad_branch),
        ]
    )
    return (grad_attn, contract_rows(normed_low, grad_hidden), contract_rows(gated, grad_down_in))


def combine_rows(first, second):
    top = jnp.maximum(first[0], second[0])
    return (top, first[1] * jnp.exp(first[0] - top) + second[1] * jnp.exp(second[0] - top))


def plan_capacity(ctx_count):
    return min(BLK_DEV * H, 2 * ((BLK_DEV * H * RND + ctx_count - 1) // ctx_count))


def sequence_meta(
    micro_index, seq_lengths, rand_owner, rand_local, global_raw, ctx_place, ctx_count
):
    length = seq_lengths[micro_index, 0]
    valid_blocks = (length + BLK - 1) // BLK
    global_ids = global_raw[micro_index, 0] % valid_blocks
    owners_all = rand_owner[micro_index, 0]
    local_all = rand_local[micro_index, 0]
    owners = lax.dynamic_slice_in_dim(owners_all, ctx_place * BLK_DEV, BLK_DEV, 0)
    local_ids = lax.dynamic_slice_in_dim(local_all, ctx_place * BLK_DEV, BLK_DEV, 0)
    offsets = jnp.arange(BLK)
    block_ids = ctx_place * BLK_DEV + jnp.arange(BLK_DEV)
    window = block_ids[:, None] + jnp.arange(3)[None, :] - 1
    window_pos = window[:, :, None] * BLK + offsets
    window_ok = (
        (window[:, :, None] >= 0)
        & (window[:, :, None] < BLK_DEV * ctx_count)
        & (window_pos < length)
    )
    window_ok = jnp.broadcast_to(window_ok.reshape(BLK_DEV, 1, 3 * BLK), (BLK_DEV, H, 3 * BLK))
    global_ok = global_ids[:, None] * BLK + offsets < length
    global_ok = jnp.broadcast_to(global_ok.reshape(1, 1, 2 * BLK), (BLK_DEV, H, 2 * BLK))
    random_blocks = owners * BLK_DEV + local_ids
    random_ok = (random_blocks[..., None] * BLK + offsets < length).reshape(BLK_DEV, H, RND * BLK)
    key_ok = jnp.concatenate([window_ok, global_ok, random_ok], -1)
    query_ok = (ctx_place * TOK_DEV + jnp.arange(TOK_DEV) < length).reshape(BLK_DEV, BLK)
    return (key_ok, query_ok, global_ids, owners, local_ids, owners_all, local_all, length)


def request_plan(owners, ctx_count):
    targets = owners.reshape(-1)
    onehot = (targets[:, None] == jnp.arange(ctx_count)[None, :]).astype(jnp.int32)
    slot_ids = jnp.sum((jnp.cumsum(onehot, 0) - 1) * onehot, 1)
    return (targets, slot_ids)


def serve_plan(owners_all, local_all, ctx_place, ctx_count):
    capacity = plan_capacity(ctx_count)
    targets_all = owners_all.reshape(ctx_count, -1)
    wanted_all = (local_all * H + jnp.arange(H)[None, :, None]).reshape(ctx_count, -1)
    mine = (targets_all == ctx_place).astype(jnp.int32)
    slot_all = jnp.where(mine > 0, jnp.cumsum(mine, 1) - 1, capacity)
    sources = jnp.broadcast_to(jnp.arange(ctx_count)[:, None], slot_all.shape)
    return (
        jnp.zeros((ctx_count, capacity), jnp.int32)
        .at[sources, slot_all]
        .set(wanted_all, mode="drop")
    )


def global_pick(global_ids, ctx_place):
    owned_here = global_ids // BLK_DEV == ctx_place
    return ((global_ids % BLK_DEV)[:, None] == jnp.arange(BLK_DEV)[None, :]) & owned_here[:, None]


def tile_table(paired):
    return (
        paired.reshape(2, BLK_DEV, BLK, H, HD)
        .transpose(1, 3, 0, 2, 4)
        .reshape(BLK_DEV * H, 2, BLK * HD)
    )


def fetch_keys(key_rows, value_rows, queries, meta, ctx_place, ctx_count):
    global_ids, owners, local_ids, owners_all, local_all = (
        meta[2],
        meta[3],
        meta[4],
        meta[5],
        meta[6],
    )
    paired = jnp.stack([key_rows, value_rows])
    extended = padded(paired, (("ctx", 1),), BLK)
    extended = extended.reshape(2, BLK_DEV + 2, BLK, H, HD)
    owned_here = global_ids // BLK_DEV == ctx_place
    triple = jnp.stack([key_rows, value_rows, queries]).reshape(3, BLK_DEV, BLK, D)
    chosen = triple[:, global_ids % BLK_DEV].astype(jnp.float32)
    chosen = jnp.where(owned_here[None, :, None, None], chosen, 0.0)
    global_kv = lax.psum(chosen.astype(jnp.bfloat16), "ctx").reshape(3, 2, BLK, H, HD)
    targets, slot_ids = request_plan(owners, ctx_count)
    route_ids = serve_plan(owners_all, local_all, ctx_place, ctx_count)
    answer = lax.all_to_all(
        tile_table(paired)[route_ids], "ctx", split_axis=0, concat_axis=0, tiled=True
    )
    tiles = answer[targets, slot_ids].reshape(BLK_DEV, H, RND, 2, BLK, HD)
    return (extended, global_kv, tiles, route_ids)


def global_forward(global_q, key_rows, value_rows, meta, ctx_place):
    global_ids, length = (meta[2], meta[7])
    score_scale = HD ** (-0.5)
    key_heads = key_rows.reshape(TOK_DEV, H, HD)
    value_heads = value_rows.reshape(TOK_DEV, H, HD)
    wide = (
        jnp.einsum("gqhd,khd->ghqk", global_q, key_heads, preferred_element_type=jnp.float32)
        * score_scale
    )
    key_live = (ctx_place * TOK_DEV + jnp.arange(TOK_DEV) < length)[None, None, None, :]
    wide = jnp.where(key_live, wide, masked_score)
    local_top = jnp.max(wide, -1, keepdims=True)
    local_total = jnp.sum(jnp.where(key_live, jnp.exp(wide - local_top), 0.0), -1, keepdims=True)
    row_top, row_total = merged((local_top, local_total), "ctx", combine_rows)
    wide_lse = row_top + jnp.log(row_total)
    wide_probs = jnp.where(key_live, jnp.exp(wide - wide_lse), 0.0)
    mixed = jnp.einsum(
        "ghqk,khd->gqhd",
        wide_probs.astype(jnp.bfloat16),
        value_heads,
        preferred_element_type=jnp.float32,
    )
    exact = jnp.einsum(
        "ghqk,khd->gqhd", wide_probs, value_heads.astype(jnp.float32), precision=peak_score
    )
    mixed, exact = (
        lax.psum(mixed.astype(jnp.bfloat16), "ctx").astype(jnp.float32),
        lax.psum(exact.astype(jnp.bfloat16), "ctx").astype(jnp.float32),
    )
    query_live = (global_ids[:, None] * BLK + jnp.arange(BLK)[None, :] < length)[:, None, :, None]
    wide_max = jnp.max(jnp.where(key_live & query_live, wide, masked_score), axis=(0, 2, 3))
    return (mixed.reshape(2, BLK, D).astype(jnp.bfloat16), exact, wide_lse, wide_max)


def window_blocks(extended):
    return jnp.stack([extended[:, offset : offset + BLK_DEV] for offset in range(3)], 2)


def pair_products(rows_four, window_part, global_part, tile_part):
    lead_shape = (BLK_DEV, H, BLK)
    with_window = jnp.einsum(
        "iqhd,iwkhd->ihqwk", rows_four, window_part, preferred_element_type=jnp.float32
    )
    with_global = jnp.einsum(
        "iqhd,gkhd->ihqgk", rows_four, global_part, preferred_element_type=jnp.float32
    )
    with_random = jnp.einsum(
        "iqhd,ihrkd->ihqrk", rows_four, tile_part, preferred_element_type=jnp.float32
    )
    return jnp.concatenate(
        [
            with_window.reshape(lead_shape + (3 * BLK,)),
            with_global.reshape(lead_shape + (2 * BLK,)),
            with_random.reshape(lead_shape + (RND * BLK,)),
        ],
        -1,
    )


def split_slots(weights):
    lead_shape = (BLK_DEV, H, BLK)
    window_weights = weights[..., : 3 * BLK].reshape(lead_shape + (3, BLK))
    global_weights = weights[..., 3 * BLK : 5 * BLK].reshape(lead_shape + (2, BLK))
    random_weights = weights[..., 5 * BLK :].reshape(lead_shape + (RND, BLK))
    return (window_weights, global_weights, random_weights)


def gather_side(weights, window_part, global_part, tile_part):
    window_weights, global_weights, random_weights = split_slots(weights)
    result = jnp.einsum(
        "ihqwk,iwkhd->iqhd", window_weights, window_part, preferred_element_type=jnp.float32
    )
    result = result + jnp.einsum(
        "ihqgk,gkhd->iqhd", global_weights, global_part, preferred_element_type=jnp.float32
    )
    result = result + jnp.einsum(
        "ihqrk,ihrkd->iqhd", random_weights, tile_part, preferred_element_type=jnp.float32
    )
    return result


def scatter_side(weights, rows_four):
    window_weights, global_weights, random_weights = split_slots(weights)
    to_window = jnp.einsum(
        "ihqwk,iqhd->iwkhd", window_weights, rows_four, preferred_element_type=jnp.float32
    )
    to_global = jnp.einsum(
        "ihqgk,iqhd->gkhd", global_weights, rows_four, preferred_element_type=jnp.float32
    )
    to_random = jnp.einsum(
        "ihqrk,iqhd->ihrkd", random_weights, rows_four, preferred_element_type=jnp.float32
    )
    return (to_window, to_global, to_random)


def forward_layer(layer_in, params, meta, ctx_place, ctx_count):
    attn_full, up_full, down_full, gains_full, biases_full, up_bias_full = params
    key_ok, query_ok, global_ids = (meta[0], meta[1], meta[2])
    score_scale = HD ** (-0.5)
    queries = product(layer_in, attn_full[0]).astype(jnp.bfloat16)
    key_rows = product(layer_in, attn_full[1]).astype(jnp.bfloat16)
    value_rows = (product(layer_in, attn_full[2]) + biases_full[0]).astype(jnp.bfloat16)
    extended, global_kv, tiles, route_ids = fetch_keys(
        key_rows, value_rows, queries, meta, ctx_place, ctx_count
    )
    window = window_blocks(extended)
    queries_four = queries.reshape(BLK_DEV, BLK, H, HD)
    key_mask = key_ok[:, :, None, :]
    scores = jnp.where(
        key_mask,
        pair_products(queries_four, window[0], global_kv[0], tiles[:, :, :, 0]) * score_scale,
        masked_score,
    )
    largest = jnp.max(scores, -1, keepdims=True)
    powers = jnp.where(key_mask, jnp.exp(scores - largest), 0.0)
    totals = jnp.sum(powers, -1, keepdims=True)
    attn_probs = powers / totals
    log_total = largest + jnp.log(totals)
    attended = gather_side(
        attn_probs.astype(jnp.bfloat16), window[1], global_kv[1], tiles[:, :, :, 1]
    )
    attended = attended.reshape(BLK_DEV, BLK, D).astype(jnp.bfloat16)
    global_rows, exact, wide_lse, wide_max = global_forward(
        global_kv[2], key_rows, value_rows, meta, ctx_place
    )
    pick = global_pick(global_ids, ctx_place)
    attended = jnp.where(pick[0][:, None, None], global_rows[0][None], attended)
    attended = jnp.where(pick[1][:, None, None], global_rows[1][None], attended)
    attended = attended.reshape(TOK_DEV, D)
    pairs_ok = key_mask & query_ok[:, None, :, None]
    head_max = jnp.maximum(
        jnp.max(jnp.where(pairs_ok, scores, masked_score), axis=(0, 2, 3)), wide_max
    )
    branch = product(attended, attn_full[3]) + biases_full[1]
    first_sum = layer_in.astype(jnp.float32) + branch
    normed = layer_norm(
        first_sum, gains_full[0].astype(jnp.float32), biases_full[3].astype(jnp.float32)
    )
    hidden_pre = product(normed.astype(jnp.bfloat16), up_full) + up_bias_full
    gated = gelu_exact(hidden_pre).astype(jnp.bfloat16)
    second_sum = normed + (product(gated, down_full) + biases_full[2])
    layer_out = layer_norm(
        second_sum, gains_full[1].astype(jnp.float32), biases_full[4].astype(jnp.float32)
    ).astype(jnp.bfloat16)
    saved = (
        layer_in,
        queries,
        extended,
        global_kv,
        tiles,
        route_ids,
        log_total,
        attended,
        first_sum,
        hidden_pre,
        second_sum,
        wide_lse,
        exact,
    )
    return (layer_out, saved, head_max)


def attention_back(
    grad_attended,
    global_rows_grad,
    queries,
    extended,
    global_kv,
    tiles,
    route_ids,
    log_total,
    wide_lse,
    exact,
    meta,
    ctx_place,
    ctx_count,
):
    key_ok, query_ok, global_ids, owners, local_ids = (meta[0], meta[1], meta[2], meta[3], meta[4])
    length = meta[7]
    score_scale = HD ** (-0.5)
    window = window_blocks(extended)
    queries_four = queries.reshape(BLK_DEV, BLK, H, HD)
    grad_rows = grad_attended.reshape(BLK_DEV, BLK, H, HD)
    key_mask = key_ok[:, :, None, :]
    scores = jnp.where(
        key_mask,
        pair_products(queries_four, window[0], global_kv[0], tiles[:, :, :, 0]) * score_scale,
        masked_score,
    )
    attn_probs = jnp.where(key_mask, jnp.exp(scores - log_total), 0.0)
    grad_probs = pair_products(grad_rows, window[1], global_kv[1], tiles[:, :, :, 1])
    centered = jnp.sum(attn_probs * grad_probs, -1, keepdims=True)
    grad_scores = (attn_probs * (grad_probs - centered)).astype(jnp.bfloat16)
    grad_queries = (
        gather_side(grad_scores, window[0], global_kv[0], tiles[:, :, :, 0]) * score_scale
    )
    key_window, key_global, key_random = scatter_side(grad_scores, queries_four)
    value_window, value_global, value_random = scatter_side(
        attn_probs.astype(jnp.bfloat16), grad_rows
    )
    window_grad = jnp.stack([key_window * score_scale, value_window])
    ext_grad = jnp.zeros((2, BLK_DEV + 2, BLK, H, HD), jnp.float32)
    for offset in range(3):
        ext_grad = ext_grad.at[:, offset : offset + BLK_DEV].add(window_grad[:, :, offset])
    ext_grad = ext_grad.reshape(2, BLK_DEV + 2, BLK, D)
    rims = jnp.concatenate([ext_grad[:, 0], ext_grad[:, BLK_DEV + 1]], 1)
    rim_back = padded(rims.astype(jnp.bfloat16), (("ctx", 1),), BLK).astype(rims.dtype)
    kv_grad = ext_grad[:, 1 : BLK_DEV + 1].reshape(2, TOK_DEV, D)
    kv_grad = kv_grad.at[:, :BLK].add(rim_back[:, :BLK])
    kv_grad = kv_grad.at[:, TOK_DEV - BLK :].add(rim_back[:, 3 * BLK :])
    local_kv = extended[:, 1 : BLK_DEV + 1].reshape(2, TOK_DEV, H, HD)
    global_q = global_kv[2]
    key_live = (ctx_place * TOK_DEV + jnp.arange(TOK_DEV) < length)[None, None, None, :]
    wide = (
        jnp.einsum("gqhd,khd->ghqk", global_q, local_kv[0], preferred_element_type=jnp.float32)
        * score_scale
    )
    wide_probs = jnp.where(key_live, jnp.exp(wide - wide_lse), 0.0)
    wide_grad_probs = jnp.einsum(
        "gqhd,khd->ghqk", global_rows_grad, local_kv[1], preferred_element_type=jnp.float32
    )
    wide_center = jnp.einsum(
        "gqhd,gqhd->ghq", global_rows_grad.astype(jnp.float32), exact, precision=peak_score
    )[..., None]
    wide_scores_grad = (wide_probs * (wide_grad_probs - wide_center)).astype(jnp.bfloat16)
    wide_keys = (
        jnp.einsum("ghqk,gqhd->khd", wide_scores_grad, global_q, preferred_element_type=jnp.float32)
        * score_scale
    )
    wide_values = jnp.einsum(
        "ghqk,gqhd->khd",
        wide_probs.astype(jnp.bfloat16),
        global_rows_grad,
        preferred_element_type=jnp.float32,
    )
    wide_queries = (
        jnp.einsum(
            "ghqk,khd->gqhd", wide_scores_grad, local_kv[0], preferred_element_type=jnp.float32
        )
        * score_scale
    )
    kv_grad = kv_grad + jnp.stack([wide_keys, wide_values]).reshape(2, TOK_DEV, D)
    global_grad = jnp.stack([key_global * score_scale, value_global]).reshape(2, 2, BLK, D)
    global_sum, query_total = (
        lax.psum(global_grad.astype(jnp.bfloat16), "ctx").astype(jnp.float32),
        lax.psum(wide_queries.reshape(2, BLK, D).astype(jnp.bfloat16), "ctx").astype(jnp.float32),
    )
    select_matrix = global_pick(global_ids, ctx_place).astype(jnp.float32)
    kv_grad = kv_grad + jnp.einsum(
        "gb,cgkd->cbkd", select_matrix, global_sum, precision=peak_score
    ).reshape(2, TOK_DEV, D)
    tile_grad = jnp.stack([key_random * score_scale, value_random], 3)
    targets, slot_ids = request_plan(owners, ctx_count)
    outgoing = jnp.zeros((ctx_count, route_ids.shape[1], 2, BLK * HD), jnp.float32)
    outgoing = outgoing.at[targets, slot_ids].set(tile_grad.reshape(-1, 2, BLK * HD))
    incoming = lax.all_to_all(
        outgoing.astype(jnp.bfloat16), "ctx", split_axis=0, concat_axis=0, tiled=True
    ).astype(outgoing.dtype)
    table_grad = (
        jnp.zeros((BLK_DEV * H, 2, BLK * HD), jnp.float32)
        .at[route_ids.reshape(-1)]
        .add(incoming.reshape(-1, 2, BLK * HD))
    )
    kv_grad = kv_grad + table_grad.reshape(BLK_DEV, H, 2, BLK, HD).transpose(2, 0, 3, 1, 4).reshape(
        2, TOK_DEV, D
    )
    grad_queries = grad_queries.reshape(TOK_DEV, D) + jnp.einsum(
        "ch,cwv->hwv", select_matrix, query_total, precision=peak_score
    ).reshape(TOK_DEV, D)
    return (
        grad_queries.astype(jnp.bfloat16),
        kv_grad[0].astype(jnp.bfloat16),
        kv_grad[1].astype(jnp.bfloat16),
    )


def backward_layer(grad_out, saved, params, flipped, meta, ctx_place, ctx_count):
    (
        layer_in,
        queries,
        extended,
        global_kv,
        tiles,
        route_ids,
        log_total,
        attended,
        first_sum,
        hidden_pre,
        second_sum,
        wide_lse,
        exact,
    ) = saved
    attn_full, up_full, down_full, gains_full, biases_full, up_bias_full = params
    query_flip, key_flip, value_flip, out_flip, up_flip, down_flip = flipped
    global_ids = meta[2]
    gains_wide = gains_full.astype(jnp.float32)
    shifts_wide = biases_full.astype(jnp.float32)
    normed, first_back = jax.vjp(layer_norm, first_sum, gains_wide[0], shifts_wide[3])
    unused_out, second_back = jax.vjp(layer_norm, second_sum, gains_wide[1], shifts_wide[4])
    grad_second, grad_gain_two, grad_shift_two = second_back(grad_out.astype(jnp.float32))
    grad_down_in = grad_second.astype(jnp.bfloat16)
    gated_wide, gelu_back = jax.vjp(gelu_exact, hidden_pre)
    gated = gated_wide.astype(jnp.bfloat16)
    grad_hidden = gelu_back(product(grad_down_in, down_flip))[0].astype(jnp.bfloat16)
    grad_normed = product(grad_hidden, up_flip) + grad_second
    grad_first, grad_gain_one, grad_shift_one = first_back(grad_normed)
    grad_branch = grad_first.astype(jnp.bfloat16)
    grad_attended = product(grad_branch, out_flip).astype(jnp.bfloat16)
    pick = global_pick(global_ids, ctx_place)
    repeated = global_ids[0] == global_ids[1]
    gather_rows = jnp.stack([pick[0] & jnp.logical_not(repeated), pick[1]]).astype(jnp.float32)
    block_gradients = grad_attended.reshape(BLK_DEV, BLK, D)
    output_rows = jnp.einsum(
        "th,hik->tik", gather_rows, block_gradients.astype(jnp.float32), precision=peak_score
    )
    global_rows_grad = lax.psum(output_rows.astype(jnp.bfloat16), "ctx").reshape(2, BLK, H, HD)
    any_pick = pick[0] | pick[1]
    grad_attended = jnp.where(
        any_pick[:, None, None], jnp.zeros_like(block_gradients), block_gradients
    ).reshape(TOK_DEV, D)
    grad_queries, grad_keys, grad_values = attention_back(
        grad_attended,
        global_rows_grad,
        queries,
        extended,
        global_kv,
        tiles,
        route_ids,
        log_total,
        wide_lse,
        exact,
        meta,
        ctx_place,
        ctx_count,
    )
    grad_in = (
        grad_first
        + product(grad_queries, query_flip)
        + product(grad_keys, key_flip)
        + product(grad_values, value_flip)
    )
    grad_gains = jnp.stack([grad_gain_one, grad_gain_two])
    grad_biases = jnp.stack(
        [
            column_sums(grad_values),
            column_sums(grad_branch),
            column_sums(grad_down_in),
            grad_shift_one,
            grad_shift_two,
        ]
    )
    small = (grad_gains, grad_biases, column_sums(grad_hidden))
    rows = (
        layer_in,
        grad_queries,
        grad_keys,
        grad_values,
        attended,
        grad_branch,
        normed.astype(jnp.bfloat16),
        grad_hidden,
        gated,
        grad_down_in,
    )
    return (grad_in.astype(jnp.bfloat16), small, rows)


def per_device(
    tokens,
    out_cotangent,
    attn_weights,
    up_weights,
    down_weights,
    norm_gains,
    bias_rows,
    up_bias,
    seq_lengths,
    rand_owner,
    rand_local,
    global_raw,
):
    ctx_count = lax.axis_size("ctx")
    ctx_place = lax.axis_index("ctx")
    section = lax.axis_index("section")
    params = (
        lax.all_gather(attn_weights[0], "wsh", axis=1, tiled=True),
        lax.all_gather(up_weights[0], "wsh", axis=0, tiled=True),
        lax.all_gather(down_weights[0], "wsh", axis=0, tiled=True),
        lax.all_gather(norm_gains[0], "wsh", axis=1, tiled=True),
        lax.all_gather(bias_rows[0], "wsh", axis=1, tiled=True),
        lax.all_gather(up_bias[0], "wsh", axis=0, tiled=True),
    )
    micro_count = tokens.shape[0]
    running = jnp.full((H,), masked_score, jnp.float32)
    arrived = jnp.zeros((TOK_DEV, D), jnp.bfloat16)
    outputs = jnp.zeros((micro_count, TOK_DEV, D), jnp.bfloat16)
    kept = []
    for step_index in range(micro_count + 1):
        micro_index = step_index - section
        active = (micro_index >= 0) & (micro_index < micro_count)
        bounded = jnp.clip(micro_index, 0, micro_count - 1)
        meta = sequence_meta(
            bounded, seq_lengths, rand_owner, rand_local, global_raw, ctx_place, ctx_count
        )
        first_in = lax.dynamic_index_in_dim(tokens[:, 0], bounded, 0, keepdims=False)
        layer_in = jnp.where(section == 0, first_in, arrived)
        layer_out, saved, head_max = forward_layer(layer_in, params, meta, ctx_place, ctx_count)
        running = jnp.where(active, jnp.maximum(running, head_max), running)
        outputs = jnp.where(
            active, lax.dynamic_update_index_in_dim(outputs, layer_out, bounded, 0), outputs
        )
        arrived = across_sections(layer_out)
        kept.append(saved)
    stacked = jax.tree.map(lambda *leaves: jnp.stack(leaves), *kept)
    head_tops = lax.pmax(running, ("ctx", "wsh"))
    factor = jnp.sqrt(clip_limit / jnp.maximum(head_tops, clip_limit))
    clipped = (
        attn_weights[0, :2].astype(jnp.float32).reshape(2, -1, H, HD) * factor[None, None, :, None]
    )
    clipped_qk = clipped.reshape(1, 2, -1, D).astype(jnp.bfloat16)
    attn_full = params[0]
    flipped = (
        attn_full[0].T,
        attn_full[1].T,
        attn_full[2].T,
        attn_full[3].T,
        params[1].T,
        params[2].T,
    )
    local_pieces = (
        attn_weights[0],
        up_weights[0],
        down_weights[0],
        norm_gains[0],
        bias_rows[0],
        up_bias[0],
    )
    grad_shards = tuple((jnp.zeros(piece.shape, jnp.float32) for piece in local_pieces))
    small_total = (
        jnp.zeros((2, D), jnp.float32),
        jnp.zeros((5, D), jnp.float32),
        jnp.zeros((FF,), jnp.float32),
    )
    row_pieces = []
    arrived = jnp.zeros((TOK_DEV, D), jnp.bfloat16)
    input_grads = jnp.zeros((micro_count, TOK_DEV, D), jnp.bfloat16)
    for step_index in range(micro_count + 1):
        micro_index = step_index - 1 + section
        active = (micro_index >= 0) & (micro_index < micro_count)
        bounded = jnp.clip(micro_index, 0, micro_count - 1)
        meta = sequence_meta(
            bounded, seq_lengths, rand_owner, rand_local, global_raw, ctx_place, ctx_count
        )
        last_cot = lax.dynamic_index_in_dim(out_cotangent[:, 0], bounded, 0, keepdims=False)
        grad_out = jnp.where(section == 1, last_cot, arrived)
        grad_out = jnp.where(active, grad_out, jnp.zeros_like(grad_out))
        stash_index = jnp.clip(step_index - 1 + 2 * section, 0, micro_count)
        saved = jax.tree.map(
            lambda leaves: lax.dynamic_index_in_dim(leaves, stash_index, 0, keepdims=False), stacked
        )
        grad_in, small, rows = backward_layer(
            grad_out, saved, params, flipped, meta, ctx_place, ctx_count
        )
        input_grads = jnp.where(
            active, lax.dynamic_update_index_in_dim(input_grads, grad_in, bounded, 0), input_grads
        )
        arrived = across_sections(grad_in)
        small_total = tuple((accum + update for accum, update in zip(small_total, small)))
        row_pieces.append(rows)
    all_rows = tuple((jnp.concatenate(pieces, 0) for pieces in zip(*row_pieces)))
    grad_shards = spread_grads(weight_grads(all_rows) + small_total)
    final = (
        lax.psum(grad_shards[0].astype(jnp.bfloat16), "ctx").astype(jnp.float32),
        lax.psum(grad_shards[1].astype(jnp.bfloat16), "ctx").astype(jnp.float32),
        lax.psum(grad_shards[2].astype(jnp.bfloat16), "ctx").astype(jnp.float32),
        lax.psum(grad_shards[3].astype(jnp.bfloat16), "ctx").astype(jnp.float32),
        lax.psum(grad_shards[4].astype(jnp.bfloat16), "ctx").astype(jnp.float32),
        lax.psum(grad_shards[5].astype(jnp.bfloat16), "ctx").astype(jnp.float32),
    )
    return (
        outputs[None, :, None],
        input_grads[None, :, None],
        final[0][None],
        final[1][None],
        final[2][None],
        final[3][None],
        final[4][None],
        final[5][None],
        clipped_qk,
    )


def solution(mesh):
    placed = (
        P(None, "wsh", "ctx", None),
        P(None, "wsh", "ctx", None),
        P("section", None, "wsh", None),
        P("section", "wsh", None),
        P("section", "wsh", None),
        P("section", None, "wsh"),
        P("section", None, "wsh"),
        P("section", "wsh"),
        P(None, "wsh"),
        P(None, "wsh", None, None, None),
        P(None, "wsh", None, None, None),
        P(None, "wsh", None),
    )
    return jax.shard_map(
        per_device,
        mesh=mesh,
        in_specs=placed,
        out_specs=(
            P("section", None, "wsh", "ctx", None),
            P("section", None, "wsh", "ctx", None),
            P("section", None, "wsh", None),
            P("section", "wsh", None),
            P("section", "wsh", None),
            P("section", None, "wsh"),
            P("section", None, "wsh"),
            P("section", "wsh"),
            P("section", None, "wsh", None),
        ),
        check_vma=False,
    )
```

profile of v0, /device:TPU:25, one launch (start us, length us, event | category | flops | bytes accessed | tf_op | source)
XLA Modules:
  0.0 2194.6 jit_solution(9455118532528468921)
XLA Ops:
  11.9 8.3 fusion.618
  21.6 26.8 %scatter_fusion = s32[8,18]{1,0:T(8,128)S(1)} fusion(s32[8,18]{1,0:T(8,128)S(1)} %broadcast.3059.clone, s32[576]{0:T(1024)S(1)} %reshape.3818, s32[576]{0:T(1024)S(1)} %reshape.3820), kind=kCustom, calls=%fused_computation.9 | custom fusion | bytes 11520 | tf_op jit(solution)/shard_map/scatter | solution.py:189
  53.8 19.6 all-gather.16.cloned.1.call-done
  81.2 52.9 %all-reduce.24.cloned.1.call-done = bf16[3,2,64,768]{3,2,0,1:T(8,128)(2,1)} async-done(((bf16[3,2,64,768]{3,2,0,1:T(8,128)(2,1)}), bf16[3,2,64,768]{3,2,0,1:T(8,128)(2,1)}) %all-reduce.24.cloned.1.call-update) | async-done | bytes 589840 | tf_op jit(solution)/shard_map/psum | solution.py:221
  137.0 15.4 all-gather.2
  153.5 14.0 all-gather.3
  210.8 8.3 fusion.620
  219.9 8.3 fusion.619
  228.5 26.8 %scatter_fusion.2 = s32[8,18]{1,0:T(8,128)S(1)} fusion(s32[8,18]{1,0:T(8,128)S(1)} %broadcast.3059.clone.1, s32[576]{0:T(1024)S(1)} %reshape.3830, s32[576]{0:T(1024)S(1)} %reshape.3832), kind=kCustom, calls=%fused_computation.11 | custom fusion | bytes 11520 | tf_op jit(solution)/shard_map/scatter | solution.py:189
  255.3 26.8 %scatter_fusion.1 = s32[8,18]{1,0:T(8,128)S(1)} fusion(s32[8,18]{1,0:T(8,128)S(1)} %broadcast.3059.clone.2, s32[576]{0:T(1024)S(1)} %reshape.3824, s32[576]{0:T(1024)S(1)} %reshape.3826), kind=kCustom, calls=%fused_computation.10 | custom fusion | bytes 11520 | tf_op jit(solution)/shard_map/scatter | solution.py:189
  305.8 10.7 gather_fusion.1
  316.6 8.9 all-to-all-start
  370.2 7.5 all-to-all-done
  377.6 11.5 gather_fusion.2
  420.1 6.6 fusion.977
  443.5 10.7 gather_fusion.4
  454.2 42.6 %all-to-all-start.1 = ((bf16[8,18,2,4096]{3,2,1,0:T(2,128)(2,1)}), bf16[8,18,2,4096]{3,2,1,0:T(2,128)(2,1)}, u32[]{:S(2)}, u32[]{:S(2)}) async-start(bf16[8,18,2,4096]{3,2,1,0:T(2,128)(2,1)} %bitcast.127), calls=%async_computation.1 | async-start | bytes 4718592 | tf_op jit(solution)/shard_map/all_to_all | solution.py:224
  521.2 54.5 %all-reduce.28.cloned.1.call-done = bf16[3,2,64,768]{3,2,0,1:T(8,128)(2,1)} async-done(((bf16[3,2,64,768]{3,2,0,1:T(8,128)(2,1)}), bf16[3,2,64,768]{3,2,0,1:T(8,128)(2,1)}) %all-reduce.28.cloned.1.call-update) | async-done | bytes 589840 | tf_op jit(solution)/shard_map/psum | solution.py:221
  584.7 15.4 all-gather.8
  601.1 14.0 all-gather.9
  615.9 5.6 while.67
  630.7 45.7 %all-reduce.30.cloned.1.call-done = bf16[2,64,12,64]{1,3,0,2:T(8,128)(2,1)} async-done(((bf16[2,64,12,64]{1,3,0,2:T(8,128)(2,1)}), bf16[2,64,12,64]{1,3,0,2:T(8,128)(2,1)}) %all-reduce.30.cloned.1.call-update) | async-done | bytes 196624 | tf_op jit(solution)/shard_map/psum | solution.py:257
  679.0 11.5 gather_fusion.5
  701.1 5.4 select_reduce_fusion.1
  721.8 6.7 fusion.979
  745.4 10.7 gather_fusion.7
  756.1 8.5 all-to-all-start.2
  776.6 7.0 constant_dynamic-slice_fusion.10
  856.2 64.3 %all-gather.10 = f32[16,12,64]{2,1,0:T(8,128)S(1)} all-gather(f32[2,12,64]{2,1,0:T(8,128)S(1)} %copy.1858), channel_id=12, replica_groups=mesh['section'=2,'ctx'=8,'wsh'=2] {'ctx'}, dimensions={0}, use_global_device_ids=true | all-gather | bytes 55296 | tf_op jit(solution)/shard_map/all_gather | solution.py:50
  921.6 14.2 all-gather.11
  937.9 9.9 while.68
  973.6 33.5 %all-reduce.34.cloned.1.call-done = bf16[2,64,12,64]{1,3,0,2:T(8,128)(2,1)} async-done(((bf16[2,64,12,64]{1,3,0,2:T(8,128)(2,1)}), bf16[2,64,12,64]{1,3,0,2:T(8,128)(2,1)}) %all-reduce.34.cloned.1.call-update) | async-done | bytes 196624 | tf_op jit(solution)/shard_map/psum | solution.py:257
  1008.5 11.4 gather_fusion.8
  1031.8 5.4 select_reduce_fusion
  1057.5 6.7 fusion.981
  1067.3 11.4 fusion.125
  1105.7 6.8 multiply_convert_fusion.2
  1157.6 11.5 scatter_fusion.3
  1169.1 6.0 convert_element_type.752
  1175.1 7.8 all-to-all-start.3
  1210.6 71.3 %all-reduce.48.cloned.1.call-done = (bf16[2,64,12,64]{3,1,0,2:T(8,128)(2,1)}, bf16[1,2,64,12,64]{2,4,1,3,0:T(8,128)(2,1)}, bf16[1,2,64,12,64]{2,4,1,3,0:T(8,128)(2,1)}, bf16[1,2,64,12,64]{2,4,1,3,0:T(8,128)(2,1)}) async-done(((bf16[2,64,12,64]{3,1,0,2:T(8,128)(2,1)}, bf16[1,2,64,12,64]{2,4,1,3,0:T(8,128)(2,1)}, bf16[1,2,64,12,64]{2,4,1,3,0:T(8,128)(2,1)}, bf16[1,2,64,12,64]{2,4,1,3,0:T(8,128)(2,1)}), ...) | async-done | bytes 786448 | tf_op jit(solution)/shard_map/psum | solution.py:546
  1294.0 53.0 %all-reduce.46.cloned.1.call-done = (bf16[2,64,768]{2,0,1:T(2,128)(2,1)}, bf16[2,2,64,768]{3,1,2,0:T(2,128)(2,1)}) async-done(((bf16[2,64,768]{2,0,1:T(2,128)(2,1)}, bf16[2,2,64,768]{3,1,2,0:T(2,128)(2,1)}), (bf16[2,64,768]{2,0,1:T(2,128)(2,1)}, bf16[2,2,64,768]{3,1,2,0:T(2,128)(2,1)})) %all-reduce.46.cloned.1.call-update) | async-done | bytes 589840 | tf_op jit(solution)/shard_map/psum | solution.py:476
  1358.7 6.1 bitcast_convert_fusion.2
  1365.2 22.1 %scatter_fusion.4 = f32[24,2,4096]{2,1,0:T(2,128)S(1)} fusion(f32[24,2,4096]{2,1,0:T(2,128)S(1)} %broadcast.3112.clone, s32[144]{0:T(256)S(1)} %bitcast.2365, f32[144,2,4096]{2,1,0:T(2,128)} %bitcast_convert_fusion.2), kind=kCustom, calls=%fused_computation.13 | custom fusion | flops 1179648 | bytes 14156352 | tf_op jit(solution)/shard_map/scatter-add | solution.py:492
  1424.6 6.9 multiply_convert_fusion.1
  1467.7 11.5 scatter_fusion.5
  1479.2 6.0 convert_element_type.775
  1485.2 8.7 all-to-all-start.4
  1519.2 64.3 %all-reduce.44.cloned.1.call-done = (bf16[2,64,768]{2,0,1:T(2,128)(2,1)}, bf16[2,2,64,768]{3,1,2,0:T(2,128)(2,1)}) async-done(((bf16[2,64,768]{2,0,1:T(2,128)(2,1)}, bf16[2,2,64,768]{3,1,2,0:T(2,128)(2,1)}), (bf16[2,64,768]{2,0,1:T(2,128)(2,1)}, bf16[2,2,64,768]{3,1,2,0:T(2,128)(2,1)})) %all-reduce.44.cloned.1.call-update) | async-done | bytes 589840 | tf_op jit(solution)/shard_map/psum | solution.py:476
  1594.2 6.1 bitcast_convert_fusion.1
  1600.6 22.3 %scatter_fusion.6 = f32[24,2,4096]{2,1,0:T(2,128)S(1)} fusion(f32[24,2,4096]{2,1,0:T(2,128)S(1)} %broadcast.3112.clone.1, s32[144]{0:T(256)S(1)} %bitcast.2364, f32[144,2,4096]{2,1,0:T(2,128)} %bitcast_convert_fusion.1), kind=kCustom, calls=%fused_computation.15 | custom fusion | flops 1179648 | bytes 14156352 | tf_op jit(solution)/shard_map/scatter-add | solution.py:492
  1665.9 12.0 multiply_convert_fusion
  1685.3 54.3 %all-reduce.38.cloned.1.call-done = bf16[2,64,12,64]{3,1,0,2:T(8,128)(2,1)} async-done(((bf16[2,64,12,64]{3,1,0,2:T(8,128)(2,1)}), bf16[2,64,12,64]{3,1,0,2:T(8,128)(2,1)}) %all-reduce.38.cloned.1.call-update) | async-done | bytes 196624 | tf_op jit(solution)/shard_map/psum | solution.py:546
  1746.3 6.4 convolution_convert_fusion.1
  1802.0 13.6 scatter_fusion.7
  1815.6 6.0 convert_element_type.798
  1821.7 7.8 all-to-all-start.5
  1862.2 19.3 all-to-all-done.5
  1881.5 6.1 bitcast_convert_fusion
  1888.0 22.1 %scatter_fusion.8 = f32[24,2,4096]{2,1,0:T(2,128)S(1)} fusion(f32[24,2,4096]{2,1,0:T(2,128)S(1)} %broadcast.3112, s32[144]{0:T(256)S(1)} %bitcast.2366, f32[144,2,4096]{2,1,0:T(2,128)} %bitcast_convert_fusion), kind=kCustom, calls=%fused_computation.17 | custom fusion | flops 1179648 | bytes 14156352 | tf_op jit(solution)/shard_map/scatter-add | solution.py:492
  1929.5 67.7 %reduce-scatter.10.cloned.1.call-done = bf16[4,384,768]{2,1,0:T(8,128)(2,1)} async-done(((bf16[4,768,768]{2,1,0:T(8,128)(2,1)}), bf16[4,384,768]{2,1,0:T(8,128)(2,1)}) %reduce-scatter.10.cloned.1.call-update) | async-done | bytes 2359312 | tf_op jit(solution)/shard_map/reduce_scatter | solution.py:89
  2001.2 27.1 %pmax.7 = f32[12]{0:T(128)S(1)} all-reduce(f32[12]{0:T(128)} %broadcast_select_fusion.5), channel_id=1, replica_groups=mesh['section'=2,'ctx'=8,'wsh'=2] {'ctx','wsh'}, use_global_device_ids=true, to_apply=%region_141.142 | all-reduce | flops 12 | bytes 96 | tf_op jit(solution)/shard_map/pmax | solution.py:645
  2046.6 29.7 %all-reduce.4 = (bf16[1,5,384]{2,1,0:T(8,128)(2,1)S(1)}, bf16[1,2,384]{2,1,0:T(2,128)(2,1)S(1)}, bf16[1,1536]{1,0:T(2,128)(2,1)S(1)}) all-reduce(bf16[1,5,384]{2,1,0:T(8,128)(2,1)S(1)} %bitcast.2356, bf16[1,2,384]{2,1,0:T(2,128)(2,1)S(1)} %bitcast.2363, ...), channel_id=1, replica_groups=mesh['section'=2,'ctx'=8,'wsh'=2] {'ctx'}, use_global_device_ids=true, to_apply=%region_129.130 | all-reduce | flops 4224 | bytes 16896 | tf_op jit(solution)/shard_map/psum | solution.py:707
  2078.1 99.7 %all-reduce.40.cloned.1.call-done = (bf16[1,4,384,768]{3,2,1,0:T(8,128)(2,1)}, bf16[1,384,3072]{2,1,0:T(8,128)(2,1)}, bf16[1,1536,768]{2,1,0:T(8,128)(2,1)}) async-done(((bf16[1,4,384,768]{3,2,1,0:T(8,128)(2,1)}, bf16[1,384,3072]{2,1,0:T(8,128)(2,1)}, bf16[1,1536,768]{2,1,0:T(8,128)(2,1)}), (bf16[1,4,384,768]{3,2,1,0:T(8,128)(2,1)}, bf16[1,384,3072]{2,1,0:T(8,128)(2,1)}, ...) | async-done | bytes 7077904 | tf_op jit(solution)/shard_map/psum | solution.py:703
  (1969 shorter events, 849.6 us)
Async XLA Ops:
  7.2 66.2 %all-gather.16.cloned.1.call-start = ((), (), s32[]{:S(2)}) async-start(), calls=%async_computation.22 | async-start | bytes 7077888 | tf_op jit(solution)/shard_map/all_gather | solution.py:616
  7.9 126.1 %all-reduce.24.cloned.1.call-start = ((), (), s32[]{:S(2)}) async-start(), calls=%async_computation.11 | async-start | bytes 1179648 | tf_op jit(solution)/shard_map/psum | solution.py:221
  21.6 51.8 %copy-start.213 = (bf16[2,1,128,768]{3,2,1,0:T(8,128)(2,1)S(1)}, bf16[2,1,128,768]{3,2,1,0:T(8,128)(2,1)}, u32[]{:S(2)}) copy-start(bf16[2,1,128,768]{3,2,1,0:T(8,128)(2,1)} %param.48) | copy-start | bytes 1179652
  75.0 257.8 %copy-start.182 = (bf16[128,768]{1,0:T(8,128)(2,1)}, bf16[128,768]{1,0:T(8,128)(2,1)S(1)}, u32[]{:S(2)}) copy-start(bf16[128,768]{1,0:T(8,128)(2,1)S(1)} %convolution_convert_fusion.19) | copy-start | bytes 589828
  80.1 287.5 %all-reduce.26.cloned.1.call-start = ((), (), s32[]{:S(2)}) async-start(), calls=%async_computation.12 | async-start | bytes 786432 | tf_op jit(solution)/shard_map/psum | solution.py:257
  80.8 87.5 %copy-start.375 = (pred[128]{0:T(512)(128)(4,1)}, pred[128]{0:T(512)(128)(4,1)S(1)}, u32[]{:S(2)}) copy-start(pred[128]{0:T(512)(128)(4,1)S(1)} %fusion.792) | copy-start | bytes 388
  81.0 221.8 %copy-start.234 = (bf16[128,768]{0,1:T(8,128)(2,1)}, bf16[128,768]{0,1:T(8,128)(2,1)S(1)}, u32[]{:S(2)}) copy-start(bf16[128,768]{0,1:T(8,128)(2,1)S(1)} %copy.1747) | copy-start | bytes 589828
  169.7 247.1 %all-gather.18.cloned.1.call-start = ((), (), s32[]{:S(2)}) async-start(), calls=%async_computation.23 | async-start | bytes 7077888 | tf_op jit(solution)/shard_map/all_gather | solution.py:617
  170.3 249.8 %all-gather.20.cloned.1.call-start = ((), (), s32[]{:S(2)}) async-start(), calls=%async_computation.24 | async-start | bytes 7077888 | tf_op jit(solution)/shard_map/all_gather | solution.py:618
  172.8 46.3 %copy-start.300 = (s32[1,1,2,12,3]{2,1,4,3,0:T(1,128)}, s32[1,1,2,12,3]{2,1,4,3,0:T(1,128)S(1)}, u32[]{:S(2)}) copy-start(s32[1,1,2,12,3]{2,1,4,3,0:T(1,128)S(1)} %get-tuple-element.1102) | copy-start | bytes 868
  176.7 106.5 %copy-start.436 = (pred[2]{0:T(512)(128)(4,1)}, pred[2]{0:T(512)(128)(4,1)S(1)}, u32[]{:S(2)}) copy-start(pred[2]{0:T(512)(128)(4,1)S(1)} %fusion.800) | copy-start | bytes 10
  179.7 107.3 %copy-start.434 = (pred[2]{0:T(512)(128)(4,1)}, pred[2]{0:T(512)(128)(4,1)S(1)}, u32[]{:S(2)}) copy-start(pred[2]{0:T(512)(128)(4,1)S(1)} %fusion.801) | copy-start | bytes 10
  316.6 61.0 %all-to-all-start = ((bf16[8,18,2,4096]{3,2,1,0:T(2,128)(2,1)}), bf16[8,18,2,4096]{3,2,1,0:T(2,128)(2,1)}, u32[]{:S(2)}, u32[]{:S(2)}) async-start(bf16[8,18,2,4096]{3,2,1,0:T(2,128)(2,1)} %bitcast.58), calls=%async_computation | async-start | bytes 4718592 | tf_op jit(solution)/shard_map/all_to_all | solution.py:224
  328.6 5.9 collective-permute-start.1
  330.9 3.7 collective-permute-start
  427.9 5.3 collective-permute-start.2
  434.9 65.5 %copy-start.184 = (bf16[128,768]{1,0:T(8,128)(2,1)}, bf16[128,768]{1,0:T(8,128)(2,1)S(1)}, u32[]{:S(2)}) copy-start(bf16[128,768]{1,0:T(8,128)(2,1)S(1)} %convolution_convert_fusion.17) | copy-start | bytes 589828
  435.7 83.6 %copy-start.134 = (bf16[2,64,12,64,1]{3,1,4,2,0:T(8,128)(2,1)}, bf16[2,64,12,64,1]{3,1,4,2,0:T(8,128)(2,1)S(1)}, u32[]{:S(2)}) copy-start(bf16[2,64,12,64,1]{3,1,4,2,0:T(8,128)(2,1)S(1)} %copy.2178) | copy-start | bytes 589828
  454.2 224.8 %all-to-all-start.1 = ((bf16[8,18,2,4096]{3,2,1,0:T(2,128)(2,1)}), bf16[8,18,2,4096]{3,2,1,0:T(2,128)(2,1)}, u32[]{:S(2)}, u32[]{:S(2)}) async-start(bf16[8,18,2,4096]{3,2,1,0:T(2,128)(2,1)} %bitcast.127), calls=%async_computation.1 | async-start | bytes 4718592 | tf_op jit(solution)/shard_map/all_to_all | solution.py:224
  496.8 78.9 %all-reduce.28.cloned.1.call-start = ((), (), s32[]{:S(2)}) async-start(), calls=%async_computation.13 | async-start | bytes 1179648 | tf_op jit(solution)/shard_map/psum | solution.py:221
  496.8 5.5 collective-permute-start.4
  499.1 3.3 collective-permute-start.3
  502.3 174.1 %all-reduce.30.cloned.1.call-start = ((), (), s32[]{:S(2)}) async-start(), calls=%async_computation.14 | async-start | bytes 786432 | tf_op jit(solution)/shard_map/psum | solution.py:257
  729.7 5.3 collective-permute-start.5
  756.1 252.3 %all-to-all-start.2 = ((bf16[8,18,2,4096]{3,2,1,0:T(2,128)(2,1)}), bf16[8,18,2,4096]{3,2,1,0:T(2,128)(2,1)}, u32[]{:S(2)}, u32[]{:S(2)}) async-start(bf16[8,18,2,4096]{3,2,1,0:T(2,128)(2,1)} %bitcast.193), calls=%async_computation.2 | async-start | bytes 4718592 | tf_op jit(solution)/shard_map/all_to_all | solution.py:224
  764.6 75.9 %all-reduce.32.cloned.1.call-start = ((), (), s32[]{:S(2)}) async-start(), calls=%async_computation.15 | async-start | bytes 1179648 | tf_op jit(solution)/shard_map/psum | solution.py:221
  766.5 240.6 %all-reduce.34.cloned.1.call-start = ((), (), s32[]{:S(2)}) async-start(), calls=%async_computation.16 | async-start | bytes 786432 | tf_op jit(solution)/shard_map/psum | solution.py:257
  766.6 5.2 collective-permute-start.7
  768.9 3.3 collective-permute-start.6
  771.1 319.1 %copy-start.31 = (bf16[2,64,12,64]{1,0,3,2:T(2,128)(2,1)}, bf16[2,64,12,64]{1,0,3,2:T(2,128)(2,1)S(1)}, u32[]{:S(2)}) copy-start(bf16[2,64,12,64]{1,0,3,2:T(2,128)(2,1)S(1)} %reshape.3634) | copy-start | bytes 589828
  771.5 191.8 %copy-start.28 = (bf16[2,64,12,64]{1,0,3,2:T(2,128)(2,1)}, bf16[2,64,12,64]{1,0,3,2:T(2,128)(2,1)S(1)}, u32[]{:S(2)}) copy-start(bf16[2,64,12,64]{1,0,3,2:T(2,128)(2,1)S(1)} %reshape.3662) | copy-start | bytes 589828
  771.8 193.0 %copy-start.25 = (bf16[2,64,12,64]{1,0,3,2:T(2,128)(2,1)}, bf16[2,64,12,64]{1,0,3,2:T(2,128)(2,1)S(1)}, u32[]{:S(2)}) copy-start(bf16[2,64,12,64]{1,0,3,2:T(2,128)(2,1)S(1)} %reshape.3690) | copy-start | bytes 589828
  853.5 67.0 %copy-start.334 = (pred[2,64,128]{2,1,0:T(8,128)(4,1)S(1)}, pred[2,64,128]{2,1,0:T(8,128)(4,1)}, u32[]{:S(2)}) copy-start(pred[2,64,128]{2,1,0:T(8,128)(4,1)} %broadcast_and_fusion) | copy-start | bytes 49156
  855.9 64.7 %copy-start.75 = (f32[12,128,128]{1,2,0}, f32[12,128,128]{1,2,0:S(1)}, u32[]{:S(2)}) copy-start(f32[12,128,128]{1,2,0:S(1)} %fusion.987) | copy-start | bytes 2359300
  1084.3 106.7 %copy-start.441 = (f32[128]{0:T(128)}, f32[128]{0:T(128)S(1)}, u32[]{:S(2)}) copy-start(f32[128]{0:T(128)S(1)} %get-tuple-element.743) | copy-start | bytes 1540
  1175.1 183.6 %all-to-all-start.3 = ((bf16[8,18,2,4096]{3,2,1,0:T(2,128)(2,1)}), bf16[8,18,2,4096]{3,2,1,0:T(2,128)(2,1)}, u32[]{:S(2)}, u32[]{:S(2)}) async-start(bf16[8,18,2,4096]{3,2,1,0:T(2,128)(2,1)} %convert_element_type.752), calls=%async_computation.3 | async-start | bytes 4718592 | tf_op jit(solution)/shard_map/all_to_all | solution.py:486
  1182.9 99.1 %all-reduce.48.cloned.1.call-start = ((), (), s32[]{:S(2)}) async-start(), calls=%async_computation.31 | async-start | bytes 3145728 | tf_op jit(solution)/shard_map/psum | solution.py:546
  1186.8 21.9 collective-permute-start.9
  1189.7 18.9 collective-permute-start.8
  1203.7 143.3 %all-reduce.46.cloned.1.call-start = ((), (), s32[]{:S(2)}) async-start(), calls=%async_computation.30 | async-start | bytes 1179648 | tf_op jit(solution)/shard_map/psum | solution.py:476
  1290.5 216.9 %all-reduce.36.cloned.1.call-start = ((), (), s32[]{:S(2)}) async-start(), calls=%async_computation.17 | async-start | bytes 786432 | tf_op jit(solution)/shard_map/psum | solution.py:546
  1293.0 57.3 %copy-start.150 = (bf16[2,12,64,128]{2,3,1,0:T(8,128)(2,1)S(1)}, bf16[2,12,64,128]{2,3,1,0:T(8,128)(2,1)}, u32[]{:S(2)}) copy-start(bf16[2,12,64,128]{2,3,1,0:T(8,128)(2,1)} %slice.1384) | copy-start | bytes 1179652
  1293.1 57.3 %copy-start.158 = (f32[2,64,12,64]{1,3,2,0:T(8,128)S(1)}, f32[2,64,12,64]{1,3,2,0:T(8,128)}, u32[]{:S(2)}) copy-start(f32[2,64,12,64]{1,3,2,0:T(8,128)} %convolution_bitcast_fusion.31) | copy-start | bytes 1179652
  1399.8 4.9 collective-permute-start.10
  1485.2 108.9 %all-to-all-start.4 = ((bf16[8,18,2,4096]{3,2,1,0:T(2,128)(2,1)}), bf16[8,18,2,4096]{3,2,1,0:T(2,128)(2,1)}, u32[]{:S(2)}, u32[]{:S(2)}) async-start(bf16[8,18,2,4096]{3,2,1,0:T(2,128)(2,1)} %convert_element_type.775), calls=%async_computation.4 | async-start | bytes 4718592 | tf_op jit(solution)/shard_map/all_to_all | solution.py:486
  1493.9 89.6 %all-reduce.44.cloned.1.call-start = ((), (), s32[]{:S(2)}) async-start(), calls=%async_computation.29 | async-start | bytes 1179648 | tf_op jit(solution)/shard_map/psum | solution.py:476
  1498.7 18.4 collective-permute-start.12
  1501.6 15.5 collective-permute-start.11
  1517.0 222.5 %all-reduce.38.cloned.1.call-start = ((), (), s32[]{:S(2)}) async-start(), calls=%async_computation.18 | async-start | bytes 786432 | tf_op jit(solution)/shard_map/psum | solution.py:546
  1517.1 66.4 %copy-start.419 = (pred[2,2]{1,0:T(4,128)(4,1)S(1)}, pred[2,2]{1,0:T(4,128)(4,1)}, u32[]{:S(2)}) copy-start(pred[2,2]{1,0:T(4,128)(4,1)} %copy-done.418) | copy-start | bytes 16
  1518.1 67.5 %copy-start.152 = (bf16[2,12,64,128]{2,3,1,0:T(8,128)(2,1)S(1)}, bf16[2,12,64,128]{2,3,1,0:T(8,128)(2,1)}, u32[]{:S(2)}) copy-start(bf16[2,12,64,128]{2,3,1,0:T(8,128)(2,1)} %slice.1411) | copy-start | bytes 1179652
  1635.5 4.9 collective-permute-start.13
  1683.9 167.3 %all-reduce.42.cloned.1.call-start = ((), (), s32[]{:S(2)}) async-start(), calls=%async_computation.28 | async-start | bytes 1179648 | tf_op jit(solution)/shard_map/psum | solution.py:475
  1746.2 180.7 %reduce-scatter.12.cloned.1.call-start = ((), (), s32[]{:S(2)}) async-start(), calls=%async_computation.20 | async-start | bytes 7077888 | tf_op jit(solution)/shard_map/reduce_scatter | solution.py:92
  1752.8 176.7 %reduce-scatter.14.cloned.1.call-start = ((), (), s32[]{:S(2)}) async-start(), calls=%async_computation.21 | async-start | bytes 7077888 | tf_op jit(solution)/shard_map/reduce_scatter | solution.py:95
  1785.7 44.8 %copy-start.43 = (bf16[2,12,64,192]{2,3,1,0:T(8,128)(2,1)}, bf16[2,12,64,192]{2,3,1,0:T(8,128)(2,1)S(1)}, u32[]{:S(2)}) copy-start(bf16[2,12,64,192]{2,3,1,0:T(8,128)(2,1)S(1)} %get-tuple-element.894) | copy-start | bytes 1769476
  1821.7 59.9 %all-to-all-start.5 = ((bf16[8,18,2,4096]{3,2,1,0:T(2,128)(2,1)}), bf16[8,18,2,4096]{3,2,1,0:T(2,128)(2,1)}, u32[]{:S(2)}, u32[]{:S(2)}) async-start(bf16[8,18,2,4096]{3,2,1,0:T(2,128)(2,1)} %convert_element_type.798), calls=%async_computation.5 | async-start | bytes 4718592 | tf_op jit(solution)/shard_map/all_to_all | solution.py:486
  1829.4 167.7 %reduce-scatter.10.cloned.1.call-start = ((), (), s32[]{:S(2)}) async-start(), calls=%async_computation.19 | async-start | bytes 7077888 | tf_op jit(solution)/shard_map/reduce_scatter | solution.py:89
  1837.8 13.1 collective-permute-start.15
  1840.3 10.7 collective-permute-start.14
  1923.6 114.7 %reduce-scatter.16.cloned.1.call-start = ((), (), s32[]{:S(2)}) async-start(), calls=%async_computation.25 | async-start | bytes 294912
  1925.8 119.7 %reduce-scatter.18.cloned.1.call-start = ((), (), s32[]{:S(2)}) async-start(), calls=%async_computation.26 | async-start | bytes 294912
  1926.8 251.0 %all-reduce.40.cloned.1.call-start = ((), (), s32[]{:S(2)}) async-start(), calls=%async_computation.27 | async-start | bytes 14155776 | tf_op jit(solution)/shard_map/psum | solution.py:703
  2045.5 136.7 %copy-start.257 = (bf16[1,2,1,128,768]{4,3,1,2,0:T(8,128)(2,1)}, bf16[1,2,1,128,768]{4,3,1,2,0:T(8,128)(2,1)S(1)}, u32[]{:S(2)}) copy-start(bf16[1,2,1,128,768]{4,3,1,2,0:T(8,128)(2,1)S(1)} %fusion.306) | copy-start | bytes 1179652
  (456 other events, 1976.8 us)
Sparse Core Ops, SparseCore 0:
  9.6 63.7 all-gather.15
  80.2 53.8 all-reduce.23
  169.8 53.2 all-reduce.25
  224.6 64.4 all-gather.17
  290.5 62.6 all-gather.19
  502.4 73.2 all-reduce.27
  623.1 53.1 all-reduce.29
  767.8 72.3 all-reduce.31
  952.4 54.6 all-reduce.33
  1203.8 78.1 all-reduce.47
  1290.6 56.3 all-reduce.45
  1443.4 55.7 all-reduce.35
  1517.1 66.3 all-reduce.43
  1684.0 55.4 all-reduce.37
  1746.3 55.6 all-reduce.41
  1804.9 61.8 reduce-scatter.11
  1869.4 59.9 reduce-scatter.13
  1932.3 64.8 reduce-scatter.9
  1999.4 11.0 reduce-scatter.15
  2012.6 11.0 reduce-scatter.17
  2026.3 151.5 all-reduce.39
where the time goes:
time: 2210 us; the launch traced here: 2190 us
  waiting for transfers between devices  656 us (30%)
  local copies, waits for them, and re-layouts  601 us (27%)
  other arithmetic  359 us (16%)
  matrix products  224 us (10%)
  blocking collectives  210 us (10%)
  starting transfers between devices  114 us (5%)
  between operations  30.6 us (1%)
    all_gather x6, blocking collectives, merged(): everything = jax.tree.map(lambda part: lax.all_gather(part, axis), value)  137 us
    psum x3, waiting for transfers between devices, backward_layer(): lax.psum(output_rows.astype(jnp.bfloat16), 'ctx').reshape(2, BLK, H, HD)  126 us
    psum x2, waiting for transfers between devices, attention_back(): lax.psum(wide_queries.reshape(2, BLK, D).astype(jnp.bfloat16), 'ctx')  117 us
    psum x3, waiting for transfers between devices, fetch_keys(): lax.psum(chosen.astype(jnp.bfloat16), 'ctx').reshape(3, 2, BLK, H, HD)  107 us
    unnamed x991, local copies, waits for them, and re-layouts  107 us
    psum x1, waiting for transfers between devices, per_device(): lax.psum(grad_shards[0].astype(jnp.bfloat16), 'ctx').astype(jnp.float32)  99.7 us
    dot_general x36, matrix products, product(): return jnp.dot(left_side, right_side, preferred_element_type=jnp.float32)  94.2 us
    scatter x3, local copies, waits for them, and re-layouts, serve_plan(): return jnp.zeros((ctx_count, capacity), jnp.int32).at[sources, slot_all]....  80.3 us
  transfers between devices with their start and end apart: 43, of which 18 were waited for; matrix products, arithmetic and copies ran while one was open for 32% of the time, Pallas kernels for 0%

commit v1 on v0

v1 whole, which is shorter than its diff:
```python
import functools

import jax
import jax.numpy as jnp
from jax import lax
from jax.experimental import pallas as pl
from jax.experimental.pallas import tpu as pltpu
from jax.sharding import PartitionSpec as P

D = 768
H = 12
HD = 64
FF = 3072
BLK = 64
TD = 128
BLK_DEV = 2
PAIRS = H // 2
CHUNK = 768
NCH = FF // CHUNK
STEP = 1024

MESH = pl.DeviceIdType.MESH
norm_eps = 1e-05
clip_limit = 6.0
masked_score = -1e30
exact_dot = lax.Precision.HIGHEST
f32 = jnp.float32
bf16 = jnp.bfloat16


def dot(a, b):
    return jnp.dot(a, b, preferred_element_type=f32)


def dot_t(a, b):
    return lax.dot_general(a, b, (((1,), (1,)), ((), ())), preferred_element_type=f32)


def dot_0(a, b):
    return lax.dot_general(a, b, (((0,), (0,)), ((), ())), preferred_element_type=f32)


def column_sum(v):
    return jnp.sum(v, 0, keepdims=True)


def norm_parts(v):
    center = v - jnp.mean(v, -1, keepdims=True)
    rstd = lax.rsqrt(jnp.mean(center * center, -1, keepdims=True) + norm_eps)
    return center * rstd, rstd


def norm_back(grad, hat, rstd, gain):
    scaled = grad * gain
    return rstd * (
        scaled
        - jnp.mean(scaled, -1, keepdims=True)
        - hat * jnp.mean(scaled * hat, -1, keepdims=True)
    )


def gelu(v):
    return 0.5 * v * (1.0 + lax.erf(v * (0.5**0.5)))


def gelu_both(v):
    phi = 0.5 * (1.0 + lax.erf(v * (0.5**0.5)))
    return v * phi, phi + v * jnp.exp(-0.5 * v * v) * 0.3989422804014327


def place():
    return lax.axis_index("section"), lax.axis_index("ctx"), lax.axis_index("wsh")


def greet(peers):
    barrier = pltpu.get_barrier_semaphore()
    for peer in peers:
        pl.semaphore_signal(barrier, inc=1, device_id=peer, device_id_type=MESH)
    pl.semaphore_wait(barrier, len(peers))


def push(src, dst, send, recv, peer):
    return pltpu.make_async_remote_copy(
        src_ref=src, dst_ref=dst, send_sem=send, recv_sem=recv, device_id=peer, device_id_type=MESH
    )


def halves(rows):
    low = lax.broadcasted_iota(jnp.int32, rows.shape, 1) < HD
    zero = jnp.zeros_like(rows)
    return jnp.concatenate([jnp.where(low, rows, zero), jnp.where(low, zero, rows)], 0)


def joined(rows):
    low = lax.broadcasted_iota(jnp.int32, (TD, 2 * HD), 1) < HD
    return jnp.where(low, rows[:TD], rows[TD:])


def spread4(rows, width):
    return jnp.concatenate(
        [jnp.broadcast_to(rows[r : r + 1], (BLK, width)) for r in range(4)], 0
    )


def block_lanes(blocks, width):
    lane = lax.broadcasted_iota(jnp.int32, (blocks, width), 1)
    row = lax.broadcasted_iota(jnp.int32, (blocks, width), 0)
    return jnp.where(lax.shift_right_logical(lane, 6) == row, 1.0, 0.0).astype(bf16)


def head_column(columns, head):
    lane = lax.broadcasted_iota(jnp.int32, columns.shape, 1)
    return jnp.sum(jnp.where(lane == head, columns, 0.0), 1, keepdims=True)


def pair_lanes(g):
    return pl.ds(pl.multiple_of(g * (2 * HD), 2 * HD), 2 * HD)


def forward_kernel(
    nz, W, MB, T,
    lens, tokens, attn_w, up_w, down_w, small_in, counts,
    out_o, xall_o, kv_o, q_o, att_o, mix_o, lse_o, first_o, second_o, hidden_o, top_o,
    attn_o, up_o, down_o, small_o,
    attn, up, down, small_all, small, xall, kv, q, att, mix, lse, top, first, second, hidden, out,
    wide,
    load_sem, w_send, w_recv, wf_send, wf_recv, s_send, s_recv,
    b_send, b_recv, f_send, f_recv, o_send, save_sem,
):
    s, c, w = place()
    z, core = c // 2, lax.rem(c, 2)
    part = D // W
    half = part // 2
    ffp = FF // W
    ffh = ffp // 2
    partner = {"ctx": c + 1 - 2 * core}
    xs = [{"wsh": lax.rem(w + k, W)} for k in range(1, W)]
    zs = [{"ctx": lax.rem(z + k, nz) * 2 + core} for k in range(1, nz)]
    over = [{"section": 1 - s, "ctx": lax.rem(z + k, nz) * 2 + core} for k in range(nz)]
    greet(xs + zs + over + [partner])

    def rows_of(zz, cc):
        return pl.ds(pl.multiple_of((zz * 2 + cc) * TD, TD), TD)

    mine = rows_of(z, core)

    def token_push(m, k):
        return push(
            tokens.at[m, 0], xall.at[m, mine], b_send.at[m, k], b_recv.at[m, k], zs[k - 1]
        )

    def block_arrival(m, k):
        zz = lax.rem(z + nz - k, nz)
        return push(
            xall.at[m, mine],
            xall.at[m, rows_of(zz, core)],
            b_send.at[m, k],
            b_recv.at[m, k],
            over[0],
        )

    def forward_push(m, k):
        zz = lax.rem(z + nz - k, nz)
        block = xall.at[m, rows_of(zz, core)]
        return push(block, block, f_send.at[m, k], f_recv.at[m, k], partner)

    def out_push(m, k):
        return push(out.at[m], xall.at[m, mine], o_send.at[m, k], b_recv.at[m, k], over[k])

    def own_tokens(m):
        return pltpu.make_async_copy(tokens.at[m, 0], xall.at[m, mine], b_recv.at[m, 0])

    def pieces(cc, ww):
        r = pl.ds(pl.multiple_of(ww * part + cc * half, 16), half)
        f = pl.ds(pl.multiple_of(ww * ffp + cc * ffh, 16), ffh)
        return [attn.at[0:3, r], attn.at[3:4, r], up.at[r], down.at[f]]

    sr = pl.ds(pl.multiple_of(core * half, 16), half)
    sf = pl.ds(pl.multiple_of(core * ffh, 16), ffh)
    sources = [attn_w.at[0, 0:3, sr], attn_w.at[0, 3:4, sr], up_w.at[0, sr], down_w.at[0, sf]]

    def weight_push(k, p):
        return push(
            sources[p], pieces(core, w)[p], w_send.at[k - 1, p], w_recv.at[k - 1, p], xs[k - 1]
        )

    def weight_forward(k, p):
        spot = pieces(core, lax.rem(w + W - k, W))[p]
        return push(spot, spot, wf_send.at[k - 1, p], wf_recv.at[k - 1, p], partner)

    def small_push(k):
        return push(small_in, small_all.at[k], s_send.at[k - 1], s_recv.at[k - 1], xs[k - 1])

    own_r = pl.ds(pl.multiple_of(w * part, 16), part)
    own_f = pl.ds(pl.multiple_of(w * ffp, 16), ffp)
    own_loads = [
        pltpu.make_async_copy(attn_w.at[0, 0:3], attn.at[0:3, own_r], load_sem.at[0]),
        pltpu.make_async_copy(attn_w.at[0, 3:4], attn.at[3:4, own_r], load_sem.at[1]),
        pltpu.make_async_copy(up_w.at[0], up.at[own_r], load_sem.at[2]),
        pltpu.make_async_copy(down_w.at[0], down.at[own_f], load_sem.at[3]),
    ]

    @pl.when(s == 0)
    def _():
        own_tokens(0).start()
        for k in range(1, nz):
            token_push(0, k).start()

    for p in range(4):
        own_loads[p].start()
    for k in range(1, W):
        small_push(k).start()
    for p in range(4):
        for k in range(1, W):
            weight_push(k, p).start()

    @pl.when(s == 0)
    def _():
        for m in range(1, MB):
            own_tokens(m).start()
            for k in range(1, nz):
                token_push(m, k).start()

    def weights_ready(p):
        for k in range(1, W):
            weight_push(k, p).wait_recv()
            weight_forward(k, p).start()
        own_loads[p].wait()
        for k in range(1, W):
            weight_forward(k, p).wait_recv()

    def rows_ready(m):
        @pl.when(s == 0)
        def _():
            own_tokens(m).wait()

        @pl.when(s == 1)
        def _():
            block_arrival(m, 0).wait_recv()

        forward_push(m, 0).start()
        for k in range(1, nz):
            block_arrival(m, k).wait_recv()
            forward_push(m, k).start()
        for k in range(nz):
            forward_push(m, k).wait_recv()

    saves = []

    def save(src, dst):
        copy = pltpu.make_async_copy(src, dst, save_sem.at[next(numbers)])
        copy.start()
        saves.append(copy)

    numbers = iter(range(100))
    lane = lax.broadcasted_iota(jnp.int32, (TD, 128), 1)
    row = lax.broadcasted_iota(jnp.int32, (TD, 128), 0)
    spots = lax.broadcasted_iota(jnp.int32, (1, T), 1)
    tops = jnp.full((1, 128), masked_score, f32)

    slots = kv.shape[0]

    for m in range(MB):
        rows_ready(m)
        if m == 0:
            weights_ready(0)
            for k in range(1, W):
                small_push(k).wait_recv()
            total = small_in[...]
            for k in range(1, W):
                total = total + small_all[k]
            small[...] = total
            save(small, small_o)
        save(xall.at[m], xall_o.at[m])
        bias_v = small[0:1, :]

        def project(i, _):
            r = pl.ds(pl.multiple_of(i * 256, 256), 256)
            x = xall[m, r, :]
            kv[m % slots, r, 0:D] = dot(x, attn[1]).astype(bf16)
            kv[m % slots, r, D : 2 * D] = (dot(x, attn[2]) + bias_v).astype(bf16)
            return 0

        lax.fori_loop(0, T // 256, project, 0)
        save(kv.at[m % slots], kv_o.at[m])
        kept_kv = saves[-1]
        x_own = xall[m, mine, :]
        q[m] = (dot(x_own, attn[0]).astype(bf16).astype(f32) * (HD**-0.5)).astype(bf16)
        save(q.at[m], q_o.at[m])
        length = lens[m]
        live = spots < length
        weights = dot(counts[m].astype(bf16), block_lanes(T // BLK, T))
        weights = jnp.where(live, weights, 0.0)
        wide[...] = weights.reshape(PAIRS, 8, T)

        def attend(g, kept):
            lse_c, top_c = kept
            keys = kv[m % slots, :, pair_lanes(g)]
            values = kv[m % slots, :, pl.ds(pl.multiple_of(D + g * 128, 128), 128)]
            scores = dot_t(halves(q[m, :, pair_lanes(g)]), keys)
            count = spread4(wide[g], T)
            scores = jnp.where(count > 0, scores, masked_score)
            largest = jnp.max(scores, 1, keepdims=True)
            powers = jnp.exp(scores - largest) * count
            total = jnp.sum(powers, 1, keepdims=True)
            mixed = dot(powers.astype(bf16), values) / total
            mix[m, :, pair_lanes(g)] = joined(mixed)
            log_total = largest + jnp.log(total)
            for e in range(2):
                lse_c = jnp.where(lane == 2 * g + e, log_total[e * TD : (e + 1) * TD], lse_c)
                top_c = jnp.where(lane == 2 * g + e, largest[e * TD : (e + 1) * TD], top_c)
            return lse_c, top_c

        zeros = jnp.zeros((TD, 128), f32)
        lse_c, top_c = lax.fori_loop(0, PAIRS, attend, (zeros, zeros))
        lse[m] = lse_c
        if slots < MB:
            saves[:] = [x for x in saves if x is not kept_kv]
            kept_kv.wait()
        top_c = jnp.where(c * TD + row < length, top_c, masked_score)
        tops = jnp.maximum(tops, jnp.max(top_c, 0, keepdims=True))
        att[m] = mix[m].astype(bf16)
        save(lse.at[m], lse_o.at[m])
        save(mix.at[m], mix_o.at[m])
        save(att.at[m], att_o.at[m])

    top[...] = jnp.broadcast_to(tops, (8, 128))
    save(top, top_o)
    for p in range(1, 4):
        weights_ready(p)
    save(attn, attn_o)
    save(up, up_o)
    save(down, down_o)

    for m in range(MB):
        branch = dot(att[m], attn[3]) + small[1:2, :]
        first_sum = xall[m, mine, :].astype(f32) + branch
        first[m] = first_sum
        save(first.at[m], first_o.at[m])
        hat, _ = norm_parts(first_sum)
        normed = hat * small[5:6, :] + small[3:4, :]
        low = normed.astype(bf16)
        second[m] = normed + small[2:3, :]
        for j in range(NCH):
            cols = slice(j * CHUNK, (j + 1) * CHUNK)
            pre = dot(low, up[:, cols]) + small[7 + j : 8 + j, :]
            hidden[m, :, cols] = pre
            second[m] += dot(gelu(pre).astype(bf16), down[cols, :])
        save(hidden.at[m], hidden_o.at[m])
        save(second.at[m], second_o.at[m])
        hat, _ = norm_parts(second[m])
        out[m] = (hat * small[6:7, :] + small[4:5, :]).astype(bf16)

        @pl.when(s == 0)
        def _():
            for k in range(nz):
                out_push(m, k).start()

        save(out.at[m], out_o.at[0, m, 0])

    for k in range(1, W):
        small_push(k).wait_send()
        for p in range(4):
            weight_push(k, p).wait_send()
            weight_forward(k, p).wait_send()
    for m in range(MB):
        for k in range(nz):
            forward_push(m, k).wait_send()

        @pl.when(s == 0)
        def _():
            for k in range(1, nz):
                token_push(m, k).wait_send()
            for k in range(nz):
                out_push(m, k).wait_send()

    for copy in saves:
        copy.wait()


def backward_kernel(
    nz, W, MB, T,
    lens, cot, counts_q, counts_k, xall_h, kv_h, q_h, mix_h, lse_h, first_h, second_h, hidden_h, top,
    attn_h, up_h, down_h, small,
    grad_in_o, rows_qkv, rows_branch, rows_normed, rows_hidden, rows_gated, rows_down, small_o, top_o,
    attn, up, down, xall, kv, q, mix, lse, first, second, hidden, dout,
    gfirst, gbranch, gall, aux, kvp, wide_q, wide_k, lse_all, del_all, del_c, dqkv, gnorm, ghid, gated,
    gdown, small_g, gin, top_x,
    load_sem, y_send, y_recv, b_send, b_recv, f_send, f_recv, a_send, a_recv, af_send, af_recv,
    t_send, t_recv, kvp_sem, save_sem,
):
    s, c, w = place()
    z, core = c // 2, lax.rem(c, 2)
    partner = {"ctx": c + 1 - 2 * core}
    xs = [{"wsh": lax.rem(w + k, W)} for k in range(1, W)]
    zs = [{"ctx": lax.rem(z + k, nz) * 2 + core} for k in range(1, nz)]
    across = {"section": 1 - s}
    greet(xs + zs + [across, partner])

    def rows_of(zz, cc):
        return pl.ds(pl.multiple_of((zz * 2 + cc) * TD, TD), TD)

    mine = rows_of(z, core)
    loads = []

    def load(src, dst):
        copy = pltpu.make_async_copy(src, dst, load_sem.at[len(loads)])
        copy.start()
        loads.append(copy)
        return copy

    saves = []

    def save(src, dst):
        copy = pltpu.make_async_copy(src, dst, save_sem.at[next(numbers)])
        copy.start()
        saves.append(copy)

    numbers = iter(range(100))

    def cot_load(m):
        return pltpu.make_async_copy(cot.at[m, 0], dout.at[m], y_recv.at[m])

    def grad_push(m):
        return push(gin.at[m], dout.at[m], y_send.at[m], y_recv.at[m], across)

    @pl.when(s == 1)
    def _():
        for m in range(MB):
            cot_load(m).start()

    load_second = [load(second_h.at[m], second.at[m]) for m in range(MB)]
    load_down = load(down_h, down)
    slots = xall.shape[0]
    load_hidden = [load(hidden_h.at[m], hidden.at[m]) for m in range(slots)]
    load_up = load(up_h, up)
    load_first = [load(first_h.at[m], first.at[m]) for m in range(MB)]
    load_mix = [load(mix_h.at[m], mix.at[m]) for m in range(MB)]
    load_attn = load(attn_h, attn)
    load_lse = [load(lse_h.at[m], lse.at[m]) for m in range(MB)]
    load_x = [load(xall_h.at[m], xall.at[m]) for m in range(slots)]
    load_kv = [load(kv_h.at[m, mine], kv.at[m]) for m in range(MB)]
    load_q = [load(q_h.at[m], q.at[m]) for m in range(MB)]

    def rows_push(m, k):
        block = gall.at[m, mine]
        peer = partner if k == 0 else zs[k - 1]
        send, recv = (f_send, f_recv) if k == 0 else (b_send, b_recv)
        return push(block, block, send.at[m, k], recv.at[m, k], peer)

    def rows_arrival(m, k):
        block = gall.at[m, rows_of(lax.rem(z + nz - k, nz), core)]
        return push(block, block, b_send.at[m, k], b_recv.at[m, k], partner)

    def rows_forward(m, k):
        block = gall.at[m, rows_of(lax.rem(z + nz - k, nz), core)]
        return push(block, block, f_send.at[m, k], f_recv.at[m, k], partner)

    def aux_push(m, k):
        block = aux.at[m, c]
        peer = partner if k == 0 else zs[k - 1]
        send, recv = (af_send, af_recv) if k == 0 else (a_send, a_recv)
        return push(block, block, send.at[m, k], recv.at[m, k], peer)

    def aux_arrival(m, k):
        block = aux.at[m, lax.rem(z + nz - k, nz) * 2 + core]
        return push(block, block, a_send.at[m, k], a_recv.at[m, k], partner)

    def aux_forward(m, k):
        block = aux.at[m, lax.rem(z + nz - k, nz) * 2 + core]
        return push(block, block, af_send.at[m, k], af_recv.at[m, k], partner)

    def top_push(k):
        return push(top_x.at[0], top_x.at[k], t_send.at[k - 1], t_recv.at[k - 1], xs[k - 1])

    heads = lax.broadcasted_iota(jnp.int32, (D, 128), 0)
    heads = lax.shift_right_logical(heads, 6) == lax.broadcasted_iota(jnp.int32, (D, 128), 1)
    heads = jnp.where(heads, 1.0, 0.0).astype(f32)
    small_g[...] = jnp.zeros_like(small_g)

    for m in range(MB):
        load_second[m].wait()
        if m == 0:
            load_down.wait()

        @pl.when(s == 1)
        def _():
            cot_load(m).wait()

        @pl.when(s == 0)
        def _():
            grad_push(m).wait_recv()

        grad_out = dout[m].astype(f32)
        hat, rstd = norm_parts(second[m])
        small_g[1:2, :] += column_sum(grad_out * hat)
        small_g[6:7, :] += column_sum(grad_out)
        grad_second = norm_back(grad_out, hat, rstd, small[6:7, :])
        low_second = grad_second.astype(bf16)
        gdown[m] = low_second
        save(gdown.at[m], rows_down.at[m])
        small_g[4:5, :] += column_sum(low_second.astype(f32))
        if m >= slots:
            load_hidden.append(load(hidden_h.at[m], hidden.at[m % slots]))
            for copy in hidden_saves:
                saves[:] = [x for x in saves if x is not copy]
                copy.wait()
        load_hidden[m].wait()
        if m == 0:
            load_up.wait()
        gfirst[m] = grad_second
        for j in range(NCH):
            cols = slice(j * CHUNK, (j + 1) * CHUNK)
            value, slope = gelu_both(hidden[m % slots, :, cols])
            gated[m % slots, :, cols] = value.astype(bf16)
            grad_hidden = (slope * dot_t(low_second, down[cols, :])).astype(bf16)
            ghid[m % slots, :, cols] = grad_hidden
            small_g[7 + j : 8 + j, :] += column_sum(grad_hidden.astype(f32))
            gfirst[m] += dot_t(grad_hidden, up[:, cols])
        save(gated.at[m % slots], rows_gated.at[m])
        save(ghid.at[m % slots], rows_hidden.at[m])
        hidden_saves = saves[-2:]
        grad_normed = gfirst[m]
        load_first[m].wait()
        hat, rstd = norm_parts(first[m])
        gnorm[m] = (hat * small[5:6, :] + small[3:4, :]).astype(bf16)
        save(gnorm.at[m], rows_normed.at[m])
        small_g[0:1, :] += column_sum(grad_normed * hat)
        small_g[5:6, :] += column_sum(grad_normed)
        grad_first = norm_back(grad_normed, hat, rstd, small[5:6, :])
        gfirst[m] = grad_first
        low_first = grad_first.astype(bf16)
        gbranch[m] = low_first
        save(gbranch.at[m], rows_branch.at[m])
        small_g[3:4, :] += column_sum(low_first.astype(f32))
        load_mix[m].wait()
        load_lse[m].wait()
        if m == 0:
            load_attn.wait()
        grad_att = dot_t(low_first, attn[3]).astype(bf16)
        gall[m, mine, :] = grad_att
        for k in range(nz):
            rows_push(m, k).start()
        weighed = grad_att.astype(f32) * mix[m]
        delta = jnp.dot(weighed, heads, preferred_element_type=f32, precision=exact_dot)
        del_c[m] = delta
        aux[m, c, 0:16] = lse[m].T[0:16]
        aux[m, c, 16:32] = delta.T[0:16]
        aux[m, c, 32:40] = top[...]
        for k in range(nz):
            aux_push(m, k).start()

    spots = lax.broadcasted_iota(jnp.int32, (1, T), 1)
    rows_here = lax.broadcasted_iota(jnp.int32, (TD, 128), 0)
    for m in range(MB):
        if m >= slots:
            load_x.append(load(xall_h.at[m], xall.at[m % slots]))
        load_x[m].wait()
        load_kv[m].wait()
        load_q[m].wait()

        def stream(g):
            slot = lax.rem(g, 2)
            return [
                pltpu.make_async_copy(
                    kv_h.at[m, :, pl.ds(pl.multiple_of(e * D + g * 128, 128), 128)],
                    kvp.at[slot, e],
                    kvp_sem.at[slot, e],
                )
                for e in range(2)
            ]

        for copy in stream(0):
            copy.start()
        length = lens[m]
        lanes = block_lanes(T // BLK, T)
        counted = jnp.where(spots < length, dot(counts_q[m].astype(bf16), lanes), 0.0)
        counted = jnp.where(counted > 0, jnp.log(jnp.maximum(counted, 1.0)), masked_score)
        wide_q[...] = counted.reshape(PAIRS, 8, T)

        def own_rows(g, _):
            @pl.when(g + 1 < PAIRS)
            def _():
                for copy in stream(g + 1):
                    copy.start()

            for copy in stream(g):
                copy.wait()
            slot = lax.rem(g, 2)
            lse_c = jnp.concatenate([head_column(lse[m], 2 * g + e) for e in range(2)], 0)
            delta = jnp.concatenate([head_column(del_c[m], 2 * g + e) for e in range(2)], 0)
            queries = halves(q[m, :, pair_lanes(g)])
            grads = halves(gall[m, mine, pair_lanes(g)])
            grad_q = jnp.zeros((2 * TD, 2 * HD), f32)
            for t in range(0, T, STEP):
                keys = kvp[slot, 0, t : t + STEP]
                values = kvp[slot, 1, t : t + STEP]
                shift = wide_q[g, :, t : t + STEP]
                probs = jnp.exp(dot_t(queries, keys) + spread4(shift, STEP) - lse_c)
                grad_probs = dot_t(grads, values)
                grad_scores = (probs * (grad_probs - delta)).astype(bf16)
                grad_q = grad_q + dot(grad_scores, keys)
            dqkv[m, :, pair_lanes(g)] = (joined(grad_q) * (HD**-0.5)).astype(bf16)
            return 0

        lax.fori_loop(0, PAIRS, own_rows, 0)

        def project(i, _):
            r = pl.ds(pl.multiple_of(i * 256, 256), 256)
            rows = dot(xall[m % slots, r, :], attn[0]).astype(bf16).astype(f32)
            xall[m % slots, r, :] = (rows * (HD**-0.5)).astype(bf16)
            return 0

        lax.fori_loop(0, T // 256, project, 0)
        for k in range(1, nz):
            rows_arrival(m, k).wait_recv()
            rows_forward(m, k).start()
            aux_arrival(m, k).wait_recv()
            aux_forward(m, k).start()
        for k in range(nz):
            rows_forward(m, k).wait_recv()
            aux_forward(m, k).wait_recv()
        for cc in range(2 * nz):
            lse_all[:, cc * TD : (cc + 1) * TD] = aux[m, cc, 0:16]
            del_all[:, cc * TD : (cc + 1) * TD] = aux[m, cc, 16:32]
        if m == 0:
            most = aux[0, 0, 32:40]
            for cc in range(1, 2 * nz):
                most = jnp.maximum(most, aux[0, cc, 32:40])
            top_x[0] = most
            for k in range(1, W):
                top_push(k).start()
        counted = dot(counts_k[m].astype(bf16), lanes)
        counted = jnp.where(counted > 0, jnp.log(jnp.maximum(counted, 1.0)), masked_score)
        wide_k[...] = counted.reshape(PAIRS, 8, T)
        live = c * TD + rows_here < length

        def own_keys(g, _):
            keys = halves(kv[m, :, pair_lanes(g)])
            values = halves(kv[m, :, pl.ds(pl.multiple_of(D + g * 128, 128), 128)])
            lse_r = [lse_all[pl.ds(2 * g + e, 1), :] for e in range(2)]
            delta = [del_all[pl.ds(2 * g + e, 1), :] for e in range(2)]
            shift = wide_k[g]
            shift = jnp.concatenate([shift[0:2] - lse_r[0], shift[2:4] - lse_r[1]], 0)
            grad_k = jnp.zeros((2 * TD, 2 * HD), f32)
            grad_v = jnp.zeros((2 * TD, 2 * HD), f32)
            for t in range(0, T, STEP):
                queries = xall[m % slots, t : t + STEP, pair_lanes(g)]
                grads = gall[m, t : t + STEP, pair_lanes(g)]
                probs = jnp.exp(dot_t(keys, queries) + spread4(shift[:, t : t + STEP], STEP))
                grad_v = grad_v + dot(probs.astype(bf16), grads)
                centre = jnp.concatenate(
                    [jnp.broadcast_to(d[:, t : t + STEP], (TD, STEP)) for d in delta], 0
                )
                grad_scores = (probs * (dot_t(values, grads) - centre)).astype(bf16)
                grad_k = grad_k + dot(grad_scores, queries)
            grad_k, grad_v = joined(grad_k), joined(grad_v)
            lanes_k = pl.ds(pl.multiple_of(D + g * 128, 128), 128)
            lanes_v = pl.ds(pl.multiple_of(2 * D + g * 128, 128), 128)
            dqkv[m, :, lanes_k] = jnp.where(live, grad_k, 0.0).astype(bf16)
            dqkv[m, :, lanes_v] = jnp.where(live, grad_v, 0.0).astype(bf16)
            return 0

        lax.fori_loop(0, PAIRS, own_keys, 0)
        save(dqkv.at[m], rows_qkv.at[m])
        small_g[2:3, :] += column_sum(dqkv[m, :, 2 * D :].astype(f32))
        total = gfirst[m]
        for p in range(3):
            total = total + dot_t(dqkv[m, :, p * D : (p + 1) * D], attn[p])
        gin[m] = total.astype(bf16)

        @pl.when(s == 1)
        def _():
            grad_push(m).start()

        save(gin.at[m], grad_in_o.at[0, m, 0])

    save(small_g, small_o)
    for k in range(1, W):
        top_push(k).wait()
    most = top_x[0]
    for k in range(1, W):
        most = jnp.maximum(most, top_x[k])
    top_o[...] = most
    for m in range(MB):
        for k in range(nz):
            rows_forward(m, k).wait_send()
            aux_forward(m, k).wait_send()
        for k in range(1, nz):
            rows_push(m, k).wait_send()
            aux_push(m, k).wait_send()

        @pl.when(s == 1)
        def _():
            grad_push(m).wait_send()

    for copy in saves:
        copy.wait()


def counts_of(seq_lengths, rand_owner, rand_local, global_raw, c, n_ctx):
    blocks = BLK_DEV * n_ctx
    length = seq_lengths[:, 0]
    valid = (length + BLK - 1) // BLK
    chosen = global_raw[:, 0] % valid[:, None]
    random = rand_owner[:, 0] * BLK_DEV + rand_local[:, 0]
    ids = jnp.arange(blocks)
    near = (jnp.abs(ids[:, None] - ids[None, :]) <= 1).astype(jnp.int32)
    named = jnp.sum((random[..., None] == ids).astype(jnp.int32), 3)
    is_global = chosen[..., None] == ids
    glob = jnp.sum(is_global.astype(jnp.int32), 1)
    wide_row = jnp.any(is_global, 1)
    table = named + near[None, :, None, :] + glob[:, None, None, :]
    table = jnp.where(wide_row[:, :, None, None], 1, table).astype(f32)
    mb = table.shape[0]
    by_q = lax.dynamic_slice_in_dim(table, c * BLK_DEV, BLK_DEV, 1)
    by_k = lax.dynamic_slice_in_dim(table, c * BLK_DEV, BLK_DEV, 3)
    by_q = by_q.transpose(0, 2, 1, 3).reshape(mb, PAIRS, 4, blocks)
    by_k = by_k.transpose(0, 2, 3, 1).reshape(mb, PAIRS, 4, blocks)
    both = jnp.pad(jnp.stack([by_q, by_k]), ((0, 0), (0, 0), (0, 0), (0, 4), (0, 0)))
    both = both.reshape(2, mb, PAIRS * 8, blocks)
    return both[0], both[1]


VMEM = pl.BlockSpec(memory_space=pltpu.VMEM)
SMEM = pl.BlockSpec(memory_space=pltpu.SMEM)
ANY = pl.BlockSpec(memory_space=pl.ANY)
DMA = pltpu.SemaphoreType.DMA


def slots_of(T, MB):
    return MB if T <= 2048 else 1


def run_forward(nz, W, MB, lens, tokens, attn_w, up_w, down_w, small_in, counts):
    T = 2 * nz * TD
    shape = jax.ShapeDtypeStruct
    outs = [
        shape((1, MB, 1, TD, D), bf16),
        shape((MB, T, D), bf16),
        shape((MB, T, 2 * D), bf16),
        shape((MB, TD, D), bf16),
        shape((MB, TD, D), bf16),
        shape((MB, TD, D), f32),
        shape((MB, TD, 128), f32),
        shape((MB, TD, D), f32),
        shape((MB, TD, D), f32),
        shape((MB, TD, FF), f32),
        shape((8, 128), f32),
        shape((4, D, D), bf16),
        shape((D, FF), bf16),
        shape((FF, D), bf16),
        shape((16, D), f32),
    ]
    scratch = [
        pltpu.VMEM((4, D, D), bf16),
        pltpu.VMEM((D, FF), bf16),
        pltpu.VMEM((FF, D), bf16),
        pltpu.VMEM((W, 16, D), f32),
        pltpu.VMEM((16, D), f32),
        pltpu.VMEM((MB, T, D), bf16),
        pltpu.VMEM((slots_of(T, MB), T, 2 * D), bf16),
        pltpu.VMEM((MB, TD, D), bf16),
        pltpu.VMEM((MB, TD, D), bf16),
        pltpu.VMEM((MB, TD, D), f32),
        pltpu.VMEM((MB, TD, 128), f32),
        pltpu.VMEM((8, 128), f32),
        pltpu.VMEM((MB, TD, D), f32),
        pltpu.VMEM((MB, TD, D), f32),
        pltpu.VMEM((MB, TD, FF), f32),
        pltpu.VMEM((MB, TD, D), bf16),
        pltpu.VMEM((PAIRS, 8, T), f32),
        DMA((4,)),
        DMA((W - 1, 4)),
        DMA((W - 1, 4)),
        DMA((W - 1, 4)),
        DMA((W - 1, 4)),
        DMA((W - 1,)),
        DMA((W - 1,)),
        DMA((MB, nz)),
        DMA((MB, nz)),
        DMA((MB, nz)),
        DMA((MB, nz)),
        DMA((MB, nz)),
        DMA((5 + 10 * MB,)),
    ]
    return pl.pallas_call(
        functools.partial(forward_kernel, nz, W, MB, T),
        out_shape=outs,
        in_specs=[SMEM, ANY, ANY, ANY, ANY, VMEM, VMEM],
        out_specs=[ANY] * len(outs),
        scratch_shapes=scratch,
        compiler_params=pltpu.CompilerParams(
            collective_id=0, has_side_effects=True, vmem_limit_bytes=60 << 20
        ),
        name="forward",
    )(lens, tokens, attn_w, up_w, down_w, small_in, counts)


def run_backward(nz, W, MB, lens, cot, counts_q, counts_k, saved):
    T = 2 * nz * TD
    slots = slots_of(T, MB)
    shape = jax.ShapeDtypeStruct
    (xall, kv, q, mix, lse, first, second, hidden, top, attn, up, down, small) = saved
    outs = [
        shape((1, MB, 1, TD, D), bf16),
        shape((MB, TD, 3 * D), bf16),
        shape((MB, TD, D), bf16),
        shape((MB, TD, D), bf16),
        shape((MB, TD, FF), bf16),
        shape((MB, TD, FF), bf16),
        shape((MB, TD, D), bf16),
        shape((16, D), f32),
        shape((8, 128), f32),
    ]
    scratch = [
        pltpu.VMEM((4, D, D), bf16),
        pltpu.VMEM((D, FF), bf16),
        pltpu.VMEM((FF, D), bf16),
        pltpu.VMEM((slots, T, D), bf16),
        pltpu.VMEM((MB, TD, 2 * D), bf16),
        pltpu.VMEM((MB, TD, D), bf16),
        pltpu.VMEM((MB, TD, D), f32),
        pltpu.VMEM((MB, TD, 128), f32),
        pltpu.VMEM((MB, TD, D), f32),
        pltpu.VMEM((MB, TD, D), f32),
        pltpu.VMEM((slots, TD, FF), f32),
        pltpu.VMEM((MB, TD, D), bf16),
        pltpu.VMEM((MB, TD, D), f32),
        pltpu.VMEM((MB, TD, D), bf16),
        pltpu.VMEM((MB, T, D), bf16),
        pltpu.VMEM((MB, 2 * nz, 40, 128), f32),
        pltpu.VMEM((2, 2, T, 2 * HD), bf16),
        pltpu.VMEM((PAIRS, 8, T), f32),
        pltpu.VMEM((PAIRS, 8, T), f32),
        pltpu.VMEM((16, T), f32),
        pltpu.VMEM((16, T), f32),
        pltpu.VMEM((MB, TD, 128), f32),
        pltpu.VMEM((MB, TD, 3 * D), bf16),
        pltpu.VMEM((MB, TD, D), bf16),
        pltpu.VMEM((slots, TD, FF), bf16),
        pltpu.VMEM((slots, TD, FF), bf16),
        pltpu.VMEM((MB, TD, D), bf16),
        pltpu.VMEM((16, D), f32),
        pltpu.VMEM((MB, TD, D), bf16),
        pltpu.VMEM((W, 8, 128), f32),
        DMA((3 + 8 * MB,)),
        DMA((MB,)),
        DMA((MB,)),
        DMA((MB, nz)),
        DMA((MB, nz)),
        DMA((MB, nz)),
        DMA((MB, nz)),
        DMA((MB, nz)),
        DMA((MB, nz)),
        DMA((MB, nz)),
        DMA((MB, nz)),
        DMA((W - 1,)),
        DMA((W - 1,)),
        DMA((2, 2)),
        DMA((1 + 7 * MB,)),
    ]
    return pl.pallas_call(
        functools.partial(backward_kernel, nz, W, MB, T),
        out_shape=outs,
        in_specs=[SMEM, ANY, VMEM, VMEM] + [ANY] * 8 + [VMEM] + [ANY] * 3 + [VMEM],
        out_specs=[ANY] * 8 + [VMEM],
        scratch_shapes=scratch,
        compiler_params=pltpu.CompilerParams(
            collective_id=1, has_side_effects=True, vmem_limit_bytes=60 << 20
        ),
        name="backward",
    )(
        lens, cot, counts_q, counts_k, xall, kv, q, mix, lse, first, second, hidden, top,
        attn, up, down, small,
    )


def contract_rows(left_side, right_side):
    return lax.dot_general(
        left_side, right_side, (((0,), (0,)), ((), ())), preferred_element_type=f32
    )


def per_device(
    tokens, out_cotangent, attn_weights, up_weights, down_weights, norm_gains, bias_rows, up_bias,
    seq_lengths, rand_owner, rand_local, global_raw,
):
    n_ctx, W = lax.axis_size("ctx"), lax.axis_size("wsh")
    nz = n_ctx // 2
    c, w = lax.axis_index("ctx"), lax.axis_index("wsh")
    MB = tokens.shape[0]
    part, ffp = D // W, FF // W
    rows = jnp.concatenate([bias_rows[0], norm_gains[0]], 0).astype(f32)
    rows = lax.dynamic_update_slice(jnp.zeros((7, D), f32), rows, (0, w * part))
    wide = lax.dynamic_update_slice(jnp.zeros((FF,), f32), up_bias[0].astype(f32), (w * ffp,))
    small_in = jnp.concatenate([rows, wide.reshape(NCH, CHUNK), jnp.zeros((5, D), f32)], 0)
    counts_q, counts_k = counts_of(seq_lengths, rand_owner, rand_local, global_raw, c, n_ctx)
    lens = seq_lengths[:, 0]
    (
        out, xall, kv, q, att, mix, lse, first, second, hidden, top, attn, up, down, small,
    ) = run_forward(nz, W, MB, lens, tokens, attn_weights, up_weights, down_weights, small_in, counts_q)
    (
        grad_in, rows_qkv, rows_branch, rows_normed, rows_hidden, rows_gated, rows_down, small_g, tops,
    ) = run_backward(
        nz, W, MB, lens, out_cotangent, counts_q, counts_k,
        (xall, kv, q, mix, lse, first, second, hidden, top, attn, up, down, small),
    )
    head_tops = tops[0, :H]
    factor = jnp.sqrt(clip_limit / jnp.maximum(head_tops, clip_limit))
    clipped = (
        attn_weights[0, :2].astype(f32).reshape(2, -1, H, HD) * factor[None, None, :, None]
    )
    clipped_qk = clipped.reshape(1, 2, -1, D).astype(bf16)

    def flat(v):
        return v.reshape(-1, v.shape[-1])

    x_own = flat(lax.dynamic_slice_in_dim(xall, c * TD, TD, 1))
    qkv = flat(rows_qkv)
    grads = (
        jnp.stack(
            [contract_rows(x_own, qkv[:, p * D : (p + 1) * D]) for p in range(3)]
            + [contract_rows(flat(att), flat(rows_branch))]
        ),
        contract_rows(flat(rows_normed), flat(rows_hidden)),
        contract_rows(flat(rows_gated), flat(rows_down)),
    )
    dims = (1, 0, 0)
    shards = tuple(
        lax.psum_scatter(g.astype(bf16), "wsh", scatter_dimension=d, tiled=True)
        for g, d in zip(grads, dims)
    )
    total = tuple(lax.psum(g, "ctx").astype(f32) for g in shards)
    small_g = lax.psum(small_g, ("ctx", "wsh"))
    gains = lax.dynamic_slice(small_g[0:2], (0, w * part), (2, part))
    biases = lax.dynamic_slice(small_g[2:7], (0, w * part), (5, part))
    up_grad = lax.dynamic_slice(small_g[7:11].reshape(-1), (w * ffp,), (ffp,))
    return (
        out, grad_in, total[0][None], total[1][None], total[2][None], gains[None], biases[None],
        up_grad[None], clipped_qk,
    )


def solution(mesh):
    placed = (
        P(None, "wsh", "ctx", None),
        P(None, "wsh", "ctx", None),
        P("section", None, "wsh", None),
        P("section", "wsh", None),
        P("section", "wsh", None),
        P("section", None, "wsh"),
        P("section", None, "wsh"),
        P("section", "wsh"),
        P(None, "wsh"),
        P(None, "wsh", None, None, None),
        P(None, "wsh", None, None, None),
        P(None, "wsh", None),
    )
    return jax.shard_map(
        per_device,
        mesh=mesh,
        in_specs=placed,
        out_specs=(
            P("section", None, "wsh", "ctx", None),
            P("section", None, "wsh", "ctx", None),
            P("section", None, "wsh", None),
            P("section", "wsh", None),
            P("section", "wsh", None),
            P("section", None, "wsh"),
            P("section", None, "wsh"),
            P("section", "wsh"),
            P("section", None, "wsh", None),
        ),
        check_vma=False,
    )
```

time: 2210 us -> 645 us (0.29)
  local copies, waits for them, and re-layouts: 601 us -> 8.31 us
  waiting for transfers between devices: 656 us -> 266 us
  other arithmetic: 359 us -> 19.2 us
  Pallas kernels: 0 us -> 265 us
  matrix products: 224 us -> 10.8 us
  blocking collectives: 210 us -> 58.3 us
  starting transfers between devices: 114 us -> 0.16 us
    psum x13 -> x1, waiting for transfers between devices: 529 us -> 91.1 us  [per_device(): total = tuple((lax.psum(g, 'ctx').astype(f32) for g in shards))]
    pallas_call x0 -> x2, Pallas kernels: none -> 265 us  [the longest x1 150 us: run_backward(): pl.pallas_call(functools.partial(backward_kernel, nz, W, MB, T), out_shap...]
    dot_general x123 -> x0, matrix products: 200 us -> none  [the longest x36 94.2 us: product(): return jnp.dot(left_side, right_side, preferred_element_type=jnp.float32)]
    all_gather x9 -> x0, blocking collectives: 147 us -> none  [the longest x6 137 us: merged(): everything = jax.tree.map(lambda part: lax.all_gather(part, axis), value)]
    scatter x6 -> x0, local copies, waits for them, and re-layouts: 117 us -> none  [the longest x3 80.3 us: serve_plan(): return jnp.zeros((ctx_count, capacity), jnp.int32).at[sources, slot_all]....]
    reduce_scatter x3, waiting for transfers between devices: 70.3 us -> 175 us  [per_device(): lax.psum_scatter(g.astype(bf16), 'wsh', scatter_dimension=d, tiled=True)]
    unnamed x991 -> x24, local copies, waits for them, and re-layouts: 107 us -> 3.69 us
    all_to_all x6 -> x0, starting transfers between devices: 84.3 us -> none  [the longest x3 60 us: fetch_keys(): lax.all_to_all(tile_table(paired)[route_ids], 'ctx', split_axis=0, concat...]
  transfers between devices with their start and end apart: 43 -> 4, of which waited for: 18 -> 4; matrix products, arithmetic and copies ran while one was open for 32% -> 2% of each run, Pallas kernels for 0% -> 0%
where the time goes in v1:
time: 645 us; the launch traced here: 642 us
  waiting for transfers between devices  266 us (41%)
  Pallas kernels  265 us (41%)
  blocking collectives  58.3 us (9%)
  other arithmetic  19.2 us (3%)
  between operations  14 us (2%)
  matrix products  10.8 us (2%)
  local copies, waits for them, and re-layouts  8.31 us (1%)
    reduce_scatter x3, waiting for transfers between devices, per_device(): lax.psum_scatter(g.astype(bf16), 'wsh', scatter_dimension=d, tiled=True)  175 us
    pallas_call x1, Pallas kernels, run_backward(): pl.pallas_call(functools.partial(backward_kernel, nz, W, MB, T), out_shap...  150 us
    pallas_call x1, Pallas kernels, run_forward(): pl.pallas_call(functools.partial(forward_kernel, nz, W, MB, T), out_shape...  115 us
    psum x1, waiting for transfers between devices, per_device(): total = tuple((lax.psum(g, 'ctx').astype(f32) for g in shards))  91.1 us
    psum x1, blocking collectives, per_device(): small_g = lax.psum(small_g, ('ctx', 'wsh'))  58.3 us
  transfers between devices with their start and end apart: 4, of which 4 were waited for; matrix products, arithmetic and copies ran while one was open for 2% of the time, Pallas kernels for 0%

profile of v1, /device:TPU:25, one launch (start us, length us, event | category | flops | bytes accessed | tf_op | source)
XLA Modules:
  0.0 642.2 jit_solution(9194996875686176928)
XLA Ops:
  7.2 0.0 reduce-scatter.8.cloned.1.call-start
  7.2 0.7 compare_bitcast_fusion
  7.9 0.9 and_select_fusion
  8.8 0.1 convert_reduce_fusion.2
  8.9 0.1 fusion.8
  9.0 0.8 multiply_add_fusion
  9.9 0.2 convert_reduce_fusion
  10.1 0.1 select_convert_fusion
  10.2 0.1 dynamic-slice_bitcast_fusion
  10.3 0.2 copy.39
  10.6 0.6 slice_bitcast_fusion
  11.2 0.7 convert_reduce_fusion.1
  11.9 0.3 dynamic_update_slice.7
  12.3 0.1 pad.13.clone
  12.3 0.7 convert_dynamic-update-slice_fusion
  13.1 0.7 maximum_maximum_fusion.small_in
  13.8 115.5 %forward.1 = (bf16[1,2,1,128,768]{4,3,2,1,0:T(8,128)(2,1)}, bf16[2,1024,768]{2,1,0:T(8,128)(2,1)}, bf16[2,1024,1536]{2,1,0:T(8,128)(2,1)}, bf16[2,128,768]{2,1,0...) custom-call(s32[2]{0:T(128)} %bitcast.67, ...), custom_call_target="tpu_custom_call" | custom-call | tf_op jit(solution)/shard_map/forward/pallas_call | solution.py:787
  129.3 149.9 %backward.1 = (bf16[1,2,1,128,768]{4,3,2,1,0:T(8,128)(2,1)}, bf16[2,128,2304]{2,1,0:T(8,128)(2,1)}, bf16[2,128,768]{2,1,0:T(8,128)(2,1)}, bf16[2,128,768]{2,1,0:...) custom-call(s32[2]{0:T(128)} %bitcast.68, ...), custom_call_target="tpu_custom_call" | custom-call | tf_op jit(solution)/shard_map/backward/pallas_call | solution.py:863
  279.2 5.1 bitcast_convert_fusion
  284.3 0.0 copy-start.3
  284.3 0.0 reduce-scatter.8.cloned.1.call-update
  284.3 0.0 reduce-scatter.6.cloned.1.call-start
  284.4 1.3 copy-done.3
  285.7 0.1 copy-done.5
  285.8 3.6 bitcast_convert_fusion.1
  289.4 0.0 reduce-scatter.6.cloned.1.call-update
  289.4 0.0 copy-start.4
  289.4 0.0 reduce-scatter.4.cloned.1.call-start
  289.5 1.2 constant_dynamic-slice_fusion.1
  290.6 0.0 copy-done.8
  290.6 0.0 copy-done.9
  290.6 0.5 fusion.3
  291.2 0.0 copy-done.4
  291.2 0.5 fusion
  291.7 0.5 fusion.1
  292.2 0.5 fusion.2
  292.7 2.5 pad_maximum_fusion
  295.2 0.0 reduce-scatter.4.cloned.1.call-update
  295.3 0.0 all-reduce.4.cloned.1.call-start
  295.3 49.1 %reduce-scatter.8.cloned.1.call-done = bf16[1536,768]{1,0:T(8,128)(2,1)} async-done(((bf16[3072,768]{1,0:T(8,128)(2,1)}), bf16[1536,768]{1,0:T(8,128)(2,1)}) %reduce-scatter.8.cloned.1.call-update) | async-done | bytes 2359312 | tf_op jit(solution)/shard_map/reduce_scatter | solution.py:931
  344.4 63.0 %reduce-scatter.6.cloned.1.call-done = bf16[384,3072]{1,0:T(8,128)(2,1)} async-done(((bf16[768,3072]{1,0:T(8,128)(2,1)}), bf16[384,3072]{1,0:T(8,128)(2,1)}) %reduce-scatter.6.cloned.1.call-update) | async-done | bytes 2359312 | tf_op jit(solution)/shard_map/reduce_scatter | solution.py:931
  407.4 62.9 %reduce-scatter.4.cloned.1.call-done = bf16[4,384,768]{2,1,0:T(8,128)(2,1)} async-done(((bf16[4,768,768]{2,1,0:T(8,128)(2,1)}), bf16[4,384,768]{2,1,0:T(8,128)(2,1)}) %reduce-scatter.4.cloned.1.call-update) | async-done | bytes 2359312 | tf_op jit(solution)/shard_map/reduce_scatter | solution.py:931
  470.3 0.0 all-reduce.4.cloned.1.call-update
  470.3 0.8 copy-done.10
  471.1 58.3 %psum.31 = f32[16,768]{1,0:T(8,128)S(1)} all-reduce(f32[16,768]{1,0:T(8,128)S(1)} %copy-done.10), channel_id=1, replica_groups=mesh['section'=2,'ctx'=8,'wsh'=2] {'ctx','wsh'}, use_global_device_ids=true, to_apply=%region_9.10 | all-reduce | flops 12288 | bytes 98304 | tf_op jit(solution)/shard_map/psum | solution.py:935
  529.4 0.7 sqrt_bitcast_fusion
  530.1 0.1 mul.47
  530.2 0.1 mul.48
  530.2 0.6 broadcast_in_dim.71
  530.9 0.1 dynamic_slice.23
  530.9 0.6 broadcast_in_dim.72
  531.5 0.6 dynamic-slice_bitcast_fusion.1
  532.1 0.0 copy-done
  532.1 1.2 multiply_convert_fusion
  533.3 91.1 %all-reduce.4.cloned.1.call-done = (bf16[1,4,384,768]{3,2,1,0:T(8,128)(2,1)}, bf16[1,384,3072]{2,1,0:T(8,128)(2,1)}, bf16[1,1536,768]{2,1,0:T(8,128)(2,1)}) async-done(((bf16[1,4,384,768]{3,2,1,0:T(8,128)(2,1)}, bf16[1,384,3072]{2,1,0:T(8,128)(2,1)}, bf16[1,1536,768]{2,1,0:T(8,128)(2,1)}), (bf16[1,4,384,768]{3,2,1,0:T(8,128)(2,1)}, bf16[1,384,3072]{2,1,0:T(8,128)(2,1)}, ...) | async-done | bytes 7077904 | tf_op jit(solution)/shard_map/psum | solution.py:934
  624.4 4.4 broadcast_in_dim.65
  628.9 0.0 copy-done.2
  628.9 2.8 broadcast_in_dim.67
  631.6 0.0 copy-done.1
  631.6 2.5 broadcast_in_dim.69
  634.2 0.0 copy-done.6
  634.2 0.7 copy.55
  634.9 0.0 copy-done.7
  634.9 0.7 copy.56
  (23 shorter events, 0.2 us)
Async XLA Ops:
  7.2 337.2 %reduce-scatter.8.cloned.1.call-start = ((), (), s32[]{:S(2)}) async-start(), calls=%async_computation.5 | async-start | bytes 7077888 | tf_op jit(solution)/shard_map/reduce_scatter | solution.py:931
  284.3 1.4 copy-start.3
  284.3 1.5 copy-start.5
  284.3 123.1 %reduce-scatter.6.cloned.1.call-start = ((), (), s32[]{:S(2)}) async-start(), calls=%async_computation.4 | async-start | bytes 7077888 | tf_op jit(solution)/shard_map/reduce_scatter | solution.py:931
  289.4 1.3 copy-start.8
  289.4 1.3 copy-start.9
  289.4 1.8 copy-start.4
  289.4 180.9 %reduce-scatter.4.cloned.1.call-start = ((), (), s32[]{:S(2)}) async-start(), calls=%async_computation.3 | async-start | bytes 7077888 | tf_op jit(solution)/shard_map/reduce_scatter | solution.py:931
  295.3 329.2 %all-reduce.4.cloned.1.call-start = ((), (), s32[]{:S(2)}) async-start(), calls=%async_computation.6 | async-start | bytes 14155776 | tf_op jit(solution)/shard_map/psum | solution.py:934
  470.3 0.8 copy-start.10
  470.3 61.8 %copy-start = (bf16[1,4,384,768]{3,2,1,0:T(8,128)(2,1)S(1)}, bf16[1,4,384,768]{3,2,1,0:T(8,128)(2,1)}, u32[]{:S(2)}) copy-start(bf16[1,4,384,768]{3,2,1,0:T(8,128)(2,1)} %attn_w.1) | copy-start | bytes 7077892
  624.4 4.4 copy-start.2
  628.9 2.8 copy-start.1
  631.6 2.6 copy-start.6
  631.6 3.3 copy-start.7
Sparse Core Ops, SparseCore 0:
  284.4 59.8 reduce-scatter.7
  347.3 59.9 reduce-scatter.5
  410.2 59.9 reduce-scatter.3
  472.9 151.4 all-reduce.3

commit v2 on v1

--- a/solution.py
+++ b/solution.py
@@ -18,6 +18,9 @@
 CHUNK = 768
 NCH = FF // CHUNK
 STEP = 1024
+ROWS = 48
+FLIGHT = 4
+LAG = 4
 
 MESH = pl.DeviceIdType.MESH
 norm_eps = 1e-05
@@ -696,6 +699,327 @@
 
     for copy in saves:
         copy.wait()
+
+
+def reduce_kernel(
+    nz, W, MB,
+    gated_h, down_h, normed_h, hidden_h, x_h, qkv_h, att_h, branch_h, small_g, tops, attn_w,
+    attn_o, up_o, down_o, small_o, clip_o,
+    lg, rd, ln, rh, la, ra, lb, rb, grads, from_x, chain, totals, theirs, own_w, core_s, wsh_s, z_s,
+    load_sem, c_send, c_recv, x_send, x_recv, ch_send, ch_recv, b_send, b_recv, p_send, p_recv,
+    o_sem, s_send, s_recv, sx_send, sx_recv, sz_send, sz_recv,
+):
+    s, c, w = place()
+    z, core = c // 2, lax.rem(c, 2)
+    part, ffp = D // W, FF // W
+    R = MB * TD
+    per = part // ROWS
+    count = 6 * per
+    root = (nz - 1) // 2
+    partner = {"ctx": c + 1 - 2 * core}
+    xs = [{"wsh": lax.rem(w + k, W)} for k in range(1, W)]
+    zs = [{"ctx": lax.rem(z + k, nz) * 2 + core} for k in range(1, nz)]
+    greet(xs + zs + [partner])
+
+    def operands(cc):
+        gate = [
+            (
+                gated_h.at[:, pl.ds(pl.multiple_of(e * ffp + cc * (ffp // 2), 128), ffp // 2)],
+                lg,
+                e * (ffp // 2),
+                ffp // 2,
+            )
+            for e in range(W)
+        ]
+        hid = hidden_h.at[:, pl.ds(pl.multiple_of(cc * (FF // 2), 128), FF // 2)]
+        return gate + [(down_h, rd, 0, D), (normed_h, ln, 0, D), (hid, rh, 0, FF // 2)]
+
+    def rows_of_x(buffer):
+        mine = pl.ds(pl.multiple_of(c * TD, TD), TD)
+        return [(x_h.at[m, mine], buffer, m) for m in range(MB)]
+
+    def heads_operands(cc):
+        if cc == 0:
+            return [(qkv_h.at[:, 0:D], ra), (qkv_h.at[:, D : 2 * D], rb)]
+        return [(qkv_h.at[:, 2 * D : 3 * D], ra), (att_h, lb), (branch_h, rb)]
+
+    first = operands(core)
+    second = operands(1 - core)
+    n1 = len(first)
+    base = [0, R]
+
+    def local(n, src, dst):
+        return pltpu.make_async_copy(src, dst, load_sem.at[n])
+
+    def to_core(n, src, dst):
+        return push(src, dst, c_send.at[n], c_recv.at[n], partner)
+
+    def window(dst, at, width, side):
+        return dst.at[side * R : side * R + R, at : at + width]
+
+    fast = [local(n, a, window(b, at, wd, 0)) for n, (a, b, at, wd) in enumerate(first)]
+    fast_x = [to_core(n, a, window(b, at, wd, 1)) for n, (a, b, at, wd) in enumerate(second)]
+    for one, two in zip(fast, fast_x):
+        two.start()
+        one.start()
+
+    def attn_copies(cc, make, side):
+        found = []
+        for n, (a, b) in enumerate(heads_operands(cc)):
+            found.append(make(n1 + n, a, b.at[side * R : side * R + R]))
+        n = n1 + 3
+        for buffer in (la, lb) if cc == 0 else (la,):
+            for a, b, m in rows_of_x(buffer):
+                lo = side * R + m * TD
+                found.append(make(n, a, b.at[lo : lo + TD]))
+                n += 1
+        return found
+
+    for cc in range(2):
+
+        @pl.when(core == cc)
+        def _():
+            for copy in attn_copies(1 - cc, to_core, 1) + attn_copies(cc, local, 0):
+                copy.start()
+
+    small_push = push(small_g, core_s.at[core], s_send, s_recv, partner)
+    small_push.start()
+    core_s[core] = small_g[...]
+    weights_in = local(n1 + 3 + 2 * MB, attn_w.at[0, 0:2], own_w)
+    weights_in.start()
+
+    def spot(i, ww):
+        at = (i // per) * D + ww * part + lax.rem(i, per) * ROWS
+        return pl.ds(pl.multiple_of(at, 16), ROWS)
+
+    def lines(i):
+        return pl.ds(pl.multiple_of(i * ROWS, 16), ROWS)
+
+    def x_push(i, k):
+        return push(
+            grads.at[spot(i, lax.rem(w + k, W))],
+            from_x.at[k - 1, lines(i)],
+            x_send.at[k - 1, i],
+            x_recv.at[k - 1, i],
+            xs[k - 1],
+        )
+
+    for n in range(W + 1):
+        fast[n].wait()
+        fast_x[n].wait_recv()
+    gate_half = ffp // 2
+    for e in range(W):
+        block = dot_0(lg[:, e * gate_half : (e + 1) * gate_half], rd[...]).astype(bf16)
+        for j in range(2):
+            grads[j * D + e * part : j * D + (e + 1) * part] = block[j * part : (j + 1) * part]
+    for i in range(FLIGHT):
+        for k in range(1, W):
+            x_push(i, k).start()
+    for n in range(W + 1, n1):
+        fast[n].wait()
+        fast_x[n].wait_recv()
+    for j in range(2):
+        block = dot_0(ln[...], rh[:, j * D : (j + 1) * D])
+        grads[(2 + j) * D : (3 + j) * D] = block.astype(bf16)
+    for cc in range(2):
+
+        @pl.when(core == cc)
+        def _():
+            for copy in attn_copies(cc, local, 0):
+                copy.wait()
+            for copy in attn_copies(cc, to_core, 1):
+                copy.wait_recv()
+
+    for j, (left, right) in enumerate(((la, ra), (lb, rb))):
+        grads[(4 + j) * D : (5 + j) * D] = dot_0(left[...], right[...]).astype(bf16)
+
+    small_push.wait_recv()
+    pair = core_s[0] + core_s[1]
+    wsh_s[w] = pair
+    small_x = [push(wsh_s.at[w], wsh_s.at[w], sx_send.at[k - 1], sx_recv.at[k - 1], xs[k - 1]) for k in range(1, W)]
+    for copy in small_x:
+        copy.start()
+    weights_in.wait()
+    factor = jnp.sqrt(clip_limit / jnp.maximum(tops[...], clip_limit))
+    lane = lax.broadcasted_iota(jnp.int32, (128, D), 1)
+    head = lax.broadcasted_iota(jnp.int32, (128, D), 0)
+    heads = jnp.where(lax.shift_right_logical(lane, 6) == head, 1.0, 0.0).astype(f32)
+    wide = jnp.dot(factor, heads, preferred_element_type=f32, precision=exact_dot)[0:1]
+    for p in range(2):
+        clip_o[0, p] = (own_w[p].astype(f32) * wide).astype(bf16)
+    for k in range(1, W):
+        e = lax.rem(w + W - k, W)
+        push(wsh_s.at[w], wsh_s.at[e], sx_send.at[k - 1], sx_recv.at[k - 1], xs[k - 1]).wait_recv()
+    total = wsh_s[0]
+    for e in range(1, W):
+        total = total + wsh_s[e]
+    z_s[z] = total
+    small_z = [push(z_s.at[z], z_s.at[z], sz_send.at[k - 1], sz_recv.at[k - 1], zs[k - 1]) for k in range(1, nz)]
+    for copy in small_z:
+        copy.start()
+
+    is_left = z < root
+    to_left = {"ctx": jnp.maximum(z - 1, 0) * 2 + core}
+    to_right = {"ctx": jnp.minimum(z + 1, nz - 1) * 2 + core}
+    far = max(root, nz - 1 - root)
+    depth = jnp.where(z == root, far, jnp.where(is_left, z, nz - 1 - z))
+    away = jnp.where(is_left, root - z, z - root)
+
+    def chain_push(i, side, peer):
+        block = grads.at[spot(i, w)]
+        return push(block, chain.at[side, lines(i)], ch_send.at[i], ch_recv.at[side, i], peer)
+
+    def total_push(i, side, peer):
+        block = totals.at[lines(i)]
+        return push(block, block, b_send.at[side, i], b_recv.at[i], peer)
+
+    def partner_push(i):
+        return push(totals.at[lines(i)], theirs.at[lines(i)], p_send.at[i], p_recv.at[i], partner)
+
+    def deliver(i, cc, source, side, go):
+        j, r = i // per, lax.rem(i, per)
+        places = [
+            (j < 2, lambda: down_o.at[pl.ds(pl.multiple_of(cc * gate_half + i * ROWS, 16), ROWS)]),
+            (
+                (j >= 2) & (j < 4),
+                lambda: up_o.at[
+                    pl.ds(pl.multiple_of(r * ROWS, 16), ROWS),
+                    pl.ds(pl.multiple_of((cc * 2 + j - 2) * D, 128), D),
+                ],
+            ),
+            (
+                j >= 4,
+                lambda: attn_o.at[cc * 2 + j - 4, pl.ds(pl.multiple_of(r * ROWS, 16), ROWS)],
+            ),
+        ]
+        for when, spot_of in places:
+
+            @pl.when(when)
+            def _():
+                go(pltpu.make_async_copy(source.at[lines(i)], spot_of(), o_sem.at[side, i]))
+
+    def start(copy):
+        copy.start()
+
+    def finish(copy):
+        copy.wait()
+
+    def step(t, _):
+        @pl.when(t + FLIGHT < count)
+        def _():
+            for k in range(1, W):
+                x_push(t, k).wait_send()
+                x_push(t + FLIGHT, k).start()
+
+        i = t - LAG * depth
+
+        @pl.when((i >= 0) & (i < count))
+        def _():
+            acc = grads[spot(i, w), :].astype(f32)
+            for k in range(1, W):
+                x_push(i, k).wait_recv()
+                acc = acc + from_x[k - 1, lines(i), :].astype(f32)
+            grads[spot(i, w), :] = acc.astype(bf16)
+
+            @pl.when((z > 0) & (z <= root))
+            def _():
+                chain_push(i, 0, to_right).wait_recv()
+                both = grads[spot(i, w), :].astype(f32) + chain[0, lines(i), :].astype(f32)
+                grads[spot(i, w), :] = both.astype(bf16)
+
+            @pl.when((z < nz - 1) & (z >= root))
+            def _():
+                chain_push(i, 1, to_left).wait_recv()
+                both = grads[spot(i, w), :].astype(f32) + chain[1, lines(i), :].astype(f32)
+                grads[spot(i, w), :] = both.astype(bf16)
+
+            @pl.when(z < root)
+            def _():
+                chain_push(i, 0, to_right).start()
+
+            @pl.when(z > root)
+            def _():
+                chain_push(i, 1, to_left).start()
+
+            @pl.when(z == root)
+            def _():
+                totals[lines(i), :] = grads[spot(i, w), :]
+
+        b = t - LAG * (far + away)
+
+        @pl.when((b >= 0) & (b < count))
+        def _():
+            @pl.when(z != root)
+            def _():
+                total_push(b, 0, to_left).wait_recv()
+
+            @pl.when((z <= root) & (z > 0))
+            def _():
+                total_push(b, 0, to_left).start()
+
+            @pl.when((z >= root) & (z < nz - 1))
+            def _():
+                total_push(b, 1, to_right).start()
+
+            partner_push(b).start()
+            deliver(b, core, totals, 0, start)
+
+        p = b - LAG
+
+        @pl.when((p >= 0) & (p < count))
+        def _():
+            partner_push(p).wait_recv()
+            deliver(p, 1 - core, theirs, 1, start)
+
+        return 0
+
+    lax.fori_loop(0, count + LAG * (2 * far + 1), step, 0)
+
+    for k in range(1, nz):
+        e = lax.rem(z + nz - k, nz)
+        push(z_s.at[z], z_s.at[e], sz_send.at[k - 1], sz_recv.at[k - 1], zs[k - 1]).wait_recv()
+    total = z_s[0]
+    for e in range(1, nz):
+        total = total + z_s[e]
+    small_o[...] = total
+
+    small_push.wait_send()
+    for copy in small_x + small_z:
+        copy.wait_send()
+    for copy in fast_x:
+        copy.wait_send()
+    for cc in range(2):
+
+        @pl.when(core == cc)
+        def _():
+            for copy in attn_copies(1 - cc, to_core, 1):
+                copy.wait_send()
+
+    def drain(i, _):
+        @pl.when(i + FLIGHT >= count)
+        def _():
+            for k in range(1, W):
+                x_push(i, k).wait_send()
+
+        partner_push(i).wait_send()
+        deliver(i, core, totals, 0, finish)
+        deliver(i, 1 - core, theirs, 1, finish)
+
+        @pl.when(z != root)
+        def _():
+            chain_push(i, 0, to_right).wait_send()
+
+        @pl.when((z <= root) & (z > 0))
+        def _():
+            total_push(i, 0, to_left).wait_send()
+
+        @pl.when((z >= root) & (z < nz - 1))
+        def _():
+            total_push(i, 1, to_right).wait_send()
+
+        return 0
+
+    lax.fori_loop(0, count, drain, 0)
 
 
 def counts_of(seq_lengths, rand_owner, rand_local, global_raw, c, n_ctx):
@@ -876,10 +1200,66 @@
     )
 
 
-def contract_rows(left_side, right_side):
-    return lax.dot_general(
-        left_side, right_side, (((0,), (0,)), ((), ())), preferred_element_type=f32
-    )
+def run_reduce(nz, W, MB, rows, small_g, tops, attn_w):
+    part, ffp, R = D // W, FF // W, MB * TD
+    per = part // ROWS
+    count = 6 * per
+    shape = jax.ShapeDtypeStruct
+    outs = [
+        shape((4, part, D), bf16),
+        shape((part, FF), bf16),
+        shape((ffp, D), bf16),
+        shape((16, D), f32),
+        shape((1, 2, part, D), bf16),
+    ]
+    scratch = [
+        pltpu.VMEM((2 * R, FF // 2), bf16),
+        pltpu.VMEM((2 * R, D), bf16),
+        pltpu.VMEM((2 * R, D), bf16),
+        pltpu.VMEM((2 * R, FF // 2), bf16),
+        pltpu.VMEM((2 * R, D), bf16),
+        pltpu.VMEM((2 * R, D), bf16),
+        pltpu.VMEM((2 * R, D), bf16),
+        pltpu.VMEM((2 * R, D), bf16),
+        pltpu.VMEM((6 * D, D), bf16),
+        pltpu.VMEM((W - 1, 6 * part, D), bf16),
+        pltpu.VMEM((2, 6 * part, D), bf16),
+        pltpu.VMEM((6 * part, D), bf16),
+        pltpu.VMEM((6 * part, D), bf16),
+        pltpu.VMEM((2, part, D), bf16),
+        pltpu.VMEM((2, 16, D), f32),
+        pltpu.VMEM((W, 16, D), f32),
+        pltpu.VMEM((nz, 16, D), f32),
+        DMA((W + 7 + 2 * MB,)),
+        DMA((W + 6 + 2 * MB,)),
+        DMA((W + 6 + 2 * MB,)),
+        DMA((W - 1, count)),
+        DMA((W - 1, count)),
+        DMA((count,)),
+        DMA((2, count)),
+        DMA((2, count)),
+        DMA((count,)),
+        DMA((count,)),
+        DMA((count,)),
+        DMA((2, count)),
+        DMA,
+        DMA,
+        DMA((W - 1,)),
+        DMA((W - 1,)),
+        DMA((nz - 1,)),
+        DMA((nz - 1,)),
+    ]
+    return pl.pallas_call(
+        functools.partial(reduce_kernel, nz, W, MB),
+        out_shape=outs,
+        in_specs=[ANY] * 8 + [VMEM, VMEM, ANY],
+        out_specs=[ANY] * 3 + [VMEM] * 2,
+        scratch_shapes=scratch,
+        compiler_params=pltpu.CompilerParams(
+            collective_id=2, has_side_effects=True, vmem_limit_bytes=60 << 20
+        ),
+        name="reduce",
+    )(*rows, small_g, tops, attn_w)
 
 
 def per_device(
@@ -906,33 +1286,18 @@
         nz, W, MB, lens, out_cotangent, counts_q, counts_k,
         (xall, kv, q, mix, lse, first, second, hidden, top, attn, up, down, small),
     )
-    head_tops = tops[0, :H]
-    factor = jnp.sqrt(clip_limit / jnp.maximum(head_tops, clip_limit))
-    clipped = (
-        attn_weights[0, :2].astype(f32).reshape(2, -1, H, HD) * factor[None, None, :, None]
-    )
-    clipped_qk = clipped.reshape(1, 2, -1, D).astype(bf16)
 
     def flat(v):
         return v.reshape(-1, v.shape[-1])
 
-    x_own = flat(lax.dynamic_slice_in_dim(xall, c * TD, TD, 1))
-    qkv = flat(rows_qkv)
-    grads = (
-        jnp.stack(
-            [contract_rows(x_own, qkv[:, p * D : (p + 1) * D]) for p in range(3)]
-            + [contract_rows(flat(att), flat(rows_branch))]
-        ),
-        contract_rows(flat(rows_normed), flat(rows_hidden)),
-        contract_rows(flat(rows_gated), flat(rows_down)),
+    rows = (
+        flat(rows_gated), flat(rows_down), flat(rows_normed), flat(rows_hidden), xall,
+        flat(rows_qkv), flat(att), flat(rows_branch),
     )
-    dims = (1, 0, 0)
-    shards = tuple(
-        lax.psum_scatter(g.astype(bf16), "wsh", scatter_dimension=d, tiled=True)
-        for g, d in zip(grads, dims)
+    grad_attn, grad_up, grad_down, small_g, clipped_qk = run_reduce(
+        nz, W, MB, rows, small_g, tops, attn_weights
     )
-    total = tuple(lax.psum(g, "ctx").astype(f32) for g in shards)
-    small_g = lax.psum(small_g, ("ctx", "wsh"))
+    total = (grad_attn.astype(f32), grad_up.astype(f32), grad_down.astype(f32))
     gains = lax.dynamic_slice(small_g[0:2], (0, w * part), (2, part))
     biases = lax.dynamic_slice(small_g[2:7], (0, w * part), (5, part))
     up_grad = lax.dynamic_slice(small_g[7:11].reshape(-1), (w * ffp,), (ffp,))

time: 645 us -> 411 us (0.64)
  waiting for transfers between devices: 266 us -> 0 us
  Pallas kernels: 265 us -> 386 us
  blocking collectives: 58.3 us -> 0 us
  between operations: 14 us -> 0.77 us
  matrix products: 10.8 us -> 0 us
    reduce_scatter x3 -> x0, waiting for transfers between devices: 175 us -> none  [per_device(): lax.psum_scatter(g.astype(bf16), 'wsh', scatter_dimension=d, tiled=True)]
    pallas_call x0 -> x1, Pallas kernels: none -> 123 us  [run_reduce(): pl.pallas_call(functools.partial(reduce_kernel, nz, W, MB), out_shape=out...]
    psum x1 -> x0, waiting for transfers between devices: 91.1 us -> none  [per_device(): total = tuple((lax.psum(g, 'ctx').astype(f32) for g in shards))]
    psum x1 -> x0, blocking collectives: 58.3 us -> none  [per_device(): small_g = lax.psum(small_g, ('ctx', 'wsh'))]
    dot_general x6 -> x0, matrix products: 10.8 us -> none  [contract_rows(): lax.dot_general(left_side, right_side, (((0,), (0,)), ((), ())), preferre...]
  transfers between devices with their start and end apart: 4 -> 0, of which waited for: 4 -> 0; matrix products, arithmetic and copies ran while one was open for 2% -> 0% of each run, Pallas kernels for 0% -> 0%
where the time goes in v2:
time: 411 us; the launch traced here: 410 us
  Pallas kernels  386 us (94%)
  other arithmetic  14.7 us (4%)
  local copies, waits for them, and re-layouts  8.11 us (2%)
    pallas_call x1, Pallas kernels, run_backward(): pl.pallas_call(functools.partial(backward_kernel, nz, W, MB, T), out_shap...  148 us
    pallas_call x1, Pallas kernels, run_reduce(): pl.pallas_call(functools.partial(reduce_kernel, nz, W, MB), out_shape=out...  123 us
    pallas_call x1, Pallas kernels, run_forward(): pl.pallas_call(functools.partial(forward_kernel, nz, W, MB, T), out_shape...  115 us

profile of v2, /device:TPU:25, one launch (start us, length us, event | category | flops | bytes accessed | tf_op | source)
XLA Modules:
  0.0 410.1 jit_solution(5415895776796127560)
XLA Ops:
  0.7 0.1 pad.9.clone
  0.7 0.7 compare_bitcast_fusion
  1.4 0.9 and_select_fusion
  2.3 0.1 fusion.1
  2.4 0.1 convert_reduce_fusion.2
  2.5 0.7 convert_reduce_fusion.1
  3.2 0.3 dynamic_update_slice.7
  3.5 0.7 convert_dynamic-update-slice_fusion
  4.3 0.7 maximum_maximum_fusion.small_in
  5.0 0.8 multiply_add_fusion
  5.8 0.2 convert_reduce_fusion
  6.1 0.1 select_convert_fusion
  6.2 0.1 dynamic-slice_bitcast_fusion
  6.3 0.2 copy.30
  6.6 0.6 slice_bitcast_fusion
  7.2 115.5 %forward.1 = (bf16[1,2,1,128,768]{4,3,2,1,0:T(8,128)(2,1)}, bf16[2,1024,768]{2,1,0:T(8,128)(2,1)}, bf16[2,1024,1536]{2,1,0:T(8,128)(2,1)}, bf16[2,128,768]{2,1,0...) custom-call(s32[2]{0:T(128)} %bitcast.49, ...), custom_call_target="tpu_custom_call" | custom-call | tf_op jit(solution)/shard_map/forward/pallas_call | solution.py:1111
  122.7 147.8 %backward.1 = (bf16[1,2,1,128,768]{4,3,2,1,0:T(8,128)(2,1)}, bf16[2,128,2304]{2,1,0:T(8,128)(2,1)}, bf16[2,128,768]{2,1,0:T(8,128)(2,1)}, bf16[2,128,768]{2,1,0:...) custom-call(s32[2]{0:T(128)} %bitcast.50, ...), custom_call_target="tpu_custom_call" | custom-call | tf_op jit(solution)/shard_map/backward/pallas_call | solution.py:1187
  270.5 123.1 %reduce.3 = (bf16[4,384,768]{2,1,0:T(8,128)(2,1)}, bf16[384,3072]{1,0:T(8,128)(2,1)}, bf16[1536,768]{1,0:T(8,128)(2,1)}, f32[16,768]{1,0:T(8,128)}, bf16[1,2,384,768]{3,2,1,0:T(8,128)(2,1)}) custom-call(bf16[256,3072]{1,0:T(8,128)(2,1)} %bitcast.39, bf16[256,768]{1,0:T(8,128)(2,1)} %bitcast.44, bf16[256,768]{1,0:T(8,128)(2,1)} %bitcast.43, ...), custom_call_target="tpu_custom_call" | custom-call | tf_op jit(solution)/shard_map/reduce/pallas_call | solution.py:1252
  393.7 0.7 slice.19
  394.4 0.6 dynamic-slice_bitcast_fusion.1
  395.0 0.8 slice.21
  395.8 0.7 slice.20
  396.6 0.6 broadcast_in_dim.70
  397.2 0.1 dynamic_slice.19
  397.2 0.6 broadcast_in_dim.71
  397.8 0.0 copy-start.1
  397.8 4.4 %bitcast_convert_fusion.2 = f32[1,4,384,768]{3,2,1,0:T(8,128)} fusion(bf16[4,384,768]{2,1,0:T(8,128)(2,1)} %get-tuple-element.62), kind=kLoop, calls=%fused_computation.2 | loop fusion | flops 1179648 | bytes 7077888 | tf_op jit(solution)/shard_map/broadcast_in_dim | solution.py:1305
  402.2 0.0 copy-done.1
  402.2 0.0 copy-start
  402.2 2.8 bitcast_convert_fusion.1
  405.0 0.0 copy-done
  405.0 0.0 copy-start.3
  405.0 0.0 copy-start.4
  405.0 2.5 bitcast_convert_fusion
  407.6 0.0 copy-done.3
  407.6 0.0 copy-start.2
  407.6 0.7 copy.38
  408.3 0.0 copy-done.4
  408.3 0.7 copy.39
  409.1 0.0 copy-done.2
  409.1 1.0 copy.40
  (11 shorter events, 0.1 us)
Async XLA Ops:
  397.8 4.4 %copy-start.1 = (bf16[384,3072]{1,0:T(8,128)(2,1)S(1)}, bf16[384,3072]{1,0:T(8,128)(2,1)}, u32[]{:S(2)}) copy-start(bf16[384,3072]{1,0:T(8,128)(2,1)} %get-tuple-element.63) | copy-start | bytes 7077892
  402.2 2.8 copy-start
  405.0 2.6 copy-start.3
  405.0 3.3 copy-start.4
  407.6 1.5 copy-start.2

commit v3 on v2

--- a/solution.py
+++ b/solution.py
@@ -128,15 +128,15 @@
     attn, up, down, small_all, small, xall, kv, q, att, mix, lse, top, first, second, hidden, out,
     wide,
     load_sem, w_send, w_recv, wf_send, wf_recv, s_send, s_recv,
-    b_send, b_recv, f_send, f_recv, o_send, save_sem,
+    b_send, b_recv, f_send, f_recv, o_send, r_send, r_recv, save_sem,
 ):
     s, c, w = place()
     z, core = c // 2, lax.rem(c, 2)
+    par = lax.rem(z, 2)
     part = D // W
-    half = part // 2
     ffp = FF // W
-    ffh = ffp // 2
     partner = {"ctx": c + 1 - 2 * core}
+    buddy = {"ctx": (z + 1 - 2 * par) * 2 + core}
     xs = [{"wsh": lax.rem(w + k, W)} for k in range(1, W)]
     zs = [{"ctx": lax.rem(z + k, nz) * 2 + core} for k in range(1, nz)]
     over = [{"section": 1 - s, "ctx": lax.rem(z + k, nz) * 2 + core} for k in range(nz)]
@@ -145,51 +145,117 @@
     def rows_of(zz, cc):
         return pl.ds(pl.multiple_of((zz * 2 + cc) * TD, TD), TD)
 
+    def direct_rows(zz, cc):
+        return pl.ds(pl.multiple_of((zz * 2 + cc) * TD, TD), BLK)
+
+    def relay_rows(zz, cc):
+        return pl.ds(pl.multiple_of((zz * 2 + cc) * TD + BLK, BLK), BLK)
+
     mine = rows_of(z, core)
 
     def token_push(m, k):
+        peer = zs[k - 1] if m == 0 else over[k]
+        return push(tokens.at[m, 0], xall.at[m, mine], b_send.at[m, k], b_recv.at[m, k], peer)
+
+    def token_arrival(m, k):
+        block = xall.at[m, rows_of(lax.rem(z + nz - k, nz), core)]
+        return push(block, block, b_send.at[m, k], b_recv.at[m, k], partner)
+
+    def own_tokens(m):
+        return pltpu.make_async_copy(tokens.at[m, 0], xall.at[m, mine], b_recv.at[m, 0])
+
+    def out_push(m, k):
         return push(
-            tokens.at[m, 0], xall.at[m, mine], b_send.at[m, k], b_recv.at[m, k], zs[k - 1]
+            out.at[m, 0:BLK],
+            xall.at[m, direct_rows(z, core)],
+            o_send.at[m, k],
+            b_recv.at[m, k],
+            over[k],
         )
 
-    def block_arrival(m, k):
-        zz = lax.rem(z + nz - k, nz)
+    def out_arrival(m, k):
+        block = xall.at[m, direct_rows(lax.rem(z + nz - k, nz), core)]
+        return push(block, block, o_send.at[m, k], b_recv.at[m, k], partner)
+
+    def out_relay(m):
         return push(
-            xall.at[m, mine],
-            xall.at[m, rows_of(zz, core)],
-            b_send.at[m, k],
-            b_recv.at[m, k],
+            out.at[m, BLK:TD],
+            xall.at[m, relay_rows(z, core)],
+            r_send.at[m, 0],
+            r_recv.at[m, 0],
             over[0],
         )
+
+    def relay_push(m, k):
+        block = xall.at[m, relay_rows(z, core)]
+        return push(block, block, r_send.at[m, k], r_recv.at[m, k], zs[k - 1])
+
+    def relay_arrival(m, k):
+        block = xall.at[m, relay_rows(lax.rem(z + nz - k, nz), core)]
+        return push(block, block, r_send.at[m, k], r_recv.at[m, k], partner)
 
     def forward_push(m, k):
         zz = lax.rem(z + nz - k, nz)
         block = xall.at[m, rows_of(zz, core)]
         return push(block, block, f_send.at[m, k], f_recv.at[m, k], partner)
 
-    def out_push(m, k):
-        return push(out.at[m], xall.at[m, mine], o_send.at[m, k], b_recv.at[m, k], over[k])
-
-    def own_tokens(m):
-        return pltpu.make_async_copy(tokens.at[m, 0], xall.at[m, mine], b_recv.at[m, 0])
-
-    def pieces(cc, ww):
-        r = pl.ds(pl.multiple_of(ww * part + cc * half, 16), half)
-        f = pl.ds(pl.multiple_of(ww * ffp + cc * ffh, 16), ffh)
-        return [attn.at[0:3, r], attn.at[3:4, r], up.at[r], down.at[f]]
-
-    sr = pl.ds(pl.multiple_of(core * half, 16), half)
-    sf = pl.ds(pl.multiple_of(core * ffh, 16), ffh)
-    sources = [attn_w.at[0, 0:3, sr], attn_w.at[0, 3:4, sr], up_w.at[0, sr], down_w.at[0, sf]]
+    def cut(base, ww, stride, rows, cc, zp, shared):
+        share = rows // 4 if shared else rows // 2
+        at = base + ww * stride + ((cc * 2 + zp) if shared else cc) * share
+        return pl.ds(pl.multiple_of(at, 16), share)
+
+    def piece(p, ww, cc, zp, local):
+        stride = 0 if local else 1
+        if p < 4:
+            r = cut(0, ww, part * stride, part, cc, zp, False)
+            matrix = (1, 2, 0, 3)[p]
+            return attn_w.at[0, matrix, r] if local else attn.at[matrix, r]
+        if p < 6:
+            r = cut(0, ww, part * stride, part, cc, zp, True)
+            cols = pl.ds((p - 4) * (FF // 2), FF // 2)
+            return up_w.at[0, r, cols] if local else up.at[r, cols]
+        base = (p - 6) * (ffp // 2)
+        r = cut(base, ww, ffp * stride, ffp // 2, cc, zp, p == 6)
+        return down_w.at[0, r] if local else down.at[r]
+
+    shared = [p in (4, 5, 6) for p in range(8)]
 
     def weight_push(k, p):
         return push(
-            sources[p], pieces(core, w)[p], w_send.at[k - 1, p], w_recv.at[k - 1, p], xs[k - 1]
+            piece(p, w, core, par, True),
+            piece(p, w, core, par, False),
+            w_send.at[k - 1, p],
+            w_recv.at[k - 1, p],
+            xs[k - 1],
         )
 
-    def weight_forward(k, p):
-        spot = pieces(core, lax.rem(w + W - k, W))[p]
-        return push(spot, spot, wf_send.at[k - 1, p], wf_recv.at[k - 1, p], partner)
+    def weight_forward(k, p, way):
+        zp = 1 - par if way == 2 else par
+        spot = piece(p, lax.rem(w + W - k, W), core, zp, False)
+        peer = buddy if way == 1 else partner
+        return push(spot, spot, wf_send.at[k - 1, p, way], wf_recv.at[k - 1, p, way], peer)
+
+    def x_start(p):
+        for k in range(1, W):
+            weight_push(k, p).start()
+
+    def x_arrive(p):
+        for k in range(1, W):
+            weight_push(k, p).wait_recv()
+            weight_forward(k, p, 0).start()
+            if shared[p]:
+                weight_forward(k, p, 1).start()
+
+    def z_arrive(p):
+        for k in range(1, W):
+            weight_forward(k, p, 1).wait_recv()
+            weight_forward(k, p, 2).start()
+
+    def core_arrive(p):
+        for k in range(1, W):
+            weight_forward(k, p, 0).wait_recv()
+            if shared[p]:
+                weight_forward(k, p, 2).wait_recv()
 
     def small_push(k):
         return push(small_in, small_all.at[k], s_send.at[k - 1], s_recv.at[k - 1], xs[k - 1])
@@ -197,40 +263,35 @@
     own_r = pl.ds(pl.multiple_of(w * part, 16), part)
     own_f = pl.ds(pl.multiple_of(w * ffp, 16), ffp)
     own_loads = [
-        pltpu.make_async_copy(attn_w.at[0, 0:3], attn.at[0:3, own_r], load_sem.at[0]),
-        pltpu.make_async_copy(attn_w.at[0, 3:4], attn.at[3:4, own_r], load_sem.at[1]),
-        pltpu.make_async_copy(up_w.at[0], up.at[own_r], load_sem.at[2]),
-        pltpu.make_async_copy(down_w.at[0], down.at[own_f], load_sem.at[3]),
+        pltpu.make_async_copy(attn_w.at[0], attn.at[:, own_r], load_sem.at[0]),
+        pltpu.make_async_copy(up_w.at[0], up.at[own_r], load_sem.at[1]),
+        pltpu.make_async_copy(down_w.at[0], down.at[own_f], load_sem.at[2]),
     ]
 
     @pl.when(s == 0)
     def _():
-        own_tokens(0).start()
         for k in range(1, nz):
             token_push(0, k).start()
-
-    for p in range(4):
-        own_loads[p].start()
+        for m in range(MB):
+            own_tokens(m).start()
+
+    @pl.when(s == 1)
+    def _():
+        for m in range(1, MB):
+            for k in range(1, nz):
+                token_push(m, k).start()
+
+    x_start(0)
+    x_start(1)
     for k in range(1, W):
         small_push(k).start()
-    for p in range(4):
-        for k in range(1, W):
-            weight_push(k, p).start()
-
-    @pl.when(s == 0)
-    def _():
-        for m in range(1, MB):
-            own_tokens(m).start()
-            for k in range(1, nz):
-                token_push(m, k).start()
-
-    def weights_ready(p):
-        for k in range(1, W):
-            weight_push(k, p).wait_recv()
-            weight_forward(k, p).start()
-        own_loads[p].wait()
-        for k in range(1, W):
-            weight_forward(k, p).wait_recv()
+    for copy in own_loads:
+        copy.start()
+
+    def relay_start(m):
+        out_relay(m).wait_recv()
+        for k in range(1, nz):
+            relay_push(m, k).start()
 
     def rows_ready(m):
         @pl.when(s == 0)
@@ -239,11 +300,20 @@
 
         @pl.when(s == 1)
         def _():
-            block_arrival(m, 0).wait_recv()
+            out_arrival(m, 0).wait_recv()
 
         forward_push(m, 0).start()
         for k in range(1, nz):
-            block_arrival(m, k).wait_recv()
+
+            @pl.when(s == 0)
+            def _():
+                token_arrival(m, k).wait_recv()
+
+            @pl.when(s == 1)
+            def _():
+                out_arrival(m, k).wait_recv()
+                relay_arrival(m, k).wait_recv()
+
             forward_push(m, k).start()
         for k in range(nz):
             forward_push(m, k).wait_recv()
@@ -263,19 +333,51 @@
 
     slots = kv.shape[0]
 
+    @pl.when(s == 1)
+    def _():
+        for p in range(8):
+            x_arrive(p)
+            if p + 2 < 8:
+                x_start(p + 2)
+            if p and shared[p - 1]:
+                z_arrive(p - 1)
+        for p in range(8):
+            core_arrive(p)
+        relay_start(0)
+
+    @pl.when(s == 0)
+    def _():
+        for p in range(3):
+            x_arrive(p)
+            x_start(p + 2)
+        x_start(5)
+
+    for k in range(1, W):
+        small_push(k).wait_recv()
+    total = small_in[...]
+    for k in range(1, W):
+        total = total + small_all[k]
+    small[...] = total
+    save(small, small_o)
+    own_loads[0].wait()
+    bias_v = small[0:1, :]
+
     for m in range(MB):
         rows_ready(m)
+        if m + 1 < MB:
+
+            @pl.when(s == 1)
+            def _():
+                relay_start(m + 1)
+
         if m == 0:
-            weights_ready(0)
-            for k in range(1, W):
-                small_push(k).wait_recv()
-            total = small_in[...]
-            for k in range(1, W):
-                total = total + small_all[k]
-            small[...] = total
-            save(small, small_o)
+
+            @pl.when(s == 0)
+            def _():
+                for p in range(3):
+                    core_arrive(p)
+
         save(xall.at[m], xall_o.at[m])
-        bias_v = small[0:1, :]
 
         def project(i, _):
             r = pl.ds(pl.multiple_of(i * 256, 256), 256)
@@ -326,21 +428,52 @@
         save(lse.at[m], lse_o.at[m])
         save(mix.at[m], mix_o.at[m])
         save(att.at[m], att_o.at[m])
+        if m < 2:
+
+            @pl.when(s == 0)
+            def _():
+                if m == 0:
+                    x_arrive(3)
+                x_start(6 + m)
+
+    if MB == 1:
+
+        @pl.when(s == 0)
+        def _():
+            x_start(7)
 
     top[...] = jnp.broadcast_to(tops, (8, 128))
     save(top, top_o)
-    for p in range(1, 4):
-        weights_ready(p)
+
+    @pl.when(s == 0)
+    def _():
+        core_arrive(3)
+
+    for m in range(MB):
+        branch = dot(att[m], attn[3]) + small[1:2, :]
+        first[m] = xall[m, mine, :].astype(f32) + branch
+        save(first.at[m], first_o.at[m])
     save(attn, attn_o)
+
+    @pl.when(s == 0)
+    def _():
+        x_arrive(4)
+        x_arrive(5)
+        z_arrive(4)
+        x_arrive(6)
+        z_arrive(5)
+        x_arrive(7)
+        z_arrive(6)
+        for p in range(4, 8):
+            core_arrive(p)
+
+    for copy in own_loads[1:]:
+        copy.wait()
     save(up, up_o)
     save(down, down_o)
 
     for m in range(MB):
-        branch = dot(att[m], attn[3]) + small[1:2, :]
-        first_sum = xall[m, mine, :].astype(f32) + branch
-        first[m] = first_sum
-        save(first.at[m], first_o.at[m])
-        hat, _ = norm_parts(first_sum)
+        hat, _ = norm_parts(first[m])
         normed = hat * small[5:6, :] + small[3:4, :]
         low = normed.astype(bf16)
         second[m] = normed + small[2:3, :]
@@ -349,33 +482,50 @@
             pre = dot(low, up[:, cols]) + small[7 + j : 8 + j, :]
             hidden[m, :, cols] = pre
             second[m] += dot(gelu(pre).astype(bf16), down[cols, :])
+        hat, _ = norm_parts(second[m])
+        out[m] = (hat * small[6:7, :] + small[4:5, :]).astype(bf16)
+
         save(hidden.at[m], hidden_o.at[m])
         save(second.at[m], second_o.at[m])
-        hat, _ = norm_parts(second[m])
-        out[m] = (hat * small[6:7, :] + small[4:5, :]).astype(bf16)
+        save(out.at[m], out_o.at[0, m, 0])
 
         @pl.when(s == 0)
         def _():
+            if m:
+                for k in range(nz):
+                    out_push(m - 1, k).wait_send()
+            out_relay(m).start()
+            out_relay(m).wait_send()
             for k in range(nz):
                 out_push(m, k).start()
 
-        save(out.at[m], out_o.at[0, m, 0])
 
     for k in range(1, W):
         small_push(k).wait_send()
-        for p in range(4):
+        for p in range(8):
             weight_push(k, p).wait_send()
-            weight_forward(k, p).wait_send()
+            for way in range(3 if shared[p] else 1):
+                weight_forward(k, p, way).wait_send()
     for m in range(MB):
         for k in range(nz):
             forward_push(m, k).wait_send()
 
-        @pl.when(s == 0)
+        if m == MB - 1:
+
+            @pl.when(s == 0)
+            def _():
+                for k in range(nz):
+                    out_push(m, k).wait_send()
+
+        @pl.when(s == 1)
+        def _():
+            for k in range(1, nz):
+                relay_push(m, k).wait_send()
+
+        @pl.when(s == (0 if m == 0 else 1))
         def _():
             for k in range(1, nz):
                 token_push(m, k).wait_send()
-            for k in range(nz):
-                out_push(m, k).wait_send()
 
     for copy in saves:
         copy.wait()
@@ -387,10 +537,10 @@
     attn_h, up_h, down_h, small,
     grad_in_o, rows_qkv, rows_branch, rows_normed, rows_hidden, rows_gated, rows_down, small_o, top_o,
     attn, up, down, xall, kv, q, mix, lse, first, second, hidden, dout,
-    gfirst, gbranch, gall, aux, kvp, wide_q, wide_k, lse_all, del_all, del_c, dqkv, gnorm, ghid, gated,
+    gfirst, gbranch, gall, relay, aux, kvp, wide_q, wide_k, lse_all, del_all, del_c, dqkv, gnorm, ghid, gated,
     gdown, small_g, gin, top_x,
     load_sem, y_send, y_recv, b_send, b_recv, f_send, f_recv, a_send, a_recv, af_send, af_recv,
-    t_send, t_recv, kvp_sem, save_sem,
+    t_send, t_recv, r_send, r_recv, kvp_sem, save_sem,
 ):
     s, c, w = place()
     z, core = c // 2, lax.rem(c, 2)
@@ -398,7 +548,8 @@
     xs = [{"wsh": lax.rem(w + k, W)} for k in range(1, W)]
     zs = [{"ctx": lax.rem(z + k, nz) * 2 + core} for k in range(1, nz)]
     across = {"section": 1 - s}
-    greet(xs + zs + [across, partner])
+    over = [{"section": 1 - s, "ctx": lax.rem(z + k, nz) * 2 + core} for k in range(1, nz)]
+    greet(xs + zs + over + [across, partner])
 
     def rows_of(zz, cc):
         return pl.ds(pl.multiple_of((zz * 2 + cc) * TD, TD), TD)
@@ -445,19 +596,52 @@
     load_kv = [load(kv_h.at[m, mine], kv.at[m]) for m in range(MB)]
     load_q = [load(q_h.at[m], q.at[m]) for m in range(MB)]
 
+    def cut_rows(zz, cc, side):
+        return pl.ds(pl.multiple_of((zz * 2 + cc) * TD + side * BLK, BLK), BLK)
+
     def rows_push(m, k):
-        block = gall.at[m, mine]
-        peer = partner if k == 0 else zs[k - 1]
-        send, recv = (f_send, f_recv) if k == 0 else (b_send, b_recv)
-        return push(block, block, send.at[m, k], recv.at[m, k], peer)
+        if k == 0:
+            block = gall.at[m, mine]
+            return push(block, block, f_send.at[m, 0], f_recv.at[m, 0], partner)
+        block = gall.at[m, cut_rows(z, core, 0)]
+        return push(block, block, b_send.at[m, k], b_recv.at[m, k], zs[k - 1])
 
     def rows_arrival(m, k):
-        block = gall.at[m, rows_of(lax.rem(z + nz - k, nz), core)]
+        block = gall.at[m, cut_rows(lax.rem(z + nz - k, nz), core, 0)]
         return push(block, block, b_send.at[m, k], b_recv.at[m, k], partner)
+
+    def relay_out(m):
+        block = gall.at[m, cut_rows(z, core, 1)]
+        return push(block, relay.at[m], r_send.at[m, 0], r_recv.at[m, 0], across)
+
+    def relay_push(m, k):
+        block = gall.at[m, cut_rows(z, core, 1)]
+        return push(relay.at[m], block, r_send.at[m, k], r_recv.at[m, k], over[k - 1])
+
+    def relay_arrival(m, k):
+        block = gall.at[m, cut_rows(lax.rem(z + nz - k, nz), core, 1)]
+        return push(block, block, r_send.at[m, k], r_recv.at[m, k], partner)
 
     def rows_forward(m, k):
         block = gall.at[m, rows_of(lax.rem(z + nz - k, nz), core)]
         return push(block, block, f_send.at[m, k], f_recv.at[m, k], partner)
+
+    def spread_start(m):
+        relay_out(m).start()
+        for k in range(nz):
+            aux_push(m, k).start()
+            rows_push(m, k).start()
+
+    def spread_sent(m):
+        relay_out(m).wait_send()
+        for k in range(1, nz):
+            rows_push(m, k).wait_send()
+
+    def relay_all():
+        for m in range(MB):
+            relay_out(m).wait_recv()
+            for k in range(1, nz):
+                relay_push(m, k).start()
 
     def aux_push(m, k):
         block = aux.at[m, c]
@@ -475,6 +659,10 @@
 
     def top_push(k):
         return push(top_x.at[0], top_x.at[k], t_send.at[k - 1], t_recv.at[k - 1], xs[k - 1])
+
+    @pl.when(s == 0)
+    def _():
+        relay_all()
 
     heads = lax.broadcasted_iota(jnp.int32, (D, 128), 0)
     heads = lax.shift_right_logical(heads, 6) == lax.broadcasted_iota(jnp.int32, (D, 128), 1)
@@ -542,16 +730,14 @@
             load_attn.wait()
         grad_att = dot_t(low_first, attn[3]).astype(bf16)
         gall[m, mine, :] = grad_att
-        for k in range(nz):
-            rows_push(m, k).start()
         weighed = grad_att.astype(f32) * mix[m]
         delta = jnp.dot(weighed, heads, preferred_element_type=f32, precision=exact_dot)
         del_c[m] = delta
         aux[m, c, 0:16] = lse[m].T[0:16]
         aux[m, c, 16:32] = delta.T[0:16]
         aux[m, c, 32:40] = top[...]
-        for k in range(nz):
-            aux_push(m, k).start()
+        if m == 0:
+            spread_start(0)
 
     spots = lax.broadcasted_iota(jnp.int32, (1, T), 1)
     rows_here = lax.broadcasted_iota(jnp.int32, (TD, 128), 0)
@@ -607,6 +793,9 @@
             return 0
 
         lax.fori_loop(0, PAIRS, own_rows, 0)
+        if m + 1 < MB:
+            spread_sent(m)
+            spread_start(m + 1)
 
         def project(i, _):
             r = pl.ds(pl.multiple_of(i * 256, 256), 256)
@@ -617,6 +806,7 @@
         lax.fori_loop(0, T // 256, project, 0)
         for k in range(1, nz):
             rows_arrival(m, k).wait_recv()
+            relay_arrival(m, k).wait_recv()
             rows_forward(m, k).start()
             aux_arrival(m, k).wait_recv()
             aux_forward(m, k).start()
@@ -678,6 +868,10 @@
 
         save(gin.at[m], grad_in_o.at[0, m, 0])
 
+    @pl.when(s == 1)
+    def _():
+        relay_all()
+
     save(small_g, small_o)
     for k in range(1, W):
         top_push(k).wait()
@@ -690,8 +884,10 @@
             rows_forward(m, k).wait_send()
             aux_forward(m, k).wait_send()
         for k in range(1, nz):
-            rows_push(m, k).wait_send()
             aux_push(m, k).wait_send()
+            relay_push(m, k).wait_send()
+        if m == MB - 1:
+            spread_sent(m)
 
         @pl.when(s == 1)
         def _():
@@ -1094,13 +1290,15 @@
         pltpu.VMEM((MB, TD, FF), f32),
         pltpu.VMEM((MB, TD, D), bf16),
         pltpu.VMEM((PAIRS, 8, T), f32),
-        DMA((4,)),
-        DMA((W - 1, 4)),
-        DMA((W - 1, 4)),
-        DMA((W - 1, 4)),
-        DMA((W - 1, 4)),
+        DMA((3,)),
+        DMA((W - 1, 8)),
+        DMA((W - 1, 8)),
+        DMA((W - 1, 8, 3)),
+        DMA((W - 1, 8, 3)),
         DMA((W - 1,)),
         DMA((W - 1,)),
+        DMA((MB, nz)),
+        DMA((MB, nz)),
         DMA((MB, nz)),
         DMA((MB, nz)),
         DMA((MB, nz)),
@@ -1153,6 +1351,7 @@
         pltpu.VMEM((MB, TD, D), f32),
         pltpu.VMEM((MB, TD, D), bf16),
         pltpu.VMEM((MB, T, D), bf16),
+        pltpu.VMEM((MB, BLK, D), bf16),
         pltpu.VMEM((MB, 2 * nz, 40, 128), f32),
         pltpu.VMEM((2, 2, T, 2 * HD), bf16),
         pltpu.VMEM((PAIRS, 8, T), f32),
@@ -1181,6 +1380,8 @@
         DMA((MB, nz)),
         DMA((W - 1,)),
         DMA((W - 1,)),
+        DMA((MB, nz)),
+        DMA((MB, nz)),
         DMA((2, 2)),
         DMA((1 + 7 * MB,)),
     ]

time: 411 us -> 361 us (0.88)
  Pallas kernels: 386 us -> 336 us
    pallas_call x1, Pallas kernels: 148 us -> 118 us  [run_backward(): pl.pallas_call(functools.partial(backward_kernel, nz, W, MB, T), out_shap...]
    pallas_call x1, Pallas kernels: 115 us -> 93.7 us  [run_forward(): pl.pallas_call(functools.partial(forward_kernel, nz, W, MB, T), out_shape...]
where the time goes in v3:
time: 361 us; the launch traced here: 360 us
  Pallas kernels  336 us (93%)
  other arithmetic  14.7 us (4%)
  local copies, waits for them, and re-layouts  8.11 us (2%)
    pallas_call x1, Pallas kernels, run_reduce(): pl.pallas_call(functools.partial(reduce_kernel, nz, W, MB), out_shape=out...  124 us
    pallas_call x1, Pallas kernels, run_backward(): pl.pallas_call(functools.partial(backward_kernel, nz, W, MB, T), out_shap...  118 us
    pallas_call x1, Pallas kernels, run_forward(): pl.pallas_call(functools.partial(forward_kernel, nz, W, MB, T), out_shape...  93.7 us

profile of v3, /device:TPU:25, one launch (start us, length us, event | category | flops | bytes accessed | tf_op | source)
XLA Modules:
  0.0 360.1 jit_solution(12028813881317779047)
XLA Ops:
  0.7 0.1 pad.9.clone
  0.7 0.7 compare_bitcast_fusion
  1.4 0.9 and_select_fusion
  2.3 0.1 fusion.1
  2.4 0.1 convert_reduce_fusion.2
  2.5 0.7 convert_reduce_fusion.1
  3.2 0.3 dynamic_update_slice.7
  3.5 0.7 convert_dynamic-update-slice_fusion
  4.3 0.7 maximum_maximum_fusion.small_in
  5.0 0.8 multiply_add_fusion
  5.8 0.2 convert_reduce_fusion
  6.1 0.1 select_convert_fusion
  6.2 0.1 dynamic-slice_bitcast_fusion
  6.3 0.2 copy.30
  6.6 0.6 slice_bitcast_fusion
  7.2 93.7 %forward.1 = (bf16[1,2,1,128,768]{4,3,2,1,0:T(8,128)(2,1)}, bf16[2,1024,768]{2,1,0:T(8,128)(2,1)}, bf16[2,1024,1536]{2,1,0:T(8,128)(2,1)}, bf16[2,128,768]{2,1,0...) custom-call(s32[2]{0:T(128)} %bitcast.49, ...), custom_call_target="tpu_custom_call" | custom-call | tf_op jit(solution)/shard_map/forward/pallas_call | solution.py:1309
  100.9 118.3 %backward.1 = (bf16[1,2,1,128,768]{4,3,2,1,0:T(8,128)(2,1)}, bf16[2,128,2304]{2,1,0:T(8,128)(2,1)}, bf16[2,128,768]{2,1,0:T(8,128)(2,1)}, bf16[2,128,768]{2,1,0:...) custom-call(s32[2]{0:T(128)} %bitcast.50, ...), custom_call_target="tpu_custom_call" | custom-call | tf_op jit(solution)/shard_map/backward/pallas_call | solution.py:1388
  219.3 124.4 %reduce.3 = (bf16[4,384,768]{2,1,0:T(8,128)(2,1)}, bf16[384,3072]{1,0:T(8,128)(2,1)}, bf16[1536,768]{1,0:T(8,128)(2,1)}, f32[16,768]{1,0:T(8,128)}, bf16[1,2,384,768]{3,2,1,0:T(8,128)(2,1)}) custom-call(bf16[256,3072]{1,0:T(8,128)(2,1)} %bitcast.39, bf16[256,768]{1,0:T(8,128)(2,1)} %bitcast.44, bf16[256,768]{1,0:T(8,128)(2,1)} %bitcast.43, ...), custom_call_target="tpu_custom_call" | custom-call | tf_op jit(solution)/shard_map/reduce/pallas_call | solution.py:1453
  343.7 0.7 slice.19
  344.4 0.6 dynamic-slice_bitcast_fusion.1
  345.0 0.8 slice.21
  345.8 0.7 slice.20
  346.5 0.6 broadcast_in_dim.70
  347.1 0.1 dynamic_slice.19
  347.2 0.6 broadcast_in_dim.71
  347.8 0.0 copy-start.1
  347.8 4.4 %bitcast_convert_fusion.2 = f32[1,4,384,768]{3,2,1,0:T(8,128)} fusion(bf16[4,384,768]{2,1,0:T(8,128)(2,1)} %get-tuple-element.62), kind=kLoop, calls=%fused_computation.2 | loop fusion | flops 1179648 | bytes 7077888 | tf_op jit(solution)/shard_map/broadcast_in_dim | solution.py:1506
  352.2 0.0 copy-done.1
  352.2 0.0 copy-start
  352.2 2.8 bitcast_convert_fusion.1
  355.0 0.0 copy-done
  355.0 0.0 copy-start.3
  355.0 0.0 copy-start.4
  355.0 2.5 bitcast_convert_fusion
  357.5 0.0 copy-done.3
  357.5 0.0 copy-start.2
  357.5 0.7 copy.38
  358.3 0.0 copy-done.4
  358.3 0.7 copy.39
  359.0 0.0 copy-done.2
  359.0 1.0 copy.40
  (11 shorter events, 0.1 us)
Async XLA Ops:
  347.8 4.4 %copy-start.1 = (bf16[384,3072]{1,0:T(8,128)(2,1)S(1)}, bf16[384,3072]{1,0:T(8,128)(2,1)}, u32[]{:S(2)}) copy-start(bf16[384,3072]{1,0:T(8,128)(2,1)} %get-tuple-element.63) | copy-start | bytes 7077892
  352.2 2.8 copy-start
  355.0 2.6 copy-start.3
  355.0 3.3 copy-start.4
  357.5 1.5 copy-start.2

commit v4 on v1

--- a/solution.py
+++ b/solution.py
@@ -1,4 +1,5 @@
 import functools
+import types
 
 import jax
 import jax.numpy as jnp
@@ -18,6 +19,12 @@
 CHUNK = 768
 NCH = FF // CHUNK
 STEP = 1024
+ROWS = 48
+FLIGHT = 4
+LAG = 3
+PACE = 1
+EARLY = 4
+RINGS = [a + b for a in ("b", "f", "a", "af", "r") for b in ("_send", "_recv")]
 
 MESH = pl.DeviceIdType.MESH
 norm_eps = 1e-05
@@ -125,15 +132,15 @@
     attn, up, down, small_all, small, xall, kv, q, att, mix, lse, top, first, second, hidden, out,
     wide,
     load_sem, w_send, w_recv, wf_send, wf_recv, s_send, s_recv,
-    b_send, b_recv, f_send, f_recv, o_send, save_sem,
+    b_send, b_recv, f_send, f_recv, o_send, r_send, r_recv, save_sem,
 ):
     s, c, w = place()
     z, core = c // 2, lax.rem(c, 2)
+    par = lax.rem(z, 2)
     part = D // W
-    half = part // 2
     ffp = FF // W
-    ffh = ffp // 2
     partner = {"ctx": c + 1 - 2 * core}
+    buddy = {"ctx": (z + 1 - 2 * par) * 2 + core}
     xs = [{"wsh": lax.rem(w + k, W)} for k in range(1, W)]
     zs = [{"ctx": lax.rem(z + k, nz) * 2 + core} for k in range(1, nz)]
     over = [{"section": 1 - s, "ctx": lax.rem(z + k, nz) * 2 + core} for k in range(nz)]
@@ -142,51 +149,117 @@
     def rows_of(zz, cc):
         return pl.ds(pl.multiple_of((zz * 2 + cc) * TD, TD), TD)
 
+    def direct_rows(zz, cc):
+        return pl.ds(pl.multiple_of((zz * 2 + cc) * TD, TD), BLK)
+
+    def relay_rows(zz, cc):
+        return pl.ds(pl.multiple_of((zz * 2 + cc) * TD + BLK, BLK), BLK)
+
     mine = rows_of(z, core)
 
     def token_push(m, k):
+        peer = zs[k - 1] if m == 0 else over[k]
+        return push(tokens.at[m, 0], xall.at[m, mine], b_send.at[m, k], b_recv.at[m, k], peer)
+
+    def token_arrival(m, k):
+        block = xall.at[m, rows_of(lax.rem(z + nz - k, nz), core)]
+        return push(block, block, b_send.at[m, k], b_recv.at[m, k], partner)
+
+    def own_tokens(m):
+        return pltpu.make_async_copy(tokens.at[m, 0], xall.at[m, mine], b_recv.at[m, 0])
+
+    def out_push(m, k):
         return push(
-            tokens.at[m, 0], xall.at[m, mine], b_send.at[m, k], b_recv.at[m, k], zs[k - 1]
+            out.at[m, 0:BLK],
+            xall.at[m, direct_rows(z, core)],
+            o_send.at[m, k],
+            b_recv.at[m, k],
+            over[k],
         )
 
-    def block_arrival(m, k):
-        zz = lax.rem(z + nz - k, nz)
+    def out_arrival(m, k):
+        block = xall.at[m, direct_rows(lax.rem(z + nz - k, nz), core)]
+        return push(block, block, o_send.at[m, k], b_recv.at[m, k], partner)
+
+    def out_relay(m):
         return push(
-            xall.at[m, mine],
-            xall.at[m, rows_of(zz, core)],
-            b_send.at[m, k],
-            b_recv.at[m, k],
+            out.at[m, BLK:TD],
+            xall.at[m, relay_rows(z, core)],
+            r_send.at[m, 0],
+            r_recv.at[m, 0],
             over[0],
         )
+
+    def relay_push(m, k):
+        block = xall.at[m, relay_rows(z, core)]
+        return push(block, block, r_send.at[m, k], r_recv.at[m, k], zs[k - 1])
+
+    def relay_arrival(m, k):
+        block = xall.at[m, relay_rows(lax.rem(z + nz - k, nz), core)]
+        return push(block, block, r_send.at[m, k], r_recv.at[m, k], partner)
 
     def forward_push(m, k):
         zz = lax.rem(z + nz - k, nz)
         block = xall.at[m, rows_of(zz, core)]
         return push(block, block, f_send.at[m, k], f_recv.at[m, k], partner)
 
-    def out_push(m, k):
-        return push(out.at[m], xall.at[m, mine], o_send.at[m, k], b_recv.at[m, k], over[k])
-
-    def own_tokens(m):
-        return pltpu.make_async_copy(tokens.at[m, 0], xall.at[m, mine], b_recv.at[m, 0])
-
-    def pieces(cc, ww):
-        r = pl.ds(pl.multiple_of(ww * part + cc * half, 16), half)
-        f = pl.ds(pl.multiple_of(ww * ffp + cc * ffh, 16), ffh)
-        return [attn.at[0:3, r], attn.at[3:4, r], up.at[r], down.at[f]]
-
-    sr = pl.ds(pl.multiple_of(core * half, 16), half)
-    sf = pl.ds(pl.multiple_of(core * ffh, 16), ffh)
-    sources = [attn_w.at[0, 0:3, sr], attn_w.at[0, 3:4, sr], up_w.at[0, sr], down_w.at[0, sf]]
+    def cut(base, ww, stride, rows, cc, zp, shared):
+        share = rows // 4 if shared else rows // 2
+        at = base + ww * stride + ((cc * 2 + zp) if shared else cc) * share
+        return pl.ds(pl.multiple_of(at, 16), share)
+
+    def piece(p, ww, cc, zp, local):
+        stride = 0 if local else 1
+        if p < 4:
+            r = cut(0, ww, part * stride, part, cc, zp, False)
+            matrix = (1, 2, 0, 3)[p]
+            return attn_w.at[0, matrix, r] if local else attn.at[matrix, r]
+        if p < 6:
+            r = cut(0, ww, part * stride, part, cc, zp, True)
+            cols = pl.ds((p - 4) * (FF // 2), FF // 2)
+            return up_w.at[0, r, cols] if local else up.at[r, cols]
+        base = (p - 6) * (ffp // 2)
+        r = cut(base, ww, ffp * stride, ffp // 2, cc, zp, p == 6)
+        return down_w.at[0, r] if local else down.at[r]
+
+    shared = [p in (4, 5, 6) for p in range(8)]
 
     def weight_push(k, p):
         return push(
-            sources[p], pieces(core, w)[p], w_send.at[k - 1, p], w_recv.at[k - 1, p], xs[k - 1]
+            piece(p, w, core, par, True),
+            piece(p, w, core, par, False),
+            w_send.at[k - 1, p],
+            w_recv.at[k - 1, p],
+            xs[k - 1],
         )
 
-    def weight_forward(k, p):
-        spot = pieces(core, lax.rem(w + W - k, W))[p]
-        return push(spot, spot, wf_send.at[k - 1, p], wf_recv.at[k - 1, p], partner)
+    def weight_forward(k, p, way):
+        zp = 1 - par if way == 2 else par
+        spot = piece(p, lax.rem(w + W - k, W), core, zp, False)
+        peer = buddy if way == 1 else partner
+        return push(spot, spot, wf_send.at[k - 1, p, way], wf_recv.at[k - 1, p, way], peer)
+
+    def x_start(p):
+        for k in range(1, W):
+            weight_push(k, p).start()
+
+    def x_arrive(p):
+        for k in range(1, W):
+            weight_push(k, p).wait_recv()
+            weight_forward(k, p, 0).start()
+            if shared[p]:
+                weight_forward(k, p, 1).start()
+
+    def z_arrive(p):
+        for k in range(1, W):
+            weight_forward(k, p, 1).wait_recv()
+            weight_forward(k, p, 2).start()
+
+    def core_arrive(p):
+        for k in range(1, W):
+            weight_forward(k, p, 0).wait_recv()
+            if shared[p]:
+                weight_forward(k, p, 2).wait_recv()
 
     def small_push(k):
         return push(small_in, small_all.at[k], s_send.at[k - 1], s_recv.at[k - 1], xs[k - 1])
@@ -194,40 +267,35 @@
     own_r = pl.ds(pl.multiple_of(w * part, 16), part)
     own_f = pl.ds(pl.multiple_of(w * ffp, 16), ffp)
     own_loads = [
-        pltpu.make_async_copy(attn_w.at[0, 0:3], attn.at[0:3, own_r], load_sem.at[0]),
-        pltpu.make_async_copy(attn_w.at[0, 3:4], attn.at[3:4, own_r], load_sem.at[1]),
-        pltpu.make_async_copy(up_w.at[0], up.at[own_r], load_sem.at[2]),
-        pltpu.make_async_copy(down_w.at[0], down.at[own_f], load_sem.at[3]),
+        pltpu.make_async_copy(attn_w.at[0], attn.at[:, own_r], load_sem.at[0]),
+        pltpu.make_async_copy(up_w.at[0], up.at[own_r], load_sem.at[1]),
+        pltpu.make_async_copy(down_w.at[0], down.at[own_f], load_sem.at[2]),
     ]
 
     @pl.when(s == 0)
     def _():
-        own_tokens(0).start()
         for k in range(1, nz):
             token_push(0, k).start()
-
-    for p in range(4):
-        own_loads[p].start()
+        for m in range(MB):
+            own_tokens(m).start()
+
+    @pl.when(s == 1)
+    def _():
+        for m in range(1, MB):
+            for k in range(1, nz):
+                token_push(m, k).start()
+
+    x_start(0)
+    x_start(1)
     for k in range(1, W):
         small_push(k).start()
-    for p in range(4):
-        for k in range(1, W):
-            weight_push(k, p).start()
-
-    @pl.when(s == 0)
-    def _():
-        for m in range(1, MB):
-            own_tokens(m).start()
-            for k in range(1, nz):
-                token_push(m, k).start()
-
-    def weights_ready(p):
-        for k in range(1, W):
-            weight_push(k, p).wait_recv()
-            weight_forward(k, p).start()
-        own_loads[p].wait()
-        for k in range(1, W):
-            weight_forward(k, p).wait_recv()
+    for copy in own_loads:
+        copy.start()
+
+    def relay_start(m):
+        out_relay(m).wait_recv()
+        for k in range(1, nz):
+            relay_push(m, k).start()
 
     def rows_ready(m):
         @pl.when(s == 0)
@@ -236,11 +304,20 @@
 
         @pl.when(s == 1)
         def _():
-            block_arrival(m, 0).wait_recv()
+            out_arrival(m, 0).wait_recv()
 
         forward_push(m, 0).start()
         for k in range(1, nz):
-            block_arrival(m, k).wait_recv()
+
+            @pl.when(s == 0)
+            def _():
+                token_arrival(m, k).wait_recv()
+
+            @pl.when(s == 1)
+            def _():
+                out_arrival(m, k).wait_recv()
+                relay_arrival(m, k).wait_recv()
+
             forward_push(m, k).start()
         for k in range(nz):
             forward_push(m, k).wait_recv()
@@ -260,19 +337,51 @@
 
     slots = kv.shape[0]
 
+    @pl.when(s == 1)
+    def _():
+        for p in range(8):
+            x_arrive(p)
+            if p + 2 < 8:
+                x_start(p + 2)
+            if p and shared[p - 1]:
+                z_arrive(p - 1)
+        for p in range(8):
+            core_arrive(p)
+        relay_start(0)
+
+    @pl.when(s == 0)
+    def _():
+        for p in range(3):
+            x_arrive(p)
+            x_start(p + 2)
+        x_start(5)
+
+    for k in range(1, W):
+        small_push(k).wait_recv()
+    total = small_in[...]
+    for k in range(1, W):
+        total = total + small_all[k]
+    small[...] = total
+    save(small, small_o)
+    own_loads[0].wait()
+    bias_v = small[0:1, :]
+
     for m in range(MB):
         rows_ready(m)
+        if m + 1 < MB:
+
+            @pl.when(s == 1)
+            def _():
+                relay_start(m + 1)
+
         if m == 0:
-            weights_ready(0)
-            for k in range(1, W):
-                small_push(k).wait_recv()
-            total = small_in[...]
-            for k in range(1, W):
-                total = total + small_all[k]
-            small[...] = total
-            save(small, small_o)
+
+            @pl.when(s == 0)
+            def _():
+                for p in range(3):
+                    core_arrive(p)
+
         save(xall.at[m], xall_o.at[m])
-        bias_v = small[0:1, :]
 
         def project(i, _):
             r = pl.ds(pl.multiple_of(i * 256, 256), 256)
@@ -323,21 +432,52 @@
         save(lse.at[m], lse_o.at[m])
         save(mix.at[m], mix_o.at[m])
         save(att.at[m], att_o.at[m])
+        if m < 2:
+
+            @pl.when(s == 0)
+            def _():
+                if m == 0:
+                    x_arrive(3)
+                x_start(6 + m)
+
+    if MB == 1:
+
+        @pl.when(s == 0)
+        def _():
+            x_start(7)
 
     top[...] = jnp.broadcast_to(tops, (8, 128))
     save(top, top_o)
-    for p in range(1, 4):
-        weights_ready(p)
+
+    @pl.when(s == 0)
+    def _():
+        core_arrive(3)
+
+    for m in range(MB):
+        branch = dot(att[m], attn[3]) + small[1:2, :]
+        first[m] = xall[m, mine, :].astype(f32) + branch
+        save(first.at[m], first_o.at[m])
     save(attn, attn_o)
+
+    @pl.when(s == 0)
+    def _():
+        x_arrive(4)
+        x_arrive(5)
+        z_arrive(4)
+        x_arrive(6)
+        z_arrive(5)
+        x_arrive(7)
+        z_arrive(6)
+        for p in range(4, 8):
+            core_arrive(p)
+
+    for copy in own_loads[1:]:
+        copy.wait()
     save(up, up_o)
     save(down, down_o)
 
     for m in range(MB):
-        branch = dot(att[m], attn[3]) + small[1:2, :]
-        first_sum = xall[m, mine, :].astype(f32) + branch
-        first[m] = first_sum
-        save(first.at[m], first_o.at[m])
-        hat, _ = norm_parts(first_sum)
+        hat, _ = norm_parts(first[m])
         normed = hat * small[5:6, :] + small[3:4, :]
         low = normed.astype(bf16)
         second[m] = normed + small[2:3, :]
@@ -346,56 +486,403 @@
             pre = dot(low, up[:, cols]) + small[7 + j : 8 + j, :]
             hidden[m, :, cols] = pre
             second[m] += dot(gelu(pre).astype(bf16), down[cols, :])
+        hat, _ = norm_parts(second[m])
+        out[m] = (hat * small[6:7, :] + small[4:5, :]).astype(bf16)
+
         save(hidden.at[m], hidden_o.at[m])
         save(second.at[m], second_o.at[m])
-        hat, _ = norm_parts(second[m])
-        out[m] = (hat * small[6:7, :] + small[4:5, :]).astype(bf16)
+        save(out.at[m], out_o.at[0, m, 0])
 
         @pl.when(s == 0)
         def _():
+            if m:
+                for k in range(nz):
+                    out_push(m - 1, k).wait_send()
+            out_relay(m).start()
+            out_relay(m).wait_send()
             for k in range(nz):
                 out_push(m, k).start()
 
-        save(out.at[m], out_o.at[0, m, 0])
 
     for k in range(1, W):
         small_push(k).wait_send()
-        for p in range(4):
+        for p in range(8):
             weight_push(k, p).wait_send()
-            weight_forward(k, p).wait_send()
+            for way in range(3 if shared[p] else 1):
+                weight_forward(k, p, way).wait_send()
     for m in range(MB):
         for k in range(nz):
             forward_push(m, k).wait_send()
 
-        @pl.when(s == 0)
+        if m == MB - 1:
+
+            @pl.when(s == 0)
+            def _():
+                for k in range(nz):
+                    out_push(m, k).wait_send()
+
+        @pl.when(s == 1)
+        def _():
+            for k in range(1, nz):
+                relay_push(m, k).wait_send()
+
+        @pl.when(s == (0 if m == 0 else 1))
         def _():
             for k in range(1, nz):
                 token_push(m, k).wait_send()
-            for k in range(nz):
-                out_push(m, k).wait_send()
 
     for copy in saves:
         copy.wait()
 
 
-def backward_kernel(
-    nz, W, MB, T,
-    lens, cot, counts_q, counts_k, xall_h, kv_h, q_h, mix_h, lse_h, first_h, second_h, hidden_h, top,
-    attn_h, up_h, down_h, small,
-    grad_in_o, rows_qkv, rows_branch, rows_normed, rows_hidden, rows_gated, rows_down, small_o, top_o,
-    attn, up, down, xall, kv, q, mix, lse, first, second, hidden, dout,
-    gfirst, gbranch, gall, aux, kvp, wide_q, wide_k, lse_all, del_all, del_c, dqkv, gnorm, ghid, gated,
-    gdown, small_g, gin, top_x,
-    load_sem, y_send, y_recv, b_send, b_recv, f_send, f_recv, a_send, a_recv, af_send, af_recv,
-    t_send, t_recv, kvp_sem, save_sem,
-):
+def sum_steps(r, nz, W, count, per):
+    s, c, w = place()
+    z, core = c // 2, lax.rem(c, 2)
+    part = D // W
+    root = (nz - 1) // 2
+    partner = {"ctx": c + 1 - 2 * core}
+    xs = [{"wsh": lax.rem(w + k, W)} for k in range(1, W)]
+    grads, from_x, chain, sums = r.grads, r.from_x, r.chain, r.sums
+
+    def spot(i, ww):
+        at = (i // per) * D + ww * part + lax.rem(i, per) * ROWS
+        return pl.ds(pl.multiple_of(at, 16), ROWS)
+
+    def lines(i):
+        return pl.ds(pl.multiple_of(i * ROWS, 16), ROWS)
+
+    def x_push(i, k):
+        return push(
+            grads.at[spot(i, lax.rem(w + k, W))],
+            from_x.at[k - 1, lines(i)],
+            r.x_send.at[k - 1, i],
+            r.x_recv.at[k - 1, i],
+            xs[k - 1],
+        )
+
+    is_left = z < root
+    to_left = {"ctx": jnp.maximum(z - 1, 0) * 2 + core}
+    to_right = {"ctx": jnp.minimum(z + 1, nz - 1) * 2 + core}
+    far = max(root, nz - 1 - root)
+    depth = jnp.where(z == root, far, jnp.where(is_left, z, nz - 1 - z))
+    away = jnp.where(is_left, root - z, z - root)
+
+    def chain_push(i, side, peer):
+        block = grads.at[spot(i, w)]
+        return push(block, chain.at[side, lines(i)], r.ch_send.at[i], r.ch_recv.at[side, i], peer)
+
+    def total_push(i, side, peer, block):
+        return push(block, sums.at[core, lines(i)], r.t_send.at[side, i], r.t_recv.at[i], peer)
+
+    def partner_push(i, block):
+        return push(block, sums.at[core, lines(i)], r.p_send.at[i], r.p_recv.at[i], partner)
+
+    def partner_arrival(i):
+        block = sums.at[1 - core, lines(i)]
+        return push(block, block, r.p_send.at[i], r.p_recv.at[i], partner)
+
+    def own_copy(i):
+        return pltpu.make_async_copy(grads.at[spot(i, w)], sums.at[core, lines(i)], r.o_sem.at[i])
+
+    def begin():
+        for i in range(FLIGHT):
+            for k in range(1, W):
+                x_push(i, k).start()
+
+    def step(t):
+        @pl.when(t + FLIGHT < count)
+        def _():
+            for k in range(1, W):
+                x_push(t, k).wait_send()
+                x_push(t + FLIGHT, k).start()
+
+        i = t - LAG * depth
+
+        @pl.when((i >= 0) & (i < count))
+        def _():
+            acc = grads[spot(i, w), :].astype(f32)
+            for k in range(1, W):
+                x_push(i, k).wait_recv()
+                acc = acc + from_x[k - 1, lines(i), :].astype(f32)
+            grads[spot(i, w), :] = acc.astype(bf16)
+
+            @pl.when((z > 0) & (z <= root))
+            def _():
+                chain_push(i, 0, to_right).wait_recv()
+                both = grads[spot(i, w), :].astype(f32) + chain[0, lines(i), :].astype(f32)
+                grads[spot(i, w), :] = both.astype(bf16)
+
+            @pl.when((z < nz - 1) & (z >= root))
+            def _():
+                chain_push(i, 1, to_left).wait_recv()
+                both = grads[spot(i, w), :].astype(f32) + chain[1, lines(i), :].astype(f32)
+                grads[spot(i, w), :] = both.astype(bf16)
+
+            @pl.when(z < root)
+            def _():
+                chain_push(i, 0, to_right).start()
+
+            @pl.when(z > root)
+            def _():
+                chain_push(i, 1, to_left).start()
+
+            @pl.when(z == root)
+            def _():
+                block = grads.at[spot(i, w)]
+                if root > 0:
+                    total_push(i, 0, to_left, block).start()
+                if root < nz - 1:
+                    total_push(i, 1, to_right, block).start()
+                partner_push(i, block).start()
+                own_copy(i).start()
+
+        b = t - LAG * (far + away)
+
+        @pl.when((b >= 0) & (b < count) & (z != root))
+        def _():
+            block = sums.at[core, lines(b)]
+            total_push(b, 0, to_left, block).wait_recv()
+
+            @pl.when((z < root) & (z > 0))
+            def _():
+                total_push(b, 0, to_left, block).start()
+
+            @pl.when((z > root) & (z < nz - 1))
+            def _():
+                total_push(b, 1, to_right, block).start()
+
+            partner_push(b, block).start()
+
+    last = count + LAG * 2 * far
+
+    def drain():
+        def one(i, _):
+            block = sums.at[core, lines(i)]
+            partner_arrival(i).wait_recv()
+            partner_push(i, block).wait_send()
+
+            @pl.when(i + FLIGHT >= count)
+            def _():
+                for k in range(1, W):
+                    x_push(i, k).wait_send()
+
+            @pl.when(z != root)
+            def _():
+                chain_push(i, 0, to_right).wait_send()
+
+            @pl.when(z == root)
+            def _():
+                own_copy(i).wait()
+
+            @pl.when((z <= root) & (z > 0))
+            def _():
+                total_push(i, 0, to_left, block).wait_send()
+
+            @pl.when((z >= root) & (z < nz - 1))
+            def _():
+                total_push(i, 1, to_right, block).wait_send()
+
+            return 0
+
+        lax.fori_loop(0, count, one, 0)
+
+    return begin, step, last, drain
+
+
+def small_steps(r, nz, W):
+    s, c, w = place()
+    z, core = c // 2, lax.rem(c, 2)
+    partner = {"ctx": c + 1 - 2 * core}
+    xs = [{"wsh": lax.rem(w + k, W)} for k in range(1, W)]
+    zs = [{"ctx": lax.rem(z + k, nz) * 2 + core} for k in range(1, nz)]
+
+    def core_push(e):
+        return push(r.core_s.at[e], r.core_s.at[e], r.sc_send, r.sc_recv, partner)
+
+    def x_push(k, e):
+        return push(
+            r.wsh_s.at[e], r.wsh_s.at[e], r.sx_send.at[k - 1], r.sx_recv.at[k - 1], xs[k - 1]
+        )
+
+    def z_push(k, e):
+        return push(r.z_s.at[e], r.z_s.at[e], r.sz_send.at[k - 1], r.sz_recv.at[k - 1], zs[k - 1])
+
+    def first(value):
+        r.core_s[core] = value
+        core_push(core).start()
+
+    def second():
+        core_push(1 - core).wait_recv()
+        r.wsh_s[w] = r.core_s[0] + r.core_s[1]
+        for k in range(1, W):
+            x_push(k, w).start()
+
+    def third():
+        for k in range(1, W):
+            x_push(k, lax.rem(w + W - k, W)).wait_recv()
+        total = r.wsh_s[0]
+        for e in range(1, W):
+            total = total + r.wsh_s[e]
+        r.z_s[z] = total
+        for k in range(1, nz):
+            z_push(k, z).start()
+
+    def finish():
+        for k in range(1, nz):
+            z_push(k, lax.rem(z + nz - k, nz)).wait_recv()
+        total = r.z_s[0]
+        for e in range(1, nz):
+            total = total + r.z_s[e]
+        r.small_o[...] = total
+        core_push(core).wait_send()
+        for k in range(1, W):
+            x_push(k, w).wait_send()
+        for k in range(1, nz):
+            z_push(k, z).wait_send()
+
+    return first, second, third, finish
+
+
+def clip_weights(r, tops, own):
+    factor = jnp.sqrt(clip_limit / jnp.maximum(tops, clip_limit))
+    lane = lax.broadcasted_iota(jnp.int32, (128, D), 1)
+    head = lax.broadcasted_iota(jnp.int32, (128, D), 0)
+    heads = jnp.where(lax.shift_right_logical(lane, 6) == head, 1.0, 0.0).astype(f32)
+    wide = jnp.dot(factor, heads, preferred_element_type=f32, precision=exact_dot)[0:1]
+    for p in range(2):
+        r.clip_o[0, p] = (own(p).astype(f32) * wide).astype(bf16)
+
+
+def down_tiles(r, W):
+    part, gate_half = D // W, FF // W // 2
+    for e in range(W):
+        cols = slice(e * gate_half, (e + 1) * gate_half)
+        block = dot_0(r.lg[:, cols], r.rd[...]).astype(bf16)
+        for j in range(2):
+            at = j * D + e * part
+            r.grads[at : at + part] = block[j * part : (j + 1) * part]
+
+
+def up_tiles(r):
+    for j in range(2):
+        block = dot_0(r.ln[...], r.rh[:, j * D : (j + 1) * D])
+        r.grads[(2 + j) * D : (3 + j) * D] = block.astype(bf16)
+
+
+def attn_tiles(r):
+    for j, (left, right) in enumerate(((r.la, r.ra), (r.lb, r.rb))):
+        r.grads[(4 + j) * D : (5 + j) * D] = dot_0(left[...], right[...]).astype(bf16)
+
+
+def ff_operands(W, cc, gated, down, normed, hidden, r):
+    ffp = FF // W
+    found = []
+    for e in range(W):
+        cols = pl.ds(pl.multiple_of(e * ffp + cc * (ffp // 2), 128), ffp // 2)
+        found.append((gated.at[:, cols], r.lg, e * (ffp // 2), ffp // 2))
+    cols = pl.ds(pl.multiple_of(cc * (FF // 2), 128), FF // 2)
+    return found + [(down, r.rd, 0, D), (normed, r.ln, 0, D), (hidden.at[:, cols], r.rh, 0, FF // 2)]
+
+
+def attn_operands(cc, qkv, att, branch, x, r):
+    if cc == 0:
+        return [(x, r.la), (qkv.at[:, 0:D], r.ra), (x, r.lb), (qkv.at[:, D : 2 * D], r.rb)]
+    return [(x, r.la), (qkv.at[:, 2 * D : 3 * D], r.ra), (att, r.lb), (branch, r.rb)]
+
+
+def reduce_kernel(nz, W, MB, r):
+    s, c, w = place()
+    z, core = c // 2, lax.rem(c, 2)
+    part = D // W
+    per = part // ROWS
+    partner = {"ctx": c + 1 - 2 * core}
+    xs = [{"wsh": lax.rem(w + k, W)} for k in range(1, W)]
+    zs = [{"ctx": lax.rem(z + k, nz) * 2 + core} for k in range(1, nz)]
+    greet(xs + zs + [partner])
+    begin, step, last, drain = sum_steps(r, nz, W, 6 * per, per)
+    small_first, small_second, small_third, small_finish = small_steps(r, nz, W)
+    mine = pl.ds(pl.multiple_of(c * TD, TD), TD)
+
+    def copies(m, cc, far):
+        n = W + 3
+        found = []
+        rows = (r.gated_h.at[m], r.down_h.at[m], r.normed_h.at[m], r.hidden_h.at[m])
+        side = (MB + m if far else m) * TD
+        for e, (src, dst, at, width) in enumerate(ff_operands(W, cc, *rows, r)):
+            spot = dst.at[side : side + TD, at : at + width]
+            found.append((src, spot, m * (n + 4) + e))
+        rows = (r.qkv_h.at[m], r.att_h.at[m], r.branch_h.at[m], r.x_h.at[m, mine])
+        for e, (src, dst) in enumerate(attn_operands(cc, *rows, r)):
+            found.append((src, dst.at[side : side + TD], m * (n + 4) + n + e))
+        if far:
+            return [push(a, b, r.c_send.at[e], r.c_recv.at[e], partner) for a, b, e in found]
+        return [pltpu.make_async_copy(a, b, r.load_sem.at[e]) for a, b, e in found]
+
+    own_load = pltpu.make_async_copy(r.attn_w.at[0, 0:2], r.own_w, r.own_sem)
+    own_load.start()
+    small_first(r.small_g[...])
+    for cc in range(2):
+
+        @pl.when(core == cc)
+        def _():
+            for m in range(MB):
+                for copy in copies(m, 1 - cc, True) + copies(m, cc, False):
+                    copy.start()
+            for m in range(MB):
+                for copy in copies(m, cc, False):
+                    copy.wait()
+                for copy in copies(m, cc, True):
+                    copy.wait_recv()
+
+    down_tiles(r, W)
+    begin()
+    up_tiles(r)
+    attn_tiles(r)
+    small_second()
+    own_load.wait()
+    clip_weights(r, r.tops[...], lambda p: r.own_w[p])
+    small_third()
+
+    def loop(t, _):
+        step(t)
+        return 0
+
+    lax.fori_loop(0, last, loop, 0)
+    small_finish()
+    for cc in range(2):
+
+        @pl.when(core == cc)
+        def _():
+            for m in range(MB):
+                for copy in copies(m, 1 - cc, True):
+                    copy.wait_send()
+
+    drain()
+
+
+def backward_kernel(nz, W, MB, T, fused, r):
+    lens, cot, counts_q, counts_k, top, small = (
+        r.lens, r.cot, r.counts_q, r.counts_k, r.top, r.small,
+    )
+    attn, up, down, xall, kv, q, mix, lse = r.attn, r.up, r.down, r.xall, r.kv, r.q, r.mix, r.lse
+    first, second, hidden, dout, gfirst = r.first, r.second, r.hidden, r.dout, r.gfirst
+    gbranch, gall, relay, aux, kvp = r.gbranch, r.gall, r.relay, r.aux, r.kvp
+    wide_q, wide_k, lse_all, del_all, del_c = r.wide_q, r.wide_k, r.lse_all, r.del_all, r.del_c
+    dqkv, gnorm, ghid, gated, gdown = r.dqkv, r.gnorm, r.ghid, r.gated, r.gdown
+    small_g, gin, top_x = r.small_g, r.gin, r.top_x
     s, c, w = place()
     z, core = c // 2, lax.rem(c, 2)
     partner = {"ctx": c + 1 - 2 * core}
     xs = [{"wsh": lax.rem(w + k, W)} for k in range(1, W)]
     zs = [{"ctx": lax.rem(z + k, nz) * 2 + core} for k in range(1, nz)]
     across = {"section": 1 - s}
-    greet(xs + zs + [across, partner])
+    over = [{"section": 1 - s, "ctx": lax.rem(z + k, nz) * 2 + core} for k in range(1, nz)]
+    greet(xs + zs + over + [across, partner])
+    part = D // W
+    per = part // ROWS
+    if fused:
+        begin, step, last, drain = sum_steps(r, nz, W, 6 * per, per)
+        small_first, small_second, small_third, small_finish = small_steps(r, nz, W)
 
     def rows_of(zz, cc):
         return pl.ds(pl.multiple_of((zz * 2 + cc) * TD, TD), TD)
@@ -404,74 +891,169 @@
     loads = []
 
     def load(src, dst):
-        copy = pltpu.make_async_copy(src, dst, load_sem.at[len(loads)])
+        copy = pltpu.make_async_copy(src, dst, r.load_sem.at[len(loads)])
         copy.start()
         loads.append(copy)
         return copy
 
     saves = []
+    numbers = iter(range(100))
 
     def save(src, dst):
-        copy = pltpu.make_async_copy(src, dst, save_sem.at[next(numbers)])
+        copy = pltpu.make_async_copy(src, dst, r.save_sem.at[next(numbers)])
         copy.start()
         saves.append(copy)
 
-    numbers = iter(range(100))
-
     def cot_load(m):
-        return pltpu.make_async_copy(cot.at[m, 0], dout.at[m], y_recv.at[m])
+        return pltpu.make_async_copy(cot.at[m, 0], dout.at[m], r.y_recv.at[m])
 
     def grad_push(m):
-        return push(gin.at[m], dout.at[m], y_send.at[m], y_recv.at[m], across)
+        return push(gin.at[m], dout.at[m], r.y_send.at[m], r.y_recv.at[m], across)
 
     @pl.when(s == 1)
     def _():
         for m in range(MB):
             cot_load(m).start()
 
-    load_second = [load(second_h.at[m], second.at[m]) for m in range(MB)]
-    load_down = load(down_h, down)
     slots = xall.shape[0]
-    load_hidden = [load(hidden_h.at[m], hidden.at[m]) for m in range(slots)]
-    load_up = load(up_h, up)
-    load_first = [load(first_h.at[m], first.at[m]) for m in range(MB)]
-    load_mix = [load(mix_h.at[m], mix.at[m]) for m in range(MB)]
-    load_attn = load(attn_h, attn)
-    load_lse = [load(lse_h.at[m], lse.at[m]) for m in range(MB)]
-    load_x = [load(xall_h.at[m], xall.at[m]) for m in range(slots)]
-    load_kv = [load(kv_h.at[m, mine], kv.at[m]) for m in range(MB)]
-    load_q = [load(q_h.at[m], q.at[m]) for m in range(MB)]
+    load_second = [load(r.second_h.at[m], second.at[m]) for m in range(MB)]
+    cuts = [slice(j * CHUNK, (j + 1) * CHUNK) for j in range(NCH)]
+    load_hidden, load_down, load_up = [[]], [], []
+    for cut in cuts:
+        load_hidden[0].append(load(r.hidden_h.at[0, :, cut], hidden.at[0, :, cut]))
+        load_down.append(load(r.down_h.at[cut], down.at[cut]))
+        load_up.append(load(r.up_h.at[:, cut], up.at[:, cut]))
+    late = {}
+
+    def load_rest():
+        late["first"] = [load(r.first_h.at[m], first.at[m]) for m in range(MB)]
+        late["attn"] = load(r.attn_h, attn)
+        late["mix"] = [load(r.mix_h.at[m], mix.at[m]) for m in range(MB)]
+        late["lse"] = [load(r.lse_h.at[m], lse.at[m]) for m in range(MB)]
+        for m in range(1, slots):
+            load_hidden.append([load(r.hidden_h.at[m], hidden.at[m])])
+        late["x"] = [load(r.xall_h.at[m], xall.at[m]) for m in range(slots)]
+        late["kv"] = [load(r.kv_h.at[m, mine], kv.at[m]) for m in range(MB)]
+        late["q"] = [load(r.q_h.at[m], q.at[m]) for m in range(MB)]
+
+    def cut_rows(zz, cc, side):
+        return pl.ds(pl.multiple_of((zz * 2 + cc) * TD + side * BLK, BLK), BLK)
 
     def rows_push(m, k):
-        block = gall.at[m, mine]
-        peer = partner if k == 0 else zs[k - 1]
-        send, recv = (f_send, f_recv) if k == 0 else (b_send, b_recv)
-        return push(block, block, send.at[m, k], recv.at[m, k], peer)
+        if k == 0:
+            block = gall.at[m, mine]
+            return push(block, block, r.f_send.at[m, 0], r.f_recv.at[m, 0], partner)
+        block = gall.at[m, cut_rows(z, core, 0)]
+        return push(block, block, r.b_send.at[m, k], r.b_recv.at[m, k], zs[k - 1])
 
     def rows_arrival(m, k):
-        block = gall.at[m, rows_of(lax.rem(z + nz - k, nz), core)]
-        return push(block, block, b_send.at[m, k], b_recv.at[m, k], partner)
+        block = gall.at[m, cut_rows(lax.rem(z + nz - k, nz), core, 0)]
+        return push(block, block, r.b_send.at[m, k], r.b_recv.at[m, k], partner)
+
+    def relay_out(m):
+        block = gall.at[m, cut_rows(z, core, 1)]
+        return push(block, relay.at[m], r.r_send.at[m, 0], r.r_recv.at[m, 0], across)
+
+    def relay_push(m, k):
+        block = gall.at[m, cut_rows(z, core, 1)]
+        return push(relay.at[m], block, r.r_send.at[m, k], r.r_recv.at[m, k], over[k - 1])
+
+    def relay_arrival(m, k):
+        block = gall.at[m, cut_rows(lax.rem(z + nz - k, nz), core, 1)]
+        return push(block, block, r.r_send.at[m, k], r.r_recv.at[m, k], partner)
 
     def rows_forward(m, k):
         block = gall.at[m, rows_of(lax.rem(z + nz - k, nz), core)]
-        return push(block, block, f_send.at[m, k], f_recv.at[m, k], partner)
+        return push(block, block, r.f_send.at[m, k], r.f_recv.at[m, k], partner)
 
     def aux_push(m, k):
         block = aux.at[m, c]
         peer = partner if k == 0 else zs[k - 1]
-        send, recv = (af_send, af_recv) if k == 0 else (a_send, a_recv)
+        send, recv = (r.af_send, r.af_recv) if k == 0 else (r.a_send, r.a_recv)
         return push(block, block, send.at[m, k], recv.at[m, k], peer)
 
     def aux_arrival(m, k):
         block = aux.at[m, lax.rem(z + nz - k, nz) * 2 + core]
-        return push(block, block, a_send.at[m, k], a_recv.at[m, k], partner)
+        return push(block, block, r.a_send.at[m, k], r.a_recv.at[m, k], partner)
 
     def aux_forward(m, k):
         block = aux.at[m, lax.rem(z + nz - k, nz) * 2 + core]
-        return push(block, block, af_send.at[m, k], af_recv.at[m, k], partner)
+        return push(block, block, r.af_send.at[m, k], r.af_recv.at[m, k], partner)
 
     def top_push(k):
-        return push(top_x.at[0], top_x.at[k], t_send.at[k - 1], t_recv.at[k - 1], xs[k - 1])
+        return push(top_x.at[0], top_x.at[k], r.tp_send.at[k - 1], r.tp_recv.at[k - 1], xs[k - 1])
+
+    def spread_start(m):
+        relay_out(m).start()
+        for k in range(nz):
+            aux_push(m, k).start()
+            rows_push(m, k).start()
+
+    def spread_sent(m):
+        relay_out(m).wait_send()
+        for k in range(1, nz):
+            rows_push(m, k).wait_send()
+
+    def relay_one(m):
+        relay_out(m).wait_recv()
+        for k in range(1, nz):
+            relay_push(m, k).start()
+
+    def rows_copies(m, cc, far, late):
+        side = (MB + m if far else m) * TD
+        found = []
+        if late:
+            rows = (dqkv.at[m], r.att_h.at[m], gbranch.at[m], r.xall_h.at[m, mine])
+            for e, (src, dst) in enumerate(attn_operands(cc, *rows, r)):
+                found.append((src, dst.at[side : side + TD], m * (W + 7) + W + 3 + e))
+        else:
+            rows = (gated.at[m], gdown.at[m], gnorm.at[m], ghid.at[m])
+            for e, (src, dst, at, width) in enumerate(ff_operands(W, cc, *rows, r)):
+                found.append((src, dst.at[side : side + TD, at : at + width], m * (W + 7) + e))
+        if far:
+            return [push(a, b, r.c_send.at[e], r.c_recv.at[e], partner) for a, b, e in found]
+        return [pltpu.make_async_copy(a, b, r.c_load.at[e]) for a, b, e in found]
+
+    def rows_start(m, late):
+        for cc in range(2):
+
+            @pl.when(core == cc)
+            def _():
+                for copy in rows_copies(m, 1 - cc, True, late) + rows_copies(m, cc, False, late):
+                    copy.start()
+
+    def rows_here(late, picked):
+        for cc in range(2):
+
+            @pl.when(core == cc)
+            def _():
+                for m in range(MB):
+                    for copy in rows_copies(m, cc, False, late)[picked]:
+                        copy.wait()
+                    for copy in rows_copies(m, cc, True, late)[picked]:
+                        copy.wait_recv()
+
+    def ff_gradients():
+        rows_here(False, slice(0, W + 1))
+        down_tiles(r, W)
+        begin()
+        rows_here(False, slice(W + 1, None))
+        up_tiles(r)
+
+    def rows_sent():
+        for cc in range(2):
+
+            @pl.when(core == cc)
+            def _():
+                for m in range(MB):
+                    for late in (False, True):
+                        for copy in rows_copies(m, 1 - cc, True, late):
+                            copy.wait_send()
+
+    @pl.when(s == 0)
+    def _():
+        for m in range(MB):
+            relay_one(m)
 
     heads = lax.broadcasted_iota(jnp.int32, (D, 128), 0)
     heads = lax.shift_right_logical(heads, 6) == lax.broadcasted_iota(jnp.int32, (D, 128), 1)
@@ -480,8 +1062,6 @@
 
     for m in range(MB):
         load_second[m].wait()
-        if m == 0:
-            load_down.wait()
 
         @pl.when(s == 1)
         def _():
@@ -498,74 +1078,106 @@
         grad_second = norm_back(grad_out, hat, rstd, small[6:7, :])
         low_second = grad_second.astype(bf16)
         gdown[m] = low_second
-        save(gdown.at[m], rows_down.at[m])
+        if not fused:
+            save(gdown.at[m], r.rows_down.at[m])
         small_g[4:5, :] += column_sum(low_second.astype(f32))
         if m >= slots:
-            load_hidden.append(load(hidden_h.at[m], hidden.at[m % slots]))
+            load_hidden.append([load(r.hidden_h.at[m], hidden.at[m % slots])])
             for copy in hidden_saves:
                 saves[:] = [x for x in saves if x is not copy]
                 copy.wait()
-        load_hidden[m].wait()
-        if m == 0:
-            load_up.wait()
+        if m:
+            load_hidden[m][0].wait()
         gfirst[m] = grad_second
         for j in range(NCH):
             cols = slice(j * CHUNK, (j + 1) * CHUNK)
+            if m == 0:
+                load_hidden[0][j].wait()
+                load_down[j].wait()
+                if j == NCH - 1:
+                    load_rest()
             value, slope = gelu_both(hidden[m % slots, :, cols])
             gated[m % slots, :, cols] = value.astype(bf16)
             grad_hidden = (slope * dot_t(low_second, down[cols, :])).astype(bf16)
             ghid[m % slots, :, cols] = grad_hidden
             small_g[7 + j : 8 + j, :] += column_sum(grad_hidden.astype(f32))
+            if m == 0:
+                load_up[j].wait()
             gfirst[m] += dot_t(grad_hidden, up[:, cols])
-        save(gated.at[m % slots], rows_gated.at[m])
-        save(ghid.at[m % slots], rows_hidden.at[m])
-        hidden_saves = saves[-2:]
+        if not fused:
+            save(gated.at[m % slots], r.rows_gated.at[m])
+            save(ghid.at[m % slots], r.rows_hidden.at[m])
+            hidden_saves = saves[-2:]
         grad_normed = gfirst[m]
-        load_first[m].wait()
+        late["first"][m].wait()
         hat, rstd = norm_parts(first[m])
         gnorm[m] = (hat * small[5:6, :] + small[3:4, :]).astype(bf16)
-        save(gnorm.at[m], rows_normed.at[m])
         small_g[0:1, :] += column_sum(grad_normed * hat)
         small_g[5:6, :] += column_sum(grad_normed)
         grad_first = norm_back(grad_normed, hat, rstd, small[5:6, :])
         gfirst[m] = grad_first
         low_first = grad_first.astype(bf16)
         gbranch[m] = low_first
-        save(gbranch.at[m], rows_branch.at[m])
+        if not fused:
+            save(gnorm.at[m], r.rows_normed.at[m])
+            save(gbranch.at[m], r.rows_branch.at[m])
         small_g[3:4, :] += column_sum(low_first.astype(f32))
-        load_mix[m].wait()
-        load_lse[m].wait()
+        late["mix"][m].wait()
+        late["lse"][m].wait()
         if m == 0:
-            load_attn.wait()
+            late["attn"].wait()
         grad_att = dot_t(low_first, attn[3]).astype(bf16)
         gall[m, mine, :] = grad_att
-        for k in range(nz):
-            rows_push(m, k).start()
         weighed = grad_att.astype(f32) * mix[m]
         delta = jnp.dot(weighed, heads, preferred_element_type=f32, precision=exact_dot)
         del_c[m] = delta
         aux[m, c, 0:16] = lse[m].T[0:16]
         aux[m, c, 16:32] = delta.T[0:16]
         aux[m, c, 32:40] = top[...]
-        for k in range(nz):
-            aux_push(m, k).start()
+        if m == 0:
+            spread_start(0)
+        elif m == 1:
+
+            @pl.when(s == 0)
+            def _():
+                spread_sent(0)
+                spread_start(1)
+
+        if fused:
+            rows_start(m, False)
+
+    if fused:
+
+        @pl.when(s == 0)
+        def _():
+            ff_gradients()
+
+    def paced(at):
+        if not fused:
+            return lambda g: None
+
+        def run(g):
+            @pl.when((s == 0) & (lax.rem(g, PACE) == PACE - 1))
+            def _():
+                step(at * (PAIRS // PACE) + g // PACE)
+
+        return run
 
     spots = lax.broadcasted_iota(jnp.int32, (1, T), 1)
-    rows_here = lax.broadcasted_iota(jnp.int32, (TD, 128), 0)
+    here = lax.broadcasted_iota(jnp.int32, (TD, 128), 0)
     for m in range(MB):
         if m >= slots:
-            load_x.append(load(xall_h.at[m], xall.at[m % slots]))
-        load_x[m].wait()
-        load_kv[m].wait()
-        load_q[m].wait()
+            late["x"].append(load(r.xall_h.at[m], xall.at[m % slots]))
+        for name in ("x", "kv", "q"):
+            late[name][m].wait()
 
         def stream(g):
             slot = lax.rem(g, 2)
             return [
                 pltpu.make_async_copy(
-                    kv_h.at[m, :, pl.ds(pl.multiple_of(e * D + g * 128, 128), 128)],
+                    r.kv_h.at[m, :, pl.ds(pl.multiple_of(e * D + g * 128, 128), 128)],
                     kvp.at[slot, e],
-                    kvp_sem.at[slot, e],
+                    r.kvp_sem.at[slot, e],
                 )
                 for e in range(2)
             ]
@@ -577,6 +1189,7 @@
         counted = jnp.where(spots < length, dot(counts_q[m].astype(bf16), lanes), 0.0)
         counted = jnp.where(counted > 0, jnp.log(jnp.maximum(counted, 1.0)), masked_score)
         wide_q[...] = counted.reshape(PAIRS, 8, T)
+        advance = paced(2 * m)
 
         def own_rows(g, _):
             @pl.when(g + 1 < PAIRS)
@@ -601,19 +1214,27 @@
                 grad_scores = (probs * (grad_probs - delta)).astype(bf16)
                 grad_q = grad_q + dot(grad_scores, keys)
             dqkv[m, :, pair_lanes(g)] = (joined(grad_q) * (HD**-0.5)).astype(bf16)
+            advance(g)
             return 0
 
         lax.fori_loop(0, PAIRS, own_rows, 0)
+        if m + 1 < MB:
+
+            @pl.when((s == 1) | (m > 0))
+            def _():
+                spread_sent(m)
+                spread_start(m + 1)
 
         def project(i, _):
-            r = pl.ds(pl.multiple_of(i * 256, 256), 256)
-            rows = dot(xall[m % slots, r, :], attn[0]).astype(bf16).astype(f32)
-            xall[m % slots, r, :] = (rows * (HD**-0.5)).astype(bf16)
+            rows = pl.ds(pl.multiple_of(i * 256, 256), 256)
+            all_q = dot(xall[m % slots, rows, :], attn[0]).astype(bf16).astype(f32)
+            xall[m % slots, rows, :] = (all_q * (HD**-0.5)).astype(bf16)
             return 0
 
         lax.fori_loop(0, T // 256, project, 0)
         for k in range(1, nz):
             rows_arrival(m, k).wait_recv()
+            relay_arrival(m, k).wait_recv()
             rows_forward(m, k).start()
             aux_arrival(m, k).wait_recv()
             aux_forward(m, k).start()
@@ -633,7 +1254,8 @@
         counted = dot(counts_k[m].astype(bf16), lanes)
         counted = jnp.where(counted > 0, jnp.log(jnp.maximum(counted, 1.0)), masked_score)
         wide_k[...] = counted.reshape(PAIRS, 8, T)
-        live = c * TD + rows_here < length
+        live = c * TD + here < length
+        advance_keys = paced(2 * m + 1)
 
         def own_keys(g, _):
             keys = halves(kv[m, :, pair_lanes(g)])
@@ -659,10 +1281,14 @@
             lanes_v = pl.ds(pl.multiple_of(2 * D + g * 128, 128), 128)
             dqkv[m, :, lanes_k] = jnp.where(live, grad_k, 0.0).astype(bf16)
             dqkv[m, :, lanes_v] = jnp.where(live, grad_v, 0.0).astype(bf16)
+            advance_keys(g)
             return 0
 
         lax.fori_loop(0, PAIRS, own_keys, 0)
-        save(dqkv.at[m], rows_qkv.at[m])
+        if fused:
+            rows_start(m, True)
+        else:
+            save(dqkv.at[m], r.rows_qkv.at[m])
         small_g[2:3, :] += column_sum(dqkv[m, :, 2 * D :].astype(f32))
         total = gfirst[m]
         for p in range(3):
@@ -673,22 +1299,63 @@
         def _():
             grad_push(m).start()
 
-        save(gin.at[m], grad_in_o.at[0, m, 0])
-
-    save(small_g, small_o)
+        save(gin.at[m], r.grad_in_o.at[0, m, 0])
+
+    def loop(t, _):
+        step(t)
+        return 0
+
+    if fused:
+        small_first(small_g[...])
+        done_1 = EARLY
+
+        @pl.when(s == 1)
+        def _():
+            relay_one(0)
+            ff_gradients()
+            lax.fori_loop(0, EARLY, loop, 0)
+            for m in range(1, MB):
+                relay_one(m)
+
+        rows_here(True, slice(None))
+        attn_tiles(r)
+        small_second()
+        done_0 = 2 * MB * (PAIRS // PACE)
+        now = jnp.where(s == 0, done_0, done_1)
+        lax.fori_loop(now, now + 3, loop, 0)
+        small_third()
+    else:
+
+        @pl.when(s == 1)
+        def _():
+            for m in range(MB):
+                relay_one(m)
+
+        save(small_g, r.small_o)
     for k in range(1, W):
         top_push(k).wait()
     most = top_x[0]
     for k in range(1, W):
         most = jnp.maximum(most, top_x[k])
-    top_o[...] = most
+    if fused:
+        clip_weights(
+            r, most, lambda p: attn[p, pl.ds(pl.multiple_of(w * part, 16), part), :]
+        )
+        lax.fori_loop(now + 3, last, loop, 0)
+        small_finish()
+        rows_sent()
+        drain()
+    else:
+        r.top_o[...] = most
     for m in range(MB):
         for k in range(nz):
             rows_forward(m, k).wait_send()
             aux_forward(m, k).wait_send()
         for k in range(1, nz):
-            rows_push(m, k).wait_send()
             aux_push(m, k).wait_send()
+            relay_push(m, k).wait_send()
+        if m == MB - 1:
+            spread_sent(m)
 
         @pl.when(s == 1)
         def _():
@@ -696,6 +1363,23 @@
 
     for copy in saves:
         copy.wait()
+
+
+def widen_kernel(sums, attn_o, up_o, down_o):
+    t = pl.program_id(0)
+    rows = sums[0].astype(f32)
+
+    @pl.when(t < 4)
+    def _():
+        down_o[...] = rows
+
+    @pl.when((t >= 4) & (t < 8))
+    def _():
+        up_o[...] = rows
+
+    @pl.when(t >= 8)
+    def _():
+        attn_o[0, 0] = rows
 
 
 def counts_of(seq_lengths, rand_owner, rand_local, global_raw, c, n_ctx):
@@ -770,13 +1454,15 @@
         pltpu.VMEM((MB, TD, FF), f32),
         pltpu.VMEM((MB, TD, D), bf16),
         pltpu.VMEM((PAIRS, 8, T), f32),
-        DMA((4,)),
-        DMA((W - 1, 4)),
-        DMA((W - 1, 4)),
-        DMA((W - 1, 4)),
-        DMA((W - 1, 4)),
+        DMA((3,)),
+        DMA((W - 1, 8)),
+        DMA((W - 1, 8)),
+        DMA((W - 1, 8, 3)),
+        DMA((W - 1, 8, 3)),
         DMA((W - 1,)),
         DMA((W - 1,)),
+        DMA((MB, nz)),
+        DMA((MB, nz)),
         DMA((MB, nz)),
         DMA((MB, nz)),
         DMA((MB, nz)),
@@ -797,89 +1483,188 @@
     )(lens, tokens, attn_w, up_w, down_w, small_in, counts)
 
 
-def run_backward(nz, W, MB, lens, cot, counts_q, counts_k, saved):
+def call(kernel, name, number, limit, ins, outs, scratch):
+    names = list(ins) + list(outs) + list(scratch)
+
+    def body(*refs):
+        kernel(types.SimpleNamespace(**dict(zip(names, refs, strict=True))))
+
+    found = pl.pallas_call(
+        body,
+        out_shape=[jax.ShapeDtypeStruct(*v[:2]) for v in outs.values()],
+        in_specs=[v[1] for v in ins.values()],
+        out_specs=[v[2] for v in outs.values()],
+        scratch_shapes=list(scratch.values()),
+        compiler_params=pltpu.CompilerParams(
+            collective_id=number, has_side_effects=True, vmem_limit_bytes=limit << 20
+        ),
+        name=name,
+    )(*(v[0] for v in ins.values()))
+    return dict(zip(outs, found))
+
+
+def sum_scratch(nz, W, MB):
+    part, R = D // W, MB * TD
+    count = 6 * (part // ROWS)
+    copies = MB * (W + 7)
+    return dict(
+        lg=pltpu.VMEM((2 * R, FF // 2), bf16),
+        rd=pltpu.VMEM((2 * R, D), bf16),
+        ln=pltpu.VMEM((2 * R, D), bf16),
+        rh=pltpu.VMEM((2 * R, FF // 2), bf16),
+        la=pltpu.VMEM((2 * R, D), bf16),
+        ra=pltpu.VMEM((2 * R, D), bf16),
+        lb=pltpu.VMEM((2 * R, D), bf16),
+        rb=pltpu.VMEM((2 * R, D), bf16),
+        from_x=pltpu.VMEM((W - 1, 6 * part, D), bf16),
+        chain=pltpu.VMEM((2, 6 * part, D), bf16),
+        core_s=pltpu.VMEM((2, 16, D), f32),
+        wsh_s=pltpu.VMEM((W, 16, D), f32),
+        z_s=pltpu.VMEM((nz, 16, D), f32),
+        c_send=DMA((copies,)),
+        c_recv=DMA((copies,)),
+        c_load=DMA((copies,)),
+        x_send=DMA((W - 1, count)),
+        x_recv=DMA((W - 1, count)),
+        ch_send=DMA((count,)),
+        ch_recv=DMA((2, count)),
+        t_send=DMA((2, count)),
+        t_recv=DMA((count,)),
+        p_send=DMA((count,)),
+        p_recv=DMA((count,)),
+        o_sem=DMA((count,)),
+        sc_send=DMA,
+        sc_recv=DMA,
+        sx_send=DMA((W - 1,)),
+        sx_recv=DMA((W - 1,)),
+        sz_send=DMA((nz - 1,)),
+        sz_recv=DMA((nz - 1,)),
+    )
+
+
+def sum_outs(W):
+    part = D // W
+    return dict(
+        sums=((2, 6 * part, D), bf16, ANY),
+        small_o=((16, D), f32, VMEM),
+        clip_o=((1, 2, part, D), bf16, VMEM),
+    )
+
+
+def run_backward(nz, W, MB, fused, lens, cot, counts_q, counts_k, saved):
     T = 2 * nz * TD
     slots = slots_of(T, MB)
-    shape = jax.ShapeDtypeStruct
-    (xall, kv, q, mix, lse, first, second, hidden, top, attn, up, down, small) = saved
-    outs = [
-        shape((1, MB, 1, TD, D), bf16),
-        shape((MB, TD, 3 * D), bf16),
-        shape((MB, TD, D), bf16),
-        shape((MB, TD, D), bf16),
-        shape((MB, TD, FF), bf16),
-        shape((MB, TD, FF), bf16),
-        shape((MB, TD, D), bf16),
-        shape((16, D), f32),
-        shape((8, 128), f32),
-    ]
-    scratch = [
-        pltpu.VMEM((4, D, D), bf16),
-        pltpu.VMEM((D, FF), bf16),
-        pltpu.VMEM((FF, D), bf16),
-        pltpu.VMEM((slots, T, D), bf16),
-        pltpu.VMEM((MB, TD, 2 * D), bf16),
-        pltpu.VMEM((MB, TD, D), bf16),
-        pltpu.VMEM((MB, TD, D), f32),
-        pltpu.VMEM((MB, TD, 128), f32),
-        pltpu.VMEM((MB, TD, D), f32),
-        pltpu.VMEM((MB, TD, D), f32),
-        pltpu.VMEM((slots, TD, FF), f32),
-        pltpu.VMEM((MB, TD, D), bf16),
-        pltpu.VMEM((MB, TD, D), f32),
-        pltpu.VMEM((MB, TD, D), bf16),
-        pltpu.VMEM((MB, T, D), bf16),
-        pltpu.VMEM((MB, 2 * nz, 40, 128), f32),
-        pltpu.VMEM((2, 2, T, 2 * HD), bf16),
-        pltpu.VMEM((PAIRS, 8, T), f32),
-        pltpu.VMEM((PAIRS, 8, T), f32),
-        pltpu.VMEM((16, T), f32),
-        pltpu.VMEM((16, T), f32),
-        pltpu.VMEM((MB, TD, 128), f32),
-        pltpu.VMEM((MB, TD, 3 * D), bf16),
-        pltpu.VMEM((MB, TD, D), bf16),
-        pltpu.VMEM((slots, TD, FF), bf16),
-        pltpu.VMEM((slots, TD, FF), bf16),
-        pltpu.VMEM((MB, TD, D), bf16),
-        pltpu.VMEM((16, D), f32),
-        pltpu.VMEM((MB, TD, D), bf16),
-        pltpu.VMEM((W, 8, 128), f32),
-        DMA((3 + 8 * MB,)),
-        DMA((MB,)),
-        DMA((MB,)),
-        DMA((MB, nz)),
-        DMA((MB, nz)),
-        DMA((MB, nz)),
-        DMA((MB, nz)),
-        DMA((MB, nz)),
-        DMA((MB, nz)),
-        DMA((MB, nz)),
-        DMA((MB, nz)),
-        DMA((W - 1,)),
-        DMA((W - 1,)),
-        DMA((2, 2)),
-        DMA((1 + 7 * MB,)),
-    ]
+    ins = dict(
+        lens=(lens, SMEM),
+        cot=(cot, ANY),
+        counts_q=(counts_q, VMEM),
+        counts_k=(counts_k, VMEM),
+        **{k: (v, VMEM if k in ("top", "small") else ANY) for k, v in saved.items()},
+    )
+    outs = dict(grad_in_o=((1, MB, 1, TD, D), bf16, ANY))
+    if fused:
+        outs.update(sum_outs(W))
+    else:
+        outs.update(
+            rows_qkv=((MB, TD, 3 * D), bf16, ANY),
+            rows_branch=((MB, TD, D), bf16, ANY),
+            rows_normed=((MB, TD, D), bf16, ANY),
+            rows_hidden=((MB, TD, FF), bf16, ANY),
+            rows_gated=((MB, TD, FF), bf16, ANY),
+            rows_down=((MB, TD, D), bf16, ANY),
+            small_o=((16, D), f32, ANY),
+            top_o=((8, 128), f32, VMEM),
+        )
+    scratch = dict(
+        attn=pltpu.VMEM((4, D, D), bf16),
+        up=pltpu.VMEM((D, FF), bf16),
+        down=pltpu.VMEM((FF + 2 * D if fused else FF, D), bf16),
+        xall=pltpu.VMEM((slots, T, D), bf16),
+        kv=pltpu.VMEM((MB, TD, 2 * D), bf16),
+        q=pltpu.VMEM((MB, TD, D), bf16),
+        mix=pltpu.VMEM((MB, TD, D), f32),
+        lse=pltpu.VMEM((MB, TD, 128), f32),
+        first=pltpu.VMEM((MB, TD, D), f32),
+        second=pltpu.VMEM((MB, TD, D), f32),
+        hidden=pltpu.VMEM((slots, TD, FF), f32),
+        dout=pltpu.VMEM((MB, TD, D), bf16),
+        gfirst=pltpu.VMEM((MB, TD, D), f32),
+        gbranch=pltpu.VMEM((MB, TD, D), bf16),
+        gall=pltpu.VMEM((MB, T, D), bf16),
+        relay=pltpu.VMEM((MB, BLK, D), bf16),
+        aux=pltpu.VMEM((MB, 2 * nz, 40, 128), f32),
+        kvp=pltpu.VMEM((2, 2, T, 2 * HD), bf16),
+        wide_q=pltpu.VMEM((PAIRS, 8, T), f32),
+        wide_k=pltpu.VMEM((PAIRS, 8, T), f32),
+        lse_all=pltpu.VMEM((16, T), f32),
+        del_all=pltpu.VMEM((16, T), f32),
+        del_c=pltpu.VMEM((MB, TD, 128), f32),
+        dqkv=pltpu.VMEM((MB, TD, 3 * D), bf16),
+        gnorm=pltpu.VMEM((MB, TD, D), bf16),
+        ghid=pltpu.VMEM((slots, TD, FF), bf16),
+        gated=pltpu.VMEM((slots, TD, FF), bf16),
+        gdown=pltpu.VMEM((MB, TD, D), bf16),
+        small_g=pltpu.VMEM((16, D), f32),
+        gin=pltpu.VMEM((MB, TD, D), bf16),
+        top_x=pltpu.VMEM((W, 8, 128), f32),
+        load_sem=DMA((1 + 3 * NCH + 8 * MB,)),
+        y_send=DMA((MB,)),
+        y_recv=DMA((MB,)),
+        tp_send=DMA((W - 1,)),
+        tp_recv=DMA((W - 1,)),
+        kvp_sem=DMA((2, 2)),
+        save_sem=DMA((1 + 7 * MB,)),
+        **{k: DMA((MB, nz)) for k in RINGS},
+    )
+    if fused:
+        scratch.update(sum_scratch(nz, W, MB))
+
+    def kernel(r):
+        if fused:
+            r.grads = r.down
+        backward_kernel(nz, W, MB, T, fused, r)
+
+    return call(kernel, "backward", 1, 63 if fused else 60, ins, outs, scratch)
+
+
+def run_reduce(nz, W, MB, ins):
+    part = D // W
+    scratch = sum_scratch(nz, W, MB)
+    scratch.update(
+        grads=pltpu.VMEM((6 * D, D), bf16),
+        own_w=pltpu.VMEM((2, part, D), bf16),
+        load_sem=DMA((MB * (W + 7),)),
+        own_sem=DMA,
+    )
+    ins = {k: (v, VMEM if k in ("small_g", "tops") else ANY) for k, v in ins.items()}
+    return call(
+        functools.partial(reduce_kernel, nz, W, MB), "reduce", 2, 60, ins, sum_outs(W), scratch
+    )
+
+
+def widen(sums, W):
+    part, ffp = D // W, FF // W
+
+    def source(t):
+        return (lax.rem(t, 4) // 2, (t // 4) * 2 + lax.rem(t, 2), 0)
+
     return pl.pallas_call(
-        functools.partial(backward_kernel, nz, W, MB, T),
-        out_shape=outs,
-        in_specs=[SMEM, ANY, VMEM, VMEM] + [ANY] * 8 + [VMEM] + [ANY] * 3 + [VMEM],
-        out_specs=[ANY] * 8 + [VMEM],
-        scratch_shapes=scratch,
-        compiler_params=pltpu.CompilerParams(
-            collective_id=1, has_side_effects=True, vmem_limit_bytes=60 << 20
-        ),
-        name="backward",
-    )(
-        lens, cot, counts_q, counts_k, xall, kv, q, mix, lse, first, second, hidden, top,
-        attn, up, down, small,
-    )
-
-
-def contract_rows(left_side, right_side):
-    return lax.dot_general(
-        left_side, right_side, (((0,), (0,)), ((), ())), preferred_element_type=f32
-    )
+        widen_kernel,
+        grid=(12,),
+        out_shape=[
+            jax.ShapeDtypeStruct((1, 4, part, D), f32),
+            jax.ShapeDtypeStruct((part, FF), f32),
+            jax.ShapeDtypeStruct((ffp, D), f32),
+        ],
+        in_specs=[pl.BlockSpec((1, part, D), source)],
+        out_specs=[
+            pl.BlockSpec((1, 1, part, D), lambda t: (0, jnp.maximum(t - 8, 0), 0, 0)),
+            pl.BlockSpec((part, D), lambda t: (0, jnp.clip(t - 4, 0, 3))),
+            pl.BlockSpec((part, D), lambda t: (jnp.minimum(t, 3), 0)),
+        ],
+        compiler_params=pltpu.CompilerParams(vmem_limit_bytes=40 << 20),
+        name="widen",
+    )(sums)
 
 
 def per_device(
@@ -900,44 +1685,29 @@
     (
         out, xall, kv, q, att, mix, lse, first, second, hidden, top, attn, up, down, small,
     ) = run_forward(nz, W, MB, lens, tokens, attn_weights, up_weights, down_weights, small_in, counts_q)
-    (
-        grad_in, rows_qkv, rows_branch, rows_normed, rows_hidden, rows_gated, rows_down, small_g, tops,
-    ) = run_backward(
-        nz, W, MB, lens, out_cotangent, counts_q, counts_k,
-        (xall, kv, q, mix, lse, first, second, hidden, top, attn, up, down, small),
+    fused = W == 2 and n_ctx * TD <= 2048
+    saved = dict(
+        xall_h=xall, kv_h=kv, q_h=q, mix_h=mix, lse_h=lse, first_h=first, second_h=second,
+        hidden_h=hidden, top=top, attn_h=attn, up_h=up, down_h=down, small=small,
     )
-    head_tops = tops[0, :H]
-    factor = jnp.sqrt(clip_limit / jnp.maximum(head_tops, clip_limit))
-    clipped = (
-        attn_weights[0, :2].astype(f32).reshape(2, -1, H, HD) * factor[None, None, :, None]
-    )
-    clipped_qk = clipped.reshape(1, 2, -1, D).astype(bf16)
-
-    def flat(v):
-        return v.reshape(-1, v.shape[-1])
-
-    x_own = flat(lax.dynamic_slice_in_dim(xall, c * TD, TD, 1))
-    qkv = flat(rows_qkv)
-    grads = (
-        jnp.stack(
-            [contract_rows(x_own, qkv[:, p * D : (p + 1) * D]) for p in range(3)]
-            + [contract_rows(flat(att), flat(rows_branch))]
-        ),
-        contract_rows(flat(rows_normed), flat(rows_hidden)),
-        contract_rows(flat(rows_gated), flat(rows_down)),
-    )
-    dims = (1, 0, 0)
-    shards = tuple(
-        lax.psum_scatter(g.astype(bf16), "wsh", scatter_dimension=d, tiled=True)
-        for g, d in zip(grads, dims)
-    )
-    total = tuple(lax.psum(g, "ctx").astype(f32) for g in shards)
-    small_g = lax.psum(small_g, ("ctx", "wsh"))
+    if fused:
+        saved["att_h"] = att
+    got = run_backward(nz, W, MB, fused, lens, out_cotangent, counts_q, counts_k, saved)
+    grad_in = got["grad_in_o"]
+    if not fused:
+        names = ("gated", "down", "normed", "hidden", "qkv", "branch")
+        rows = {k + "_h": got["rows_" + k] for k in names}
+        rows.update(
+            att_h=att, x_h=xall, small_g=got["small_o"], tops=got["top_o"], attn_w=attn_weights
+        )
+        got = run_reduce(nz, W, MB, rows)
+    small_g, clipped_qk = got["small_o"], got["clip_o"]
+    grad_attn, grad_up, grad_down = widen(got["sums"], W)
     gains = lax.dynamic_slice(small_g[0:2], (0, w * part), (2, part))
     biases = lax.dynamic_slice(small_g[2:7], (0, w * part), (5, part))
     up_grad = lax.dynamic_slice(small_g[7:11].reshape(-1), (w * ffp,), (ffp,))
     return (
-        out, grad_in, total[0][None], total[1][None], total[2][None], gains[None], biases[None],
+        out, grad_in, grad_attn, grad_up[None], grad_down[None], gains[None], biases[None],
         up_grad[None], clipped_qk,
     )
 

time: 645 us -> 325 us (0.50)
  waiting for transfers between devices: 266 us -> 0 us
  blocking collectives: 58.3 us -> 0 us
  Pallas kernels: 265 us -> 307 us
  other arithmetic: 19.2 us -> 5.03 us
  between operations: 14 us -> 0.77 us
  matrix products: 10.8 us -> 0 us
    reduce_scatter x3 -> x0, waiting for transfers between devices: 175 us -> none  [per_device(): lax.psum_scatter(g.astype(bf16), 'wsh', scatter_dimension=d, tiled=True)]
    psum x1 -> x0, waiting for transfers between devices: 91.1 us -> none  [per_device(): total = tuple((lax.psum(g, 'ctx').astype(f32) for g in shards))]
    pallas_call x1 -> x2, Pallas kernels: 150 us -> 214 us  [the longest x1 205 us: call(): pl.pallas_call(body, out_shape=[jax.ShapeDtypeStruct(*v[:2]) for v in out...]
    psum x1 -> x0, blocking collectives: 58.3 us -> none  [per_device(): small_g = lax.psum(small_g, ('ctx', 'wsh'))]
    pallas_call x1, Pallas kernels: 115 us -> 93.7 us  [run_forward(): pl.pallas_call(functools.partial(forward_kernel, nz, W, MB, T), out_shape...]
    dot_general x6 -> x0, matrix products: 10.8 us -> none  [contract_rows(): lax.dot_general(left_side, right_side, (((0,), (0,)), ((), ())), preferre...]
    broadcast_in_dim x3 -> x0, other arithmetic: 9.71 us -> none  [the longest x1 4.4 us: per_device(): total[0][None]]
  transfers between devices with their start and end apart: 4 -> 0, of which waited for: 4 -> 0; matrix products, arithmetic and copies ran while one was open for 2% -> 0% of each run, Pallas kernels for 0% -> 0%
where the time goes in v4:
time: 325 us; the launch traced here: 324 us
  Pallas kernels  307 us (94%)
  local copies, waits for them, and re-layouts  11.1 us (3%)
  other arithmetic  5.03 us (2%)
    pallas_call x1, Pallas kernels, call(): pl.pallas_call(body, out_shape=[jax.ShapeDtypeStruct(*v[:2]) for v in out...  205 us
    pallas_call x1, Pallas kernels, run_forward(): pl.pallas_call(functools.partial(forward_kernel, nz, W, MB, T), out_shape...  93.7 us
    pallas_call x1, Pallas kernels, widen(): pl.pallas_call(widen_kernel, grid=(12,), out_shape=[jax.ShapeDtypeStruct(...  8.11 us

profile of v4, /device:TPU:25, one launch (start us, length us, event | category | flops | bytes accessed | tf_op | source)
XLA Modules:
  0.0 324.1 jit_solution(12552456926190992047)
XLA Ops:
  0.7 0.1 pad.9.clone
  0.7 0.7 compare_bitcast_fusion
  1.4 0.9 and_select_fusion
  2.3 0.1 fusion.1
  2.4 0.1 convert_reduce_fusion.2
  2.5 0.7 convert_reduce_fusion.1
  3.2 0.3 dynamic_update_slice.7
  3.5 0.7 convert_dynamic-update-slice_fusion
  4.3 0.7 maximum_maximum_fusion.small_in
  5.0 0.8 multiply_add_fusion
  5.8 0.2 convert_reduce_fusion
  6.1 0.1 select_convert_fusion
  6.2 0.1 dynamic-slice_bitcast_fusion
  6.3 0.2 copy.30
  6.6 0.6 slice_bitcast_fusion
  7.2 93.7 %forward.1 = (bf16[1,2,1,128,768]{4,3,2,1,0:T(8,128)(2,1)}, bf16[2,1024,768]{2,1,0:T(8,128)(2,1)}, bf16[2,1024,1536]{2,1,0:T(8,128)(2,1)}, bf16[2,128,768]{2,1,0...) custom-call(s32[2]{0:T(128)} %bitcast.28, ...), custom_call_target="tpu_custom_call" | custom-call | tf_op jit(solution)/shard_map/forward/pallas_call | solution.py:1473
  100.9 0.0 copy-start.2
  100.9 205.4 %backward.1 = (bf16[1,2,1,128,768]{4,3,2,1,0:T(8,128)(2,1)}, bf16[2,2304,768]{2,1,0:T(8,128)(2,1)}, f32[16,768]{1,0:T(8,128)}, bf16[1,2,384,768]{3,2,1,0:T(8,128)(2,1)}) custom-call(s32[2]{0:T(128)} %bitcast.29, bf16[2,1,128,768]{3,2,1,0:T(8,128)(2,1)} %refs_1_.1, f32[2,48,16]{2,1,0:T(8,128)} %get-tuple-element.56.counts.refs_2_, ...), custom_call_target="tpu_custom_call" | custom-call | tf_op jit(solution)/shard_map/backward/pallas_call | solution.py:1492
  306.3 0.7 slice.19
  307.1 0.6 dynamic-slice_bitcast_fusion.1
  307.7 0.8 slice.21
  308.5 0.7 slice.20
  309.2 0.6 broadcast_in_dim.54
  309.8 0.1 dynamic_slice.19
  309.9 0.6 broadcast_in_dim.55
  310.5 0.0 copy-start
  310.5 3.0 copy-done
  313.5 0.0 copy-start.3
  313.5 0.0 copy-start.1
  313.5 8.1 %widen.1 = (f32[1,4,384,768]{3,2,1,0:T(8,128)}, f32[384,3072]{1,0:T(8,128)}, f32[1536,768]{1,0:T(8,128)}) custom-call(bf16[2,2304,768]{2,1,0:T(8,128)(2,1)S(1)} %copy-done), custom_call_target="tpu_custom_call" | custom-call | tf_op jit(solution)/shard_map/widen/pallas_call | solution.py:1651
  321.6 0.0 copy-done.2
  321.6 0.7 copy.38
  322.4 0.0 copy-done.3
  322.4 0.7 copy.39
  323.1 0.0 copy-done.1
  323.1 1.0 copy.40
  (11 shorter events, 0.1 us)
Async XLA Ops:
  100.9 220.7 %copy-start.2 = (bf16[1,2,1,128,768]{4,3,2,1,0:T(8,128)(2,1)S(1)}, bf16[1,2,1,128,768]{4,3,2,1,0:T(8,128)(2,1)}, u32[]{:S(2)}) copy-start(bf16[1,2,1,128,768]{4,3,2,1,0:T(8,128)(2,1)} %get-tuple-element.66) | copy-start | bytes 1179652
  310.5 3.0 copy-start
  313.5 8.9 %copy-start.3 = (bf16[1,2,1,128,768]{4,3,2,1,0:T(8,128)(2,1)S(1)}, bf16[1,2,1,128,768]{4,3,2,1,0:T(8,128)(2,1)}, u32[]{:S(2)}) copy-start(bf16[1,2,1,128,768]{4,3,2,1,0:T(8,128)(2,1)} %get-tuple-element.67) | copy-start | bytes 1179652
  313.5 9.6 %copy-start.1 = (bf16[1,2,384,768]{3,2,1,0:T(8,128)(2,1)S(1)}, bf16[1,2,384,768]{3,2,1,0:T(8,128)(2,1)}, u32[]{:S(2)}) copy-start(bf16[1,2,384,768]{3,2,1,0:T(8,128)(2,1)} %get-tuple-element.74) | copy-start | bytes 3538948
